TPU v7x, 128 devices: a whole 4x4x4 slice. The times are simulated.
128 devices in a mesh: dp: 16 (over z_lo, x, core), seq: 8 (over z_hi, y).
Axes of the slice: x: 4, y: 4, z: 4 (z_hi: 2, z_lo: 2; z = z_hi * 2 + z_lo), core: 2. Of those that a mesh axis runs over, the one named last changes fastest.
Arguments:
- query_all: bfloat16 [16, 2048, 3072], P('dp', 'seq'), may hold values from -6 to 6
- key_all: bfloat16 [16, 2048, 3072], P('dp', 'seq'), may hold values from -6 to 6
- value_all: bfloat16 [16, 2048, 3072], P('dp', 'seq'), may hold values from -6 to 6
- out_weight: bfloat16 [3072, 5120], P('seq'), may hold values from -0.109375 to 0.109375
- cotangent: bfloat16 [16, 1280, 5120], P('dp', 'seq'), may hold values from -6 to 6
- visible: int32 [16, 1280], P('dp', 'seq'), may hold values from 0 to 255, as said below
- counts: int32 [16, 8], P('dp'), may hold values from 96 to 160, as said below
Outputs:
- output_rows: bfloat16 [16, 1280, 5120], P('dp', 'seq')
- grad_query: bfloat16 [16, 2048, 3072], P('dp', 'seq')
- grad_key: bfloat16 [16, 2048, 3072], P('dp', 'seq')
- grad_value: bfloat16 [16, 2048, 3072], P('dp', 'seq')
- grad_weight: float32 [3072, 5120], P('seq', 'dp')
Inputs may be any that keep to these rules, and one draw needn't show every extreme that they name: `counts`: in each clip one shard holds exactly 160 visible tokens. `visible`: for clip c and shard s, entries s * 160 to s * 160 + counts[c, s] - 1 are distinct token numbers within the shard in increasing order; the remaining entries of the shard are 0.
All inputs are finite; a program needn't handle non-finite values.
Results may differ from a plain program's by a relative error of at most 0.022.
Values may be sent and summed in bfloat16 or wider, within the bound.
No kernel may reach another device: no remote copies, remote signals or barrier semaphores. Data moves between devices by JAX's collectives and lax.ppermute only.
A program may use at most 192 MiB of HBM per device.

v0:
```python
import math

import jax
import jax.numpy as jnp
from jax import lax
from jax.sharding import PartitionSpec as P

HEAD_DIM = 128


def attend_weights(query_heads, key_heads, alive_all, score_scale):
    scores = (
        jnp.einsum("qhd,khd->hqk", query_heads, key_heads, preferred_element_type=jnp.float32)
        * score_scale
    )
    masked = jnp.where(alive_all[None, None, :], scores, -1e30)
    row_max = jnp.max(masked, axis=-1, keepdims=True)
    expo = jnp.exp(masked - row_max)
    return expo / jnp.sum(expo, axis=-1, keepdims=True)


def on_device(query_all, key_all, value_all, out_weight, cotangent, visible, counts):
    n_seq = lax.axis_size("seq")
    place = lax.axis_index("seq")
    capacity = visible.shape[1]
    total_rows = n_seq * capacity
    score_scale = 1.0 / math.sqrt(HEAD_DIM)
    local_list = visible[0]
    count_row = counts[0]
    shard_ids = jnp.arange(n_seq, dtype=jnp.int32)
    own_count = jnp.sum(jnp.where(shard_ids == place, count_row, 0))
    alive_here = jnp.arange(capacity, dtype=jnp.int32) < own_count
    keep_rows = alive_here.astype(jnp.bfloat16)[:, None]
    query_rows = jnp.take(query_all[0], local_list, axis=0) * keep_rows
    key_rows = jnp.take(key_all[0], local_list, axis=0) * keep_rows
    value_rows = jnp.take(value_all[0], local_list, axis=0) * keep_rows
    query_group, key_group, value_group = (
        lax.all_to_all(query_rows, "seq", split_axis=1, concat_axis=0, tiled=True),
        lax.all_to_all(key_rows, "seq", split_axis=1, concat_axis=0, tiled=True),
        lax.all_to_all(value_rows, "seq", split_axis=1, concat_axis=0, tiled=True),
    )
    group_width = query_group.shape[1]
    head_count = group_width // HEAD_DIM
    position = jnp.arange(total_rows, dtype=jnp.int32)
    matching = (position // capacity)[:, None] == shard_ids[None, :]
    count_each = jnp.sum(jnp.where(matching, count_row[None, :], 0), axis=1)
    alive_all = position % capacity < count_each
    alive_float = alive_all.astype(jnp.float32)
    query_heads = query_group.reshape(total_rows, head_count, HEAD_DIM)
    key_heads = key_group.reshape(total_rows, head_count, HEAD_DIM)
    value_heads = value_group.reshape(total_rows, head_count, HEAD_DIM)
    soft = attend_weights(query_heads, key_heads, alive_all, score_scale)
    soft_round = soft.astype(jnp.bfloat16)
    attn_heads = jnp.einsum(
        "hqk,khd->qhd", soft_round, value_heads, preferred_element_type=jnp.float32
    )
    attention_rows = (
        (attn_heads * alive_float[:, None, None])
        .reshape(total_rows, group_width)
        .astype(jnp.bfloat16)
    )
    picked = attention_rows
    output_local = lax.psum_scatter(
        jnp.dot(picked, out_weight, preferred_element_type=jnp.float32).astype(jnp.bfloat16),
        "seq",
        scatter_dimension=0,
        tiled=True,
    )
    piece = lax.all_gather(cotangent[0], "seq", axis=0, tiled=True)
    picked = attention_rows
    weight_acc = lax.dot_general(
        picked, piece, (((0,), (0,)), ((), ())), preferred_element_type=jnp.float32
    )
    rows_grad = lax.dot_general(
        piece, out_weight, (((1,), (1,)), ((), ())), preferred_element_type=jnp.float32
    )
    attn_grad = rows_grad
    grad_weight = lax.psum_scatter(
        weight_acc.astype(jnp.bfloat16), "dp", scatter_dimension=1, tiled=True
    ).astype(jnp.float32)
    attn_grad = (
        (attn_grad * alive_float[:, None])
        .astype(jnp.bfloat16)
        .reshape(total_rows, head_count, HEAD_DIM)
    )
    grad_value_heads = jnp.einsum(
        "hqk,qhd->khd", soft_round, attn_grad, preferred_element_type=jnp.float32
    ).astype(jnp.bfloat16)
    dsoft = jnp.einsum("qhd,khd->hqk", attn_grad, value_heads, preferred_element_type=jnp.float32)
    delta = jnp.sum(soft * dsoft, axis=-1, keepdims=True)
    dscore = (soft * (dsoft - delta) * score_scale).astype(jnp.bfloat16)
    grad_query_heads = jnp.einsum(
        "hqk,khd->qhd", dscore, key_heads, preferred_element_type=jnp.float32
    ).astype(jnp.bfloat16)
    grad_key_heads = jnp.einsum(
        "hqk,qhd->khd", dscore, query_heads, preferred_element_type=jnp.float32
    ).astype(jnp.bfloat16)
    grad_query_rows, grad_key_rows, grad_value_rows = (
        lax.all_to_all(
            grad_query_heads.reshape(total_rows, group_width),
            "seq",
            split_axis=0,
            concat_axis=1,
            tiled=True,
        ),
        lax.all_to_all(
            grad_key_heads.reshape(total_rows, group_width),
            "seq",
            split_axis=0,
            concat_axis=1,
            tiled=True,
        ),
        lax.all_to_all(
            grad_value_heads.reshape(total_rows, group_width),
            "seq",
            split_axis=0,
            concat_axis=1,
            tiled=True,
        ),
    )
    empty = jnp.zeros((query_all.shape[1], query_all.shape[2]), jnp.bfloat16)
    grad_query = empty.at[local_list].add(grad_query_rows)
    grad_key = empty.at[local_list].add(grad_key_rows)
    grad_value = empty.at[local_list].add(grad_value_rows)
    return (output_local[None], grad_query[None], grad_key[None], grad_value[None], grad_weight)


def solution(mesh):
    return jax.shard_map(
        on_device,
        mesh=mesh,
        in_specs=(
            P("dp", "seq", None),
            P("dp", "seq", None),
            P("dp", "seq", None),
            P("seq", None),
            P("dp", "seq", None),
            P("dp", "seq"),
            P("dp", None),
        ),
        out_specs=(
            P("dp", "seq", None),
            P("dp", "seq", None),
            P("dp", "seq", None),
            P("dp", "seq", None),
            P("seq", "dp"),
        ),
        check_vma=False,
    )
```

profile of v0, /device:TPU:0, one launch (start us, length us, event | category | flops | bytes accessed | tf_op | source)
XLA Modules:
  0.0 461.9 jit_solution(16417759013846726601)
XLA Ops:
  8.8 2.1 gather_fusion
  11.0 2.1 gather_fusion.1
  18.4 7.9 %all-to-all-start.2 = ((bf16[160,8,384]{2,0,1:T(8,128)(2,1)}), bf16[160,8,384]{2,0,1:T(8,128)(2,1)S(1)}, u32[]{:S(2)}, u32[]{:S(2)}) async-start(bf16[160,8,384]{2,0,1:T(8,128)(2,1)} %bitcast.84), calls=%async_computation.2 | async-start | bytes 1966080 | tf_op jit(solution)/shard_map/all_to_all | solution.py:39
  27.3 21.4 %all-to-all-done.2 = bf16[160,8,384]{2,0,1:T(8,128)(2,1)S(1)} async-done(((bf16[160,8,384]{2,0,1:T(8,128)(2,1)}), bf16[160,8,384]{2,0,1:T(8,128)(2,1)S(1)}, u32[]{:S(2)}, u32[]{:S(2)}) %all-to-all-start.2) | async-done | bytes 983072 | tf_op jit(solution)/shard_map/all_to_all | solution.py:39
  48.7 8.3 %all-to-all-start.1 = ((bf16[160,8,384]{2,0,1:T(8,128)(2,1)}), bf16[160,8,384]{2,0,1:T(8,128)(2,1)S(1)}, u32[]{:S(2)}, u32[]{:S(2)}) async-start(bf16[160,8,384]{2,0,1:T(8,128)(2,1)} %bitcast.83), calls=%async_computation.1 | async-start | bytes 1966080 | tf_op jit(solution)/shard_map/all_to_all | solution.py:38
  58.0 20.6 %all-to-all-done.1 = bf16[160,8,384]{2,0,1:T(8,128)(2,1)S(1)} async-done(((bf16[160,8,384]{2,0,1:T(8,128)(2,1)}), bf16[160,8,384]{2,0,1:T(8,128)(2,1)S(1)}, u32[]{:S(2)}, u32[]{:S(2)}) %all-to-all-start.1) | async-done | bytes 983072 | tf_op jit(solution)/shard_map/all_to_all | solution.py:38
  78.6 4.7 %all-to-all-start = ((bf16[160,8,384]{2,0,1:T(8,128)(2,1)}), bf16[160,8,384]{2,0,1:T(8,128)(2,1)}, u32[]{:S(2)}, u32[]{:S(2)}) async-start(bf16[160,8,384]{2,0,1:T(8,128)(2,1)} %bitcast.81), calls=%async_computation | async-start | bytes 1966080 | tf_op jit(solution)/shard_map/all_to_all | solution.py:40
  87.0 16.5 %all-to-all-done = bf16[160,8,384]{2,0,1:T(8,128)(2,1)} async-done(((bf16[160,8,384]{2,0,1:T(8,128)(2,1)}), bf16[160,8,384]{2,0,1:T(8,128)(2,1)}, u32[]{:S(2)}, u32[]{:S(2)}) %all-to-all-start) | async-done | bytes 983072 | tf_op jit(solution)/shard_map/all_to_all | solution.py:40
  103.5 2.6 reshape.140
  106.2 11.3 %exponential_reduce_fusion = (f32[3,1280]{1,0:T(4,128)S(1)}, f32[3,1280,1280]{1,2,0:T(8,128)}) fusion(bf16[1280,3,128]{0,2,1:T(8,128)(2,1)S(1)} %copy.74, bf16[1280,3,128]{0,2,1:T(8,128)(2,1)S(1)} %copy.70, pred[1280]{0:T(1024)(128)(4,1)S(1)} %get-tuple-element.7), kind=kOutput, calls=%fused_computation.18 | convolution fusion | flops 1277953280 | bytes 21643520 | tf_op jit(solution)/shard_map/sub | solution.py:18
  117.5 9.6 %fusion.34 = bf16[3,128,1280]{2,1,0:T(8,128)(2,1)} fusion(f32[1280]{0:T(1024)S(1)} %get-tuple-element.6, bf16[1280,3,128]{2,1,0:T(4,128)(2,1)S(1)} %reshape.140, f32[3,1280]{1,0:T(4,128)S(1)} %get-tuple-element.11, bf16[1280,3,128]{0,2,1:T(8,128)(2,1)S(1)} %copy.74, bf16[1280,3,128]{0,2,1:T(8,128)(2,1)S(1)} %copy.70, pred[1280]{0:T(1024)(128)(4,1)S(1)} %get-tuple-element.7), kind=kOutput, calls=%fused_computation.33 | convolution fusion | flops 2542146560 | bytes 3953920 | tf_op jit(solution)/shard_map/hqk,khd->qhd/dot_general | solution.py:54
  127.1 66.0 %all-gather.3.cloned.1.call-done = bf16[1,1280,5120]{2,1,0:T(8,128)(2,1)} async-done(((bf16[1,160,5120]{2,1,0:T(8,128)(2,1)}), bf16[1,1280,5120]{2,1,0:T(8,128)(2,1)}) %all-gather.3.cloned.1.call-update) | async-done | bytes 13107216 | tf_op jit(solution)/shard_map/all_gather | solution.py:69
  193.1 11.6 %fusion.15 = bf16[384,5120]{0,1:T(8,128)(2,1)} fusion(bf16[1280,384]{0,1:T(8,128)(2,1)} %bitcast.100, bf16[1,1280,5120]{2,1,0:T(8,128)(2,1)} %all-gather.3.cloned.1.call-done), kind=kOutput, calls=%fused_computation.24 | convolution fusion | flops 5035130880 | bytes 18022400 | tf_op jit(solution)/shard_map/dot_general | solution.py:71
  204.7 12.3 %convolution_convert_fusion = bf16[1280,5120]{1,0:T(8,128)(2,1)} fusion(bf16[1280,384]{0,1:T(8,128)(2,1)} %bitcast.101, bf16[384,5120]{1,0:T(8,128)(2,1)} %param.12), kind=kOutput, calls=%fused_computation.14 | convolution fusion | flops 5039718400 | bytes 18022400 | tf_op jit(solution)/shard_map/dot_general | solution.py:64
  217.0 14.4 %fusion.37 = bf16[1280,384]{0,1:T(8,128)(2,1)S(1)} fusion(bf16[384,5120]{1,0:T(8,128)(2,1)} %param.12, bf16[1,1280,5120]{2,1,0:T(8,128)(2,1)} %all-gather.3.cloned.1.call-done, f32[1280]{0:T(1024)S(1)} %get-tuple-element.6), kind=kOutput, calls=%fused_computation.34 | convolution fusion | flops 5034147840 | bytes 18027520 | tf_op jit(solution)/shard_map/dot_general | solution.py:74
  231.4 8.3 %fusion.65 = f32[3,1280,1280]{1,2,0:T(8,128)} fusion(bf16[1280,3,128]{0,2,1:T(8,128)(2,1)S(1)} %bitcast.91, bf16[1280,3,128]{2,1,0:T(4,128)(2,1)S(1)} %reshape.140), kind=kOutput, calls=%fused_computation.54 | convolution fusion | flops 1258291200 | bytes 21626880 | tf_op jit(solution)/shard_map/qhd,khd->hqk/dot_general | solution.py:89
  239.7 27.5 %fusion.49 = bf16[1280,3,128]{0,2,1:T(8,128)(2,1)} fusion(bf16[1280,3,128]{0,2,1:T(8,128)(2,1)S(1)} %copy.74, f32[3,1280,1280]{1,2,0:T(8,128)} %fusion.65, f32[3,1280,1280]{1,2,0:T(8,128)} %get-tuple-element.12, f32[3,1280]{1,0:T(4,128)S(1)} %get-tuple-element.11), kind=kOutput, calls=%fused_computation.38 | convolution fusion | flops 1293194240 | bytes 41303040 | tf_op jit(solution)/shard_map/hqk,qhd->khd/dot_general | solution.py:95
  267.2 2.8 copy.76
  271.7 3.7 all-to-all-start.4
  275.5 31.5 %fusion.52 = bf16[1280,3,128]{0,2,1:T(8,128)(2,1)} fusion(bf16[1280,3,128]{0,2,1:T(8,128)(2,1)S(1)} %copy.70, f32[3,1280,1280]{1,2,0:T(8,128)} %fusion.65, f32[3,1280,1280]{1,2,0:T(8,128)} %get-tuple-element.12, f32[3,1280]{1,0:T(4,128)S(1)} %get-tuple-element.11), kind=kOutput, calls=%fused_computation.39 | convolution fusion | flops 1293194240 | bytes 41303040 | tf_op jit(solution)/shard_map/hqk,khd->qhd/dot_general | solution.py:92
  306.9 2.8 copy.72
  311.4 7.2 %all-to-all-start.3 = ((bf16[8,160,384]{2,1,0:T(8,128)(2,1)}), bf16[8,160,384]{2,1,0:T(8,128)(2,1)}, u32[]{:S(2)}, u32[]{:S(2)}) async-start(bf16[8,160,384]{2,1,0:T(8,128)(2,1)} %all_to_all.87), calls=%async_computation.4 | async-start | bytes 1966080 | tf_op jit(solution)/shard_map/all_to_all | solution.py:99
  318.7 11.6 %fusion.55 = bf16[1280,3,128]{0,2,1:T(8,128)(2,1)} fusion(bf16[1280,3,128]{0,2,1:T(8,128)(2,1)} %bitcast.92, f32[3,1280]{1,0:T(4,128)} %copy-done.10, bf16[1280,3,128]{0,2,1:T(8,128)(2,1)} %copy-done.5, bf16[1280,3,128]{0,2,1:T(8,128)(2,1)S(1)} %copy.70, pred[1280]{0:T(1024)(128)(4,1)S(1)} %get-tuple-element.7), kind=kOutput, calls=%fused_computation.40 | convolution fusion | flops 2541655040 | bytes 3948800 | tf_op jit(solution)/shard_map/hqk,qhd->khd/dot_general | solution.py:86
  330.3 2.8 copy.79
  334.7 6.2 %all-to-all-done.3 = bf16[8,160,384]{2,1,0:T(8,128)(2,1)} async-done(((bf16[8,160,384]{2,1,0:T(8,128)(2,1)}), bf16[8,160,384]{2,1,0:T(8,128)(2,1)}, u32[]{:S(2)}, u32[]{:S(2)}) %all-to-all-start.3) | async-done | bytes 983072 | tf_op jit(solution)/shard_map/all_to_all | solution.py:99
  340.9 8.6 %all-to-all-start.5 = ((bf16[8,160,384]{2,1,0:T(8,128)(2,1)}), bf16[8,160,384]{2,1,0:T(8,128)(2,1)S(1)}, u32[]{:S(2)}, u32[]{:S(2)}) async-start(bf16[8,160,384]{2,1,0:T(8,128)(2,1)} %all_to_all.95), calls=%async_computation.6 | async-start | bytes 1966080 | tf_op jit(solution)/shard_map/all_to_all | solution.py:113
  350.9 2.3 copy.89
  353.2 4.7 %scatter_custom_fusion.1 = bf16[256,3072]{1,0:T(8,128)(2,1)} fusion(s32[160]{0:T(256)S(1)} %bitcast.95, bf16[160,3072]{1,0:T(8,128)(2,1)S(1)} %bitcast.88, bf16[]{:T(256)} %constant.46.clone.1), kind=kCustom, calls=%fused_computation.49 | custom fusion | flops 491520 | bytes 1572866 | tf_op jit(solution)/shard_map/scatter-add | solution.py:123
  357.9 5.4 %scatter_custom_fusion = bf16[256,3072]{1,0:T(8,128)(2,1)} fusion(s32[160]{0:T(256)S(1)} %bitcast.96, bf16[160,3072]{1,0:T(8,128)(2,1)} %bitcast.89, bf16[]{:T(256)} %constant.46.clone.1), kind=kCustom, calls=%fused_computation.51 | custom fusion | flops 491520 | bytes 1573376 | tf_op jit(solution)/shard_map/scatter-add | solution.py:122
  363.3 7.3 %all-to-all-done.5 = bf16[8,160,384]{2,1,0:T(8,128)(2,1)S(1)} async-done(((bf16[8,160,384]{2,1,0:T(8,128)(2,1)}), bf16[8,160,384]{2,1,0:T(8,128)(2,1)S(1)}, u32[]{:S(2)}, u32[]{:S(2)}) %all-to-all-start.5) | async-done | bytes 983072 | tf_op jit(solution)/shard_map/all_to_all | solution.py:113
  370.7 4.7 %scatter_custom_fusion.2 = bf16[256,3072]{1,0:T(8,128)(2,1)} fusion(s32[160]{0:T(256)S(1)} %bitcast.97, bf16[160,3072]{1,0:T(8,128)(2,1)S(1)} %bitcast.90, bf16[]{:T(256)} %constant.46.clone.1), kind=kCustom, calls=%fused_computation.47 | custom fusion | flops 491520 | bytes 1572866 | tf_op jit(solution)/shard_map/scatter-add | solution.py:124
  377.2 78.0 %reduce-scatter.3.cloned.1.call-done = bf16[160,5120]{1,0:T(8,128)(2,1)} async-done(((bf16[1280,5120]{1,0:T(8,128)(2,1)}), bf16[160,5120]{1,0:T(8,128)(2,1)}) %reduce-scatter.3.cloned.1.call-update) | async-done | bytes 1638416 | tf_op jit(solution)/shard_map/reduce_scatter | solution.py:63
  (53 shorter events, 21.1 us)
Async XLA Ops:
  7.2 1.6 copy-start
  7.2 3.8 copy-start.2
  7.2 185.9 %all-gather.3.cloned.1.call-start = ((), (), s32[]{:S(2)}) async-start(), calls=%async_computation.10 | async-start | bytes 14745600 | tf_op jit(solution)/shard_map/all_gather | solution.py:69
  8.8 5.5 %copy-start.9 = (s32[1,8]{1,0:T(1,128)S(1)}, s32[1,8]{1,0:T(1,128)}, u32[]{:S(2)}) copy-start(s32[1,8]{1,0:T(1,128)} %param.15) | copy-start | bytes 100
  8.8 6.1 %copy-start.7 = (s32[1,160]{1,0:T(1,128)S(1)}, s32[1,160]{1,0:T(1,128)}, u32[]{:S(2)}) copy-start(s32[1,160]{1,0:T(1,128)} %param.14) | copy-start | bytes 1924
  11.0 2.1 copy-start.3
  18.4 30.3 %all-to-all-start.2 = ((bf16[160,8,384]{2,0,1:T(8,128)(2,1)}), bf16[160,8,384]{2,0,1:T(8,128)(2,1)S(1)}, u32[]{:S(2)}, u32[]{:S(2)}) async-start(bf16[160,8,384]{2,0,1:T(8,128)(2,1)} %bitcast.84), calls=%async_computation.2 | async-start | bytes 1966080 | tf_op jit(solution)/shard_map/all_to_all | solution.py:39
  48.7 29.9 %all-to-all-start.1 = ((bf16[160,8,384]{2,0,1:T(8,128)(2,1)}), bf16[160,8,384]{2,0,1:T(8,128)(2,1)S(1)}, u32[]{:S(2)}, u32[]{:S(2)}) async-start(bf16[160,8,384]{2,0,1:T(8,128)(2,1)} %bitcast.83), calls=%async_computation.1 | async-start | bytes 1966080 | tf_op jit(solution)/shard_map/all_to_all | solution.py:38
  78.6 25.0 %all-to-all-start = ((bf16[160,8,384]{2,0,1:T(8,128)(2,1)}), bf16[160,8,384]{2,0,1:T(8,128)(2,1)}, u32[]{:S(2)}, u32[]{:S(2)}) async-start(bf16[160,8,384]{2,0,1:T(8,128)(2,1)} %bitcast.81), calls=%async_computation | async-start | bytes 1966080 | tf_op jit(solution)/shard_map/all_to_all | solution.py:40
  83.2 292.2 %reduce-scatter.5.cloned.1.call-start = ((), (), s32[]{:S(2)}) async-start(), calls=%async_computation.9 | async-start | bytes 4177920 | tf_op jit(solution)/shard_map/reduce_scatter | solution.py:78
  87.0 152.7 %copy-start.5 = (bf16[1280,3,128]{0,2,1:T(8,128)(2,1)}, bf16[1280,3,128]{0,2,1:T(8,128)(2,1)S(1)}, u32[]{:S(2)}) copy-start(bf16[1280,3,128]{0,2,1:T(8,128)(2,1)S(1)} %copy.74) | copy-start | bytes 2949124
  117.5 158.0 %copy-start.10 = (f32[3,1280]{1,0:T(4,128)}, f32[3,1280]{1,0:T(4,128)S(1)}, u32[]{:S(2)}) copy-start(f32[3,1280]{1,0:T(4,128)S(1)} %get-tuple-element.11) | copy-start | bytes 46084
  204.7 250.5 %reduce-scatter.3.cloned.1.call-start = ((), (), s32[]{:S(2)}) async-start(), calls=%async_computation.8 | async-start | bytes 14745600 | tf_op jit(solution)/shard_map/reduce_scatter | solution.py:63
  231.4 8.3 %copy-start.6 = (bf16[1280,384]{0,1:T(8,128)(2,1)}, bf16[1280,384]{0,1:T(8,128)(2,1)S(1)}, u32[]{:S(2)}) copy-start(bf16[1280,384]{0,1:T(8,128)(2,1)S(1)} %fusion.37) | copy-start | bytes 2949124
  271.7 39.7 %all-to-all-start.4 = ((bf16[8,160,384]{2,1,0:T(8,128)(2,1)}), bf16[8,160,384]{2,1,0:T(8,128)(2,1)S(1)}, u32[]{:S(2)}, u32[]{:S(2)}) async-start(bf16[8,160,384]{2,1,0:T(8,128)(2,1)} %all_to_all.91), calls=%async_computation.5 | async-start | bytes 1966080 | tf_op jit(solution)/shard_map/all_to_all | solution.py:106
  311.4 7.2 %copy-start.4 = (bf16[8,160,384]{2,1,0:T(8,128)(2,1)}, bf16[8,160,384]{2,1,0:T(8,128)(2,1)S(1)}, u32[]{:S(2)}) copy-start(bf16[8,160,384]{2,1,0:T(8,128)(2,1)S(1)} %all-to-all-done.4) | copy-start | bytes 2949124
  311.4 29.5 %all-to-all-start.3 = ((bf16[8,160,384]{2,1,0:T(8,128)(2,1)}), bf16[8,160,384]{2,1,0:T(8,128)(2,1)}, u32[]{:S(2)}, u32[]{:S(2)}) async-start(bf16[8,160,384]{2,1,0:T(8,128)(2,1)} %all_to_all.87), calls=%async_computation.4 | async-start | bytes 1966080 | tf_op jit(solution)/shard_map/all_to_all | solution.py:99
  318.6 30.9 %copy-start.8 = (s32[1,160]{1,0:T(1,128)S(1)}, s32[1,160]{1,0:T(1,128)}, u32[]{:S(2)}) copy-start(s32[1,160]{1,0:T(1,128)} %param.14) | copy-start | bytes 1924
  318.7 136.5 %copy-start.1 = (bf16[1,256,3072]{2,1,0:T(8,128)(2,1)S(1)}, bf16[1,256,3072]{2,1,0:T(8,128)(2,1)}, u32[]{:S(2)}) copy-start(bf16[1,256,3072]{2,1,0:T(8,128)(2,1)} %param.11) | copy-start | bytes 4718596
  340.9 29.6 %all-to-all-start.5 = ((bf16[8,160,384]{2,1,0:T(8,128)(2,1)}), bf16[8,160,384]{2,1,0:T(8,128)(2,1)S(1)}, u32[]{:S(2)}, u32[]{:S(2)}) async-start(bf16[8,160,384]{2,1,0:T(8,128)(2,1)} %all_to_all.95), calls=%async_computation.6 | async-start | bytes 1966080 | tf_op jit(solution)/shard_map/all_to_all | solution.py:113
Sparse Core Ops, SparseCore 0:
  10.3 182.6 all-gather.2
  204.8 64.6 reduce-scatter.4
  274.6 180.5 reduce-scatter.2
where the time goes:
time: 469 us; the launch traced here: 462 us
  waiting for transfers between devices  217 us (46%)
  matrix products  138 us (29%)
  starting transfers between devices  40.4 us (9%)
  local copies, waits for them, and re-layouts  32.1 us (7%)
  other arithmetic  20.6 us (4%)
  between operations  14.2 us (3%)
    reduce_scatter x1, waiting for transfers between devices, on_device(): lax.psum_scatter(jnp.dot(picked, out_weight, preferred_element_type=jnp.f...  78 us
    all_gather x1, waiting for transfers between devices, on_device(): piece = lax.all_gather(cotangent[0], 'seq', axis=0, tiled=True)  66 us
    dot_general x1, matrix products, on_device(): jnp.einsum('hqk,khd->qhd', dscore, key_heads, preferred_element_type=jnp....  31.5 us
    dot_general x1, matrix products, on_device(): jnp.einsum('hqk,qhd->khd', dscore, query_heads, preferred_element_type=jn...  27.5 us
    all_to_all x1, waiting for transfers between devices, on_device(): lax.all_to_all(key_rows, 'seq', split_axis=1, concat_axis=0, tiled=True)  21.4 us
    all_to_all x1, waiting for transfers between devices, on_device(): lax.all_to_all(query_rows, 'seq', split_axis=1, concat_axis=0, tiled=True)  20.6 us
    all_to_all x1, waiting for transfers between devices, on_device(): lax.all_to_all(value_rows, 'seq', split_axis=1, concat_axis=0, tiled=True)  16.5 us
    dot_general x1, matrix products, on_device(): lax.dot_general(piece, out_weight, (((1,), (1,)), ((), ())), preferred_el...  14.4 us
  transfers between devices with their start and end apart: 9, of which 7 were waited for; matrix products, arithmetic and copies ran while one was open for 38% of the time, Pallas kernels for 0%

commit v1 on v0

v1 whole, which is shorter than its diff:
```python
import functools
import math

import jax
import jax.numpy as jnp
import numpy as np
from jax import lax
from jax.experimental import pallas as pl
from jax.experimental.pallas import tpu as pltpu
from jax.sharding import Mesh, PartitionSpec as P

HEAD_DIM = 128
HEADS = 3
GROUP = HEADS * HEAD_DIM
CAP = 160
TOK = 256
NS = 8
NX = 4
D = 5120
HALF = D // (2 * NX)
ROWS = NS * CAP
XROWS = NX * CAP
VMEM = 56 * 1024 * 1024
F32 = jnp.float32
BF16 = jnp.bfloat16
AXES = ("zl", "x", "c", "zh", "y")
SEQ = ("zh", "y")


def params(*semantics):
    return pltpu.CompilerParams(dimension_semantics=semantics, vmem_limit_bytes=VMEM)


def dot(a, b, dims):
    return lax.dot_general(a, b, (dims, ((), ())), preferred_element_type=F32)


def gather_kernel(pick_ref, q_ref, k_ref, v_ref, out_ref):
    token = lax.broadcasted_iota(jnp.int32, (CAP, TOK), 1)
    hot = (token == pick_ref[...]).astype(F32).astype(BF16)
    for i, ref in enumerate((q_ref, k_ref, v_ref)):
        out_ref[0, i] = dot(hot, ref[...], ((1,), (0,))).astype(BF16)


def gather_rows(pick, q, k, v):
    block = pl.BlockSpec((TOK, GROUP), lambda s: (0, s))
    return pl.pallas_call(
        gather_kernel,
        grid=(NS,),
        in_specs=[pl.BlockSpec((CAP, 1), lambda s: (0, 0)), block, block, block],
        out_specs=pl.BlockSpec((1, 3, CAP, GROUP), lambda s: (s, 0, 0, 0)),
        out_shape=jax.ShapeDtypeStruct((NS, 3, CAP, GROUP), BF16),
        compiler_params=params("arbitrary"),
        cost_estimate=pl.CostEstimate(flops=2 * 3 * CAP * TOK * GROUP * NS, bytes_accessed=8 << 20, transcendentals=0),
    )(pick, q, k, v)


def scatter_kernel(pick_ref, rows_ref, q_ref, k_ref, v_ref):
    token = lax.broadcasted_iota(jnp.int32, (TOK, CAP), 0)
    hot = (token == pick_ref[...]).astype(F32).astype(BF16)
    for i, ref in enumerate((q_ref, k_ref, v_ref)):
        ref[...] = dot(hot, rows_ref[0, i], ((1,), (0,))).astype(BF16)


def scatter_rows(pick, rows):
    block = pl.BlockSpec((TOK, GROUP), lambda s: (0, s))
    return pl.pallas_call(
        scatter_kernel,
        grid=(NS,),
        in_specs=[
            pl.BlockSpec((1, CAP), lambda s: (0, 0)),
            pl.BlockSpec((1, 3, CAP, GROUP), lambda s: (s, 0, 0, 0)),
        ],
        out_specs=[block] * 3,
        out_shape=[jax.ShapeDtypeStruct((TOK, NS * GROUP), BF16)] * 3,
        compiler_params=params("arbitrary"),
        cost_estimate=pl.CostEstimate(flops=2 * 3 * CAP * TOK * GROUP * NS, bytes_accessed=8 << 20, transcendentals=0),
    )(pick, rows)


QB = 2
NQ = NS // QB


def forward_kernel(bias_ref, live_ref, q_ref, k_ref, v_ref, attn_ref, soft_ref):
    scale = math.log2(math.e) / math.sqrt(HEAD_DIM)
    keys = k_ref[...].reshape(ROWS, HEAD_DIM)
    values = v_ref[...].reshape(ROWS, HEAD_DIM)
    bias = bias_ref[...]
    for j in range(QB):
        scores = dot(q_ref[j, 0], keys, ((1,), (1,))) + bias
        top = jnp.max(scores, axis=1, keepdims=True)
        expo = jnp.exp2((scores - top) * scale)
        soft = (expo * (1.0 / jnp.sum(expo, axis=1, keepdims=True))).astype(BF16)
        soft_ref[0, j * CAP : (j + 1) * CAP, :] = soft
        attn_ref[j] = (dot(soft, values, ((1,), (0,))) * live_ref[j]).astype(BF16)


def forward(bias, live, qkv):
    def part(i, rows):
        if rows == QB:
            return pl.BlockSpec((QB, 1, CAP, HEAD_DIM), lambda h, r: (r, i, 0, h))
        return pl.BlockSpec((NS, 1, CAP, HEAD_DIM), lambda h, r: (0, i, 0, h))

    return pl.pallas_call(
        forward_kernel,
        grid=(HEADS, NQ),
        in_specs=[
            pl.BlockSpec((1, ROWS), lambda h, r: (0, 0)),
            pl.BlockSpec((QB, CAP, 1), lambda h, r: (r, 0, 0)),
            part(0, QB),
            part(1, NS),
            part(2, NS),
        ],
        out_specs=[
            pl.BlockSpec((QB, CAP, HEAD_DIM), lambda h, r: (r, 0, h)),
            pl.BlockSpec((1, QB * CAP, ROWS), lambda h, r: (h, r, 0)),
        ],
        out_shape=[
            jax.ShapeDtypeStruct((NS, CAP, GROUP), BF16),
            jax.ShapeDtypeStruct((HEADS, ROWS, ROWS), BF16),
        ],
        compiler_params=params("arbitrary", "arbitrary"),
        cost_estimate=pl.CostEstimate(flops=8 * ROWS * ROWS * GROUP, bytes_accessed=14 << 20, transcendentals=HEADS * ROWS * ROWS),
    )(bias, live, qkv, qkv, qkv)


def backward_kernel(live_ref, q_ref, k_ref, v_ref, grad_ref, soft_ref, out_ref, gk_ref, gv_ref):
    r = pl.program_id(1)
    scale = 1.0 / math.sqrt(HEAD_DIM)
    keys = k_ref[...].reshape(ROWS, HEAD_DIM)
    values = v_ref[...].reshape(ROWS, HEAD_DIM)

    @pl.when(r == 0)
    def _():
        gk_ref[...] = jnp.zeros_like(gk_ref)
        gv_ref[...] = jnp.zeros_like(gv_ref)

    for j in range(QB):
        grad = (grad_ref[j].astype(F32) * live_ref[j]).astype(BF16)
        soft_b = soft_ref[0, j * CAP : (j + 1) * CAP, :]
        soft = soft_b.astype(F32)
        dsoft = dot(grad, values, ((1,), (1,)))
        delta = jnp.sum(soft * dsoft, axis=1, keepdims=True)
        dscore = (soft * ((dsoft - delta) * scale)).astype(BF16)
        out_ref[r * QB + j, 0] = dot(dscore, keys, ((1,), (0,))).astype(BF16)
        gv_ref[...] += dot(grad, soft_b, ((0,), (0,)))
        gk_ref[...] += dot(q_ref[j, 0], dscore, ((0,), (0,)))

    @pl.when(r == NQ - 1)
    def _():
        out_ref[:, 1] = gk_ref[...].T.astype(BF16).reshape(NS, CAP, HEAD_DIM)
        out_ref[:, 2] = gv_ref[...].T.astype(BF16).reshape(NS, CAP, HEAD_DIM)


def backward(live, qkv, grad, soft):
    def part(i, rows):
        if rows == QB:
            return pl.BlockSpec((QB, 1, CAP, HEAD_DIM), lambda h, r: (r, i, 0, h))
        return pl.BlockSpec((NS, 1, CAP, HEAD_DIM), lambda h, r: (0, i, 0, h))

    return pl.pallas_call(
        backward_kernel,
        grid=(HEADS, NQ),
        in_specs=[
            pl.BlockSpec((QB, CAP, 1), lambda h, r: (r, 0, 0)),
            part(0, QB),
            part(1, NS),
            part(2, NS),
            pl.BlockSpec((QB, CAP, HEAD_DIM), lambda h, r: (r, 0, h)),
            pl.BlockSpec((1, QB * CAP, ROWS), lambda h, r: (h, r, 0)),
        ],
        out_specs=pl.BlockSpec((NS, 3, CAP, HEAD_DIM), lambda h, r: (0, 0, 0, h)),
        out_shape=jax.ShapeDtypeStruct((NS, 3, CAP, GROUP), BF16),
        scratch_shapes=[pltpu.VMEM((HEAD_DIM, ROWS), F32), pltpu.VMEM((HEAD_DIM, ROWS), F32)],
        compiler_params=params("arbitrary", "arbitrary"),
        cost_estimate=pl.CostEstimate(flops=16 * ROWS * ROWS * GROUP, bytes_accessed=18 << 20, transcendentals=0),
    )(live, qkv, qkv, qkv, grad, soft)


def split_kernel(core_ref, in_ref, out_ref):
    out_ref[0, 0] = in_ref[...]


def split_columns(core, rows):
    return pl.pallas_call(
        split_kernel,
        grid_spec=pltpu.PrefetchScalarGridSpec(
            num_scalar_prefetch=1,
            grid=(NX, 2),
            in_specs=[pl.BlockSpec((CAP, HALF), lambda x, h, core: (0, (h ^ core[0]) * NX + x))],
            out_specs=pl.BlockSpec((1, 1, CAP, HALF), lambda x, h, core: (x, h, 0, 0)),
        ),
        out_shape=jax.ShapeDtypeStruct((NX, 2, CAP, HALF), BF16),
        compiler_params=params("arbitrary", "arbitrary"),
        cost_estimate=pl.CostEstimate(flops=0, bytes_accessed=4 * CAP * D, transcendentals=0),
    )(core, rows)


def join_kernel(core_ref, in_ref, out_ref):
    out_ref[...] = in_ref[0, 0]


def join_columns(core, blocks):
    return pl.pallas_call(
        join_kernel,
        grid_spec=pltpu.PrefetchScalarGridSpec(
            num_scalar_prefetch=1,
            grid=(NX, 2),
            in_specs=[pl.BlockSpec((1, 1, CAP, HALF), lambda x, h, core: (x, h, 0, 0))],
            out_specs=pl.BlockSpec((CAP, HALF), lambda x, h, core: (0, (h ^ core[0]) * NX + x)),
        ),
        out_shape=jax.ShapeDtypeStruct((CAP, D), BF16),
        compiler_params=params("arbitrary", "arbitrary"),
        cost_estimate=pl.CostEstimate(flops=0, bytes_accessed=4 * CAP * D, transcendentals=0),
    )(core, blocks)


def grad_attn_kernel(cot_ref, own_ref, oth_ref, out_ref):
    own = cot_ref[:, 0].reshape(XROWS, HALF)
    oth = cot_ref[:, 1].reshape(XROWS, HALF)
    total = dot(own, own_ref[0], ((1,), (1,))) + dot(oth, oth_ref[0], ((1,), (1,)))
    out_ref[:, 0] = total.astype(BF16).reshape(NX, CAP, GROUP)


def grad_attn_part(cot, own, oth):
    weight = pl.BlockSpec((1, GROUP, HALF), lambda s: (s, 0, 0))
    return pl.pallas_call(
        grad_attn_kernel,
        grid=(NS,),
        in_specs=[pl.BlockSpec((NX, 2, CAP, HALF), lambda s: (0, 0, 0, 0)), weight, weight],
        out_specs=pl.BlockSpec((NX, 1, CAP, GROUP), lambda s: (0, s, 0, 0)),
        out_shape=jax.ShapeDtypeStruct((NX, NS, CAP, GROUP), BF16),
        compiler_params=params("arbitrary"),
        cost_estimate=pl.CostEstimate(flops=4 * XROWS * HALF * NS * GROUP, bytes_accessed=14 << 20, transcendentals=0),
    )(cot, own, oth)


def dense_kernel(core_ref, attn_ref, cot_ref, own_ref, oth_ref, out_ref, keep_ref, send_ref, acc_ref, turn_ref):
    s = pl.program_id(0)
    core = core_ref[0]
    third = HALF // 2

    @pl.when(s == 0)
    def _():
        acc_ref[...] = jnp.zeros_like(acc_ref)
        for h in range(2):
            turned = cot_ref[:, h].reshape(XROWS, HALF).T
            for c in range(2):
                rows = turned[c * third : (c + 1) * third]
                turn_ref[c ^ core, h ^ core] = rows

    rows = attn_ref[:, 0].reshape(XROWS, GROUP)
    acc_ref[0] += dot(rows, own_ref[0], ((1,), (0,)))
    acc_ref[1] += dot(rows, oth_ref[0], ((1,), (0,)))
    for zl in range(2):
        keep_ref[zl, 0] = dot(turn_ref[0, zl], rows, ((1,), (0,))).astype(BF16)
        send_ref[zl, 0] = dot(turn_ref[1, zl], rows, ((1,), (0,))).astype(BF16)

    @pl.when(s == NS - 1)
    def _():
        for h in range(2):
            out_ref[:, h] = acc_ref[h].astype(BF16).reshape(NX, CAP, HALF)


def dense(core, attn, cot, own, oth):
    weight = pl.BlockSpec((1, GROUP, HALF), lambda s, core: (s, 0, 0))
    wide = pl.BlockSpec((NX, 2, CAP, HALF), lambda s, core: (0, 0, 0, 0))
    grad = pl.BlockSpec((2, 1, HALF // 2, GROUP), lambda s, core: (0, s, 0, 0))
    return pl.pallas_call(
        dense_kernel,
        grid_spec=pltpu.PrefetchScalarGridSpec(
            num_scalar_prefetch=1,
            grid=(NS,),
            in_specs=[pl.BlockSpec((NX, 1, CAP, GROUP), lambda s, core: (0, s, 0, 0)), wide, weight, weight],
            out_specs=[wide, grad, grad],
            scratch_shapes=[
                pltpu.VMEM((2, XROWS, HALF), F32),
                pltpu.VMEM((2, 2, HALF // 2, XROWS), BF16),
            ],
        ),
        out_shape=[
            jax.ShapeDtypeStruct((NX, 2, CAP, HALF), BF16),
            jax.ShapeDtypeStruct((2, NS, HALF // 2, GROUP), BF16),
            jax.ShapeDtypeStruct((2, NS, HALF // 2, GROUP), BF16),
        ],
        compiler_params=params("arbitrary"),
        cost_estimate=pl.CostEstimate(flops=8 * XROWS * HALF * NS * GROUP, bytes_accessed=26 << 20, transcendentals=0),
    )(core, attn, cot, own, oth)


def other_core(value, n_dp):
    return lax.ppermute(value, ("zl", "x", "c"), [(i, i ^ 1) for i in range(n_dp)])


def swap(value, axes):
    return lax.all_to_all(value, axes, split_axis=0, concat_axis=0, tiled=True)


def on_device(query_all, key_all, value_all, out_weight, cotangent, visible, counts):
    n_dp = 4 * NX
    x = lax.axis_index("x")
    core = lax.axis_index("c")
    core_arg = core.astype(jnp.int32).reshape(1)
    place = lax.axis_index(SEQ)

    slots = jnp.arange(CAP, dtype=jnp.int32)
    alive_all = slots[None, :] < counts[0][:, None]
    own_count = jnp.sum(jnp.where(jnp.arange(NS, dtype=jnp.int32) == place, counts[0], 0))
    pick = jnp.where(slots < own_count, visible[0], -1)
    bias = jnp.where(alive_all, 0.0, -1e30).astype(F32).reshape(1, ROWS)
    live = alive_all.astype(F32)[:, :, None]

    mine = lax.dynamic_slice(out_weight, (0, core * (NX * HALF) + x * HALF), (GROUP, HALF))
    own = lax.all_gather(mine, SEQ, axis=0, tiled=False)
    oth = other_core(own, n_dp)

    qkv = swap(gather_rows(pick[:, None], query_all[0], key_all[0], value_all[0]), SEQ)
    cot = swap(split_columns(core_arg, cotangent[0]), "x")

    attn, soft = forward(bias, live, qkv)
    attn = swap(attn, SEQ)
    attn_x = lax.all_gather(attn, "x", axis=0, tiled=False)

    grad_part = grad_attn_part(cot, own, oth)
    grad_attn = lax.psum_scatter(grad_part, "x", scatter_dimension=0, tiled=False)
    grad_attn = swap(grad_attn, SEQ)

    out, keep, send = dense(core_arg, attn_x, cot, own, oth)
    output = join_columns(core_arg, swap(out, "x"))
    weight_part = (keep.astype(F32) + other_core(send, n_dp).astype(F32)).astype(BF16)
    weight_part = weight_part.reshape(2 * NS, HALF // 2, GROUP)
    grad_weight = lax.psum_scatter(weight_part, ("zl",) + SEQ, scatter_dimension=0, tiled=False)
    grad_weight = grad_weight.astype(F32).T

    grads = swap(backward(live, qkv, grad_attn, soft), SEQ)
    grad_query, grad_key, grad_value = scatter_rows(pick[None, :], grads)
    return (output[None], grad_query[None], grad_key[None], grad_value[None], grad_weight)


def solution(mesh):
    fine = Mesh(np.asarray(mesh.devices).reshape(2, NX, 2, 2, 4), AXES)
    dp = ("zl", "x", "c")
    return jax.shard_map(
        on_device,
        mesh=fine,
        in_specs=(
            P(dp, SEQ, None),
            P(dp, SEQ, None),
            P(dp, SEQ, None),
            P(SEQ, None),
            P(dp, SEQ, None),
            P(dp, SEQ),
            P(dp, None),
        ),
        out_specs=(
            P(dp, SEQ, None),
            P(dp, SEQ, None),
            P(dp, SEQ, None),
            P(dp, SEQ, None),
            P(SEQ, dp),
        ),
        check_vma=False,
    )
```

time: 469 us -> 359 us (0.77)
  matrix products: 138 us -> 0 us
  waiting for transfers between devices: 217 us -> 96.2 us
  blocking collectives: 0 us -> 106 us
  Pallas kernels: 0 us -> 100 us
  starting transfers between devices: 40.4 us -> 15.5 us
  local copies, waits for them, and re-layouts: 32.1 us -> 9.58 us
  other arithmetic: 20.6 us -> 12 us
    dot_general x8 -> x0, matrix products: 127 us -> none  [the longest x1 31.5 us: on_device(): jnp.einsum('hqk,khd->qhd', dscore, key_heads, preferred_element_type=jnp....]
    all_to_all x0 -> x3, blocking collectives: none -> 106 us  [swap(): return lax.all_to_all(value, axes, split_axis=0, concat_axis=0, tiled=True)]
    pallas_call x0 -> x8, Pallas kernels: none -> 100 us  [the longest x1 22.2 us: backward(): pl.pallas_call(backward_kernel, grid=(HEADS, NQ), in_specs=[pl.BlockSpec(...]
    reduce_scatter x2, waiting for transfers between devices: 78 us -> 11.1 us  [the longest x1 9.76 us: on_device(): lax.psum_scatter(grad_part, 'x', scatter_dimension=0, tiled=False)]
    all_gather x1 -> x2, waiting for transfers between devices: 66 us -> 0.03 us  [the longest x1 0.02 us: on_device(): own = lax.all_gather(mine, SEQ, axis=0, tiled=False)]
    all_to_all x6 -> x3, starting transfers between devices: 40.3 us -> 15.2 us  [swap(): return lax.all_to_all(value, axes, split_axis=0, concat_axis=0, tiled=True)]
    scatter-add x3 -> x0, other arithmetic: 14.8 us -> none  [the longest x1 5.36 us: on_device(): grad_query = empty.at[local_list].add(grad_query_rows)]
    all_to_all x9 -> x0, local copies, waits for them, and re-layouts: 11.9 us -> none  [the longest x2 3.94 us: on_device(): lax.all_to_all(grad_query_heads.reshape(total_rows, group_width), 'seq',...]
  transfers between devices with their start and end apart: 9 -> 9, of which waited for: 7 -> 5; matrix products, arithmetic and copies ran while one was open for 38% -> 3% of each run, Pallas kernels for 0% -> 28%
where the time goes in v1:
time: 359 us; the launch traced here: 354 us
  blocking collectives  106 us (30%)
  Pallas kernels  100 us (28%)
  waiting for transfers between devices  96.2 us (27%)
  starting transfers between devices  15.5 us (4%)
  between operations  13.9 us (4%)
  other arithmetic  12 us (3%)
  local copies, waits for them, and re-layouts  9.58 us (3%)
    all_to_all x3, blocking collectives, swap(): return lax.all_to_all(value, axes, split_axis=0, concat_axis=0, tiled=True)  106 us
    all_to_all x3, waiting for transfers between devices, swap(): return lax.all_to_all(value, axes, split_axis=0, concat_axis=0, tiled=True)  77.9 us
    pallas_call x1, Pallas kernels, backward(): pl.pallas_call(backward_kernel, grid=(HEADS, NQ), in_specs=[pl.BlockSpec(...  22.2 us
    pallas_call x1, Pallas kernels, dense(): pl.pallas_call(dense_kernel, grid_spec=pltpu.PrefetchScalarGridSpec(num_s...  21 us
    pallas_call x1, Pallas kernels, forward(): pl.pallas_call(forward_kernel, grid=(HEADS, NQ), in_specs=[pl.BlockSpec((...  18.7 us
    all_to_all x3, starting transfers between devices, swap(): return lax.all_to_all(value, axes, split_axis=0, concat_axis=0, tiled=True)  15.2 us
    pallas_call x1, Pallas kernels, grad_attn_part(): pl.pallas_call(grad_attn_kernel, grid=(NS,), in_specs=[pl.BlockSpec((NX,...  12.4 us
    reduce_scatter x1, waiting for transfers between devices, on_device(): lax.psum_scatter(grad_part, 'x', scatter_dimension=0, tiled=False)  9.76 us
  transfers between devices with their start and end apart: 9, of which 5 were waited for; matrix products, arithmetic and copies ran while one was open for 3% of the time, Pallas kernels for 28%

profile of v1, /device:TPU:0, one launch (start us, length us, event | category | flops | bytes accessed | tf_op | source)
XLA Modules:
  0.0 353.7 jit_solution(9295188994335661657)
XLA Ops:
  7.2 1.9 constant_dynamic-slice_fusion
  9.1 0.8 copy.13
  9.9 1.4 fusion.3
  11.3 1.3 fusion.1.pick_ref
  12.6 7.8 %shard_map.110 = bf16[8,3,160,384]{3,2,1,0:T(8,128)(2,1)} custom-call(s32[160,1]{1,0:T(8,128)} %fusion.1.pick_ref, bf16[256,3072]{1,0:T(8,128)(2,1)} %bitcast.24, bf16[256,3072]{1,0:T(8,128)(2,1)} %bitcast.25, bf16[256,3072]{1,0:T(8,128)(2,1)} %bitcast.26), custom_call_target="tpu_custom_call" | custom-call | flops 754974720 | bytes 8388608 | tf_op jit(solution)/shard_map/pallas_call | solution.py:47
  20.4 8.0 %all-to-all-start = ((bf16[8,3,160,384]{3,2,1,0:T(8,128)(2,1)}), bf16[8,3,160,384]{3,2,1,0:T(8,128)(2,1)S(1)}, u32[]{:S(2)}, u32[]{:S(2)}) async-start(bf16[8,3,160,384]{3,2,1,0:T(8,128)(2,1)} %shard_map.110), calls=%async_computation | async-start | bytes 5898240 | tf_op jit(solution)/shard_map/all_to_all | solution.py:297
  28.6 0.7 select_n.36.bias_ref
  29.2 0.9 fusion.live_ref
  30.2 40.1 %all-to-all-done.q_ref.k_ref.v_ref = bf16[8,3,160,384]{3,2,1,0:T(8,128)(2,1)S(1)} async-done(((bf16[8,3,160,384]{3,2,1,0:T(8,128)(2,1)}), bf16[8,3,160,384]{3,2,1,0:T(8,128)(2,1)S(1)}, u32[]{:S(2)}, u32[]{:S(2)}) %all-to-all-start) | async-done | bytes 2949152 | tf_op jit(solution)/shard_map/all_to_all | solution.py:297
  70.2 1.6 copy-done.2
  71.8 18.7 %shard_map.111 = (bf16[8,160,384]{2,1,0:T(8,128)(2,1)}, bf16[3,1280,1280]{2,1,0:T(8,128)(2,1)}) custom-call(f32[1,1280]{1,0:T(1,128)} %select_n.36.bias_ref, f32[8,160,1]{2,1,0:T(8,128)} %fusion.live_ref, bf16[8,3,160,384]{3,2,1,0:T(8,128)(2,1)} %copy-done.2, bf16[8,3,160,384]{3,2,1,0:T(8,128)(2,1)} %copy-done.2, bf16[8,3,160,384]{3,2,1,0:T(8,128)(2,1)} %copy-done.2), custom_call_target="tpu_custom_call" | custom-call | flops 5033164800 | bytes 14680064 | tf_op jit(solution)/shard_map/pallas_call | solution.py:105
  90.5 31.6 %all_to_all.30 = bf16[8,160,384]{2,1,0:T(8,128)(2,1)} all-to-all(bf16[8,160,384]{2,1,0:T(8,128)(2,1)} %get-tuple-element.13), channel_id=1, replica_groups=mesh['zl'=2,'x'=4,'c'=2,'zh'=2,'y'=4] {'zh','y'}, dimensions={0} | all-to-all | bytes 1966080 | tf_op jit(solution)/shard_map/all_to_all | solution.py:297
  122.3 5.5 %shard_map.112 = bf16[4,2,160,640]{3,2,1,0:T(8,128)(2,1)} custom-call(s32[1]{0:T(128)} %bitcast.core_ref, bf16[160,5120]{1,0:T(8,128)(2,1)} %bitcast.22), custom_call_target="tpu_custom_call" | custom-call | bytes 3276800 | tf_op jit(solution)/shard_map/pallas_call | solution.py:186
  127.8 44.4 %all_to_all.31.cot_ref = bf16[4,2,160,640]{3,2,1,0:T(8,128)(2,1)} all-to-all(bf16[4,2,160,640]{3,2,1,0:T(8,128)(2,1)} %shard_map.112), channel_id=1, replica_groups=mesh['zl'=2,'x'=4,'c'=2,'zh'=2,'y'=4] {'x'}, dimensions={0} | all-to-all | bytes 3276800 | tf_op jit(solution)/shard_map/all_to_all | solution.py:297
  172.2 1.9 copy-done.5
  174.1 12.4 %shard_map.115 = bf16[4,8,160,384]{3,2,1,0:T(8,128)(2,1)} custom-call(bf16[4,2,160,640]{3,2,1,0:T(8,128)(2,1)} %all_to_all.31.cot_ref, bf16[8,384,640]{2,1,0:T(8,128)(2,1)} %bitcast.32, bf16[8,384,640]{2,1,0:T(8,128)(2,1)} %copy-done.5), custom_call_target="tpu_custom_call" | custom-call | flops 5033164800 | bytes 14680064 | tf_op jit(solution)/shard_map/pallas_call | solution.py:228
  186.6 21.0 %shard_map.113 = (bf16[4,2,160,640]{3,2,1,0:T(8,128)(2,1)}, bf16[2,8,320,384]{3,2,1,0:T(8,128)(2,1)}, bf16[2,8,320,384]{3,2,1,0:T(8,128)(2,1)}) custom-call(s32[1]{0:T(128)} %bitcast.core_ref, bf16[4,8,160,384]{3,2,1,0:T(8,128)(2,1)} %bitcast.34, bf16[4,2,160,640]{3,2,1,0:T(8,128)(2,1)} %all_to_all.31.cot_ref, bf16[8,384,640]{2,1,0:T(8,128)(2,1)} %bitcast.33, ...), custom_call_target="tpu_custom_call" | custom-call | flops 10066329600 | bytes 27262976 | tf_op jit(solution)/shard_map/pallas_call | solution.py:270
  207.6 7.0 %collective-permute-done.1 = bf16[2,8,320,384]{3,2,1,0:T(8,128)(2,1)S(1)} collective-permute-done((bf16[2,8,320,384]{3,2,1,0:T(8,128)(2,1)}, bf16[2,8,320,384]{3,2,1,0:T(8,128)(2,1)S(1)}, u32[]{:S(2)}, u32[]{:S(2)}) %collective-permute-start.1) | collective-permute-done | bytes 3932192 | tf_op jit(solution)/shard_map/ppermute | solution.py:293
  214.6 5.3 %add_convert_fusion = bf16[2,8,320,384]{3,2,1,0:T(8,128)(2,1)} fusion(bf16[2,8,320,384]{3,2,1,0:T(8,128)(2,1)S(1)} %collective-permute-done.1, bf16[2,8,320,384]{3,2,1,0:T(8,128)(2,1)} %get-tuple-element.19), kind=kLoop, calls=%fused_computation | loop fusion | flops 7864320 | bytes 11796480 | tf_op jit(solution)/shard_map/convert_element_type | solution.py:331
  219.9 9.8 %reduce-scatter.3.cloned.1.call-done = bf16[1,8,160,384]{3,2,1,0:T(8,128)(2,1)} async-done(((bf16[4,8,160,384]{3,2,1,0:T(8,128)(2,1)}), bf16[1,8,160,384]{3,2,1,0:T(8,128)(2,1)}) %reduce-scatter.3.cloned.1.call-update) | async-done | bytes 983056 | tf_op jit(solution)/shard_map/reduce_scatter | solution.py:326
  229.7 30.3 %all_to_all.32.grad_ref = bf16[8,160,384]{2,1,0:T(8,128)(2,1)} all-to-all(bf16[8,160,384]{2,1,0:T(8,128)(2,1)} %bitcast.27), channel_id=1, replica_groups=mesh['zl'=2,'x'=4,'c'=2,'zh'=2,'y'=4] {'zh','y'}, dimensions={0} | all-to-all | bytes 1966080 | tf_op jit(solution)/shard_map/all_to_all | solution.py:297
  259.9 3.6 %all-to-all-start.3 = ((bf16[4,2,160,640]{3,2,1,0:T(8,128)(2,1)}), bf16[4,2,160,640]{3,2,1,0:T(8,128)(2,1)S(1)}, u32[]{:S(2)}, u32[]{:S(2)}) async-start(bf16[4,2,160,640]{3,2,1,0:T(8,128)(2,1)} %get-tuple-element.14), calls=%async_computation.3 | async-start | bytes 3276800 | tf_op jit(solution)/shard_map/all_to_all | solution.py:297
  263.5 22.2 %shard_map.116 = bf16[8,3,160,384]{3,2,1,0:T(8,128)(2,1)} custom-call(f32[8,160,1]{2,1,0:T(8,128)} %fusion.live_ref, bf16[8,3,160,384]{3,2,1,0:T(8,128)(2,1)} %copy-done.2, bf16[8,3,160,384]{3,2,1,0:T(8,128)(2,1)} %copy-done.2, bf16[8,3,160,384]{3,2,1,0:T(8,128)(2,1)} %copy-done.2, bf16[8,160,384]{2,1,0:T(8,128)(2,1)} %all_to_all.32.grad_ref, ...), custom_call_target="tpu_custom_call" | custom-call | flops 10066329600 | bytes 18874368 | tf_op jit(solution)/shard_map/pallas_call | solution.py:162
  285.8 1.2 copy-done.1
  286.9 3.6 %all-to-all-start.5 = ((bf16[8,3,160,384]{3,2,1,0:T(8,128)(2,1)}), bf16[8,3,160,384]{3,2,1,0:T(8,128)(2,1)S(1)}, u32[]{:S(2)}, u32[]{:S(2)}) async-start(bf16[8,3,160,384]{3,2,1,0:T(8,128)(2,1)} %shard_map.116), calls=%async_computation.6 | async-start | bytes 5898240 | tf_op jit(solution)/shard_map/all_to_all | solution.py:297
  290.6 1.3 compare_select_fusion.pick_ref
  291.9 5.5 %shard_map.114 = bf16[160,5120]{1,0:T(8,128)(2,1)} custom-call(s32[1]{0:T(128)} %bitcast.core_ref, bf16[4,2,160,640]{3,2,1,0:T(8,128)(2,1)} %copy-done.1), custom_call_target="tpu_custom_call" | custom-call | bytes 3276800 | tf_op jit(solution)/shard_map/pallas_call | solution.py:205
  297.3 37.9 %all-to-all-done.5.rows_ref = bf16[8,3,160,384]{3,2,1,0:T(8,128)(2,1)S(1)} async-done(((bf16[8,3,160,384]{3,2,1,0:T(8,128)(2,1)}), bf16[8,3,160,384]{3,2,1,0:T(8,128)(2,1)S(1)}, u32[]{:S(2)}, u32[]{:S(2)}) %all-to-all-start.5) | async-done | bytes 2949152 | tf_op jit(solution)/shard_map/all_to_all | solution.py:297
  335.2 1.6 copy-done
  336.8 7.2 %shard_map.117 = (bf16[256,3072]{1,0:T(8,128)(2,1)}, bf16[256,3072]{1,0:T(8,128)(2,1)}, bf16[256,3072]{1,0:T(8,128)(2,1)}) custom-call(s32[1,160]{1,0:T(1,128)} %compare_select_fusion.pick_ref, bf16[8,3,160,384]{3,2,1,0:T(8,128)(2,1)} %copy-done), custom_call_target="tpu_custom_call" | custom-call | flops 754974720 | bytes 8388608 | tf_op jit(solution)/shard_map/pallas_call | solution.py:67
  344.0 1.4 reduce-scatter.5.cloned.1.call-done
  345.4 1.8 convert_bitcast_fusion
  (23 shorter events, 0.4 us)
Async XLA Ops:
  7.2 115.0 %all-gather.7.cloned.1.call-start = ((), (), s32[]{:S(2)}) async-start(), calls=%async_computation.11 | async-start | bytes 4423680 | tf_op jit(solution)/shard_map/all_gather | solution.py:315
  20.4 8.0 %copy-start.4 = (s32[1,8]{1,0:T(1,128)S(1)}, s32[1,8]{1,0:T(1,128)}, u32[]{:S(2)}) copy-start(s32[1,8]{1,0:T(1,128)} %param.13) | copy-start | bytes 100
  20.4 49.8 %all-to-all-start = ((bf16[8,3,160,384]{3,2,1,0:T(8,128)(2,1)}), bf16[8,3,160,384]{3,2,1,0:T(8,128)(2,1)S(1)}, u32[]{:S(2)}, u32[]{:S(2)}) async-start(bf16[8,3,160,384]{3,2,1,0:T(8,128)(2,1)} %shard_map.110), calls=%async_computation | async-start | bytes 5898240 | tf_op jit(solution)/shard_map/all_to_all | solution.py:297
  28.4 158.2 %all-gather.5.cloned.1.call-start = ((), (), s32[]{:S(2)}) async-start(), calls=%async_computation.10 | async-start | bytes 4915200 | tf_op jit(solution)/shard_map/all_gather | solution.py:323
  70.2 1.6 copy-start.2
  122.1 107.5 %reduce-scatter.3.cloned.1.call-start = ((), (), s32[]{:S(2)}) async-start(), calls=%async_computation.8 | async-start | bytes 4915200 | tf_op jit(solution)/shard_map/reduce_scatter | solution.py:326
  122.2 50.0 %collective-permute-start = (bf16[8,384,640]{2,1,0:T(8,128)(2,1)}, bf16[8,384,640]{2,1,0:T(8,128)(2,1)S(1)}, u32[]{:S(2)}, u32[]{:S(2)}) collective-permute-start(bf16[8,384,640]{2,1,0:T(8,128)(2,1)} %bitcast.31), channel_id=1, source_target_pairs={{0,8},{8,0},{16,24},{24,16},{32,40},{40,32},{48,56},{56,48},{64,72... | collective-permute-start | bytes 11796488 | tf_op jit(solution)/shard_map/ppermute | solution.py:293
  172.2 1.9 copy-start.5
  186.5 158.8 %reduce-scatter.5.cloned.1.call-start = ((), (), s32[]{:S(2)}) async-start(), calls=%async_computation.9 | async-start | bytes 4177920 | tf_op jit(solution)/shard_map/reduce_scatter | solution.py:333
  207.6 7.0 %collective-permute-start.1 = (bf16[2,8,320,384]{3,2,1,0:T(8,128)(2,1)}, bf16[2,8,320,384]{3,2,1,0:T(8,128)(2,1)S(1)}, u32[]{:S(2)}, u32[]{:S(2)}) collective-permute-start(bf16[2,8,320,384]{3,2,1,0:T(8,128)(2,1)} %get-tuple-element.20), channel_id=1, source_target_pairs={{0,8},{8,0},{16,24},{24,16},{32,40},{40,32},{48,56},{56,48},{64,72... | collective-permute-start | bytes 11796488 | tf_op jit(solution)/shard_map/ppermute | solution.py:293
  259.9 25.8 %all-to-all-start.3 = ((bf16[4,2,160,640]{3,2,1,0:T(8,128)(2,1)}), bf16[4,2,160,640]{3,2,1,0:T(8,128)(2,1)S(1)}, u32[]{:S(2)}, u32[]{:S(2)}) async-start(bf16[4,2,160,640]{3,2,1,0:T(8,128)(2,1)} %get-tuple-element.14), calls=%async_computation.3 | async-start | bytes 3276800 | tf_op jit(solution)/shard_map/all_to_all | solution.py:297
  285.8 4.8 %copy-start.3 = (s32[1,160]{1,0:T(1,128)S(1)}, s32[1,160]{1,0:T(1,128)}, u32[]{:S(2)}) copy-start(s32[1,160]{1,0:T(1,128)} %param.12) | copy-start | bytes 1924
  285.8 1.2 copy-start.1
  286.9 48.3 %all-to-all-start.5 = ((bf16[8,3,160,384]{3,2,1,0:T(8,128)(2,1)}), bf16[8,3,160,384]{3,2,1,0:T(8,128)(2,1)S(1)}, u32[]{:S(2)}, u32[]{:S(2)}) async-start(bf16[8,3,160,384]{3,2,1,0:T(8,128)(2,1)} %shard_map.116), calls=%async_computation.6 | async-start | bytes 5898240 | tf_op jit(solution)/shard_map/all_to_all | solution.py:297
  335.2 1.6 copy-start
Sparse Core Ops, SparseCore 0:
  10.9 110.1 all-gather.6
  122.7 62.4 all-gather.4
  187.6 41.9 reduce-scatter.2
  231.9 113.3 reduce-scatter.4

commit v2 on v1

v2 whole, which is shorter than its diff:
```python
import functools
import math

import jax
import jax.numpy as jnp
import numpy as np
from jax import lax
from jax.experimental import pallas as pl
from jax.experimental.pallas import tpu as pltpu
from jax.sharding import Mesh, PartitionSpec as P

HEAD_DIM = 128
HEADS = 3
GROUP = HEADS * HEAD_DIM
CAP = 160
TOK = 256
NS = 8
NX = 4
D = 5120
HALF = D // (2 * NX)
ROWS = NS * CAP
XROWS = NX * CAP
VMEM = 56 * 1024 * 1024
F32 = jnp.float32
BF16 = jnp.bfloat16
BRIEF = pl.CostEstimate(flops=1, bytes_accessed=1, transcendentals=0)
LONG = pl.CostEstimate(flops=2 * 10**11, bytes_accessed=1, transcendentals=0)
AXES = ("zl", "x", "c", "zh", "y")
SEQ = ("zh", "y")


def params(*semantics):
    return pltpu.CompilerParams(dimension_semantics=semantics, vmem_limit_bytes=VMEM)


def dot(a, b, dims):
    return lax.dot_general(a, b, (dims, ((), ())), preferred_element_type=F32)


def gather_kernel(pick_ref, q_ref, k_ref, v_ref, out_ref):
    token = lax.broadcasted_iota(jnp.int32, (CAP, TOK), 1)
    hot = (token == pick_ref[...]).astype(F32).astype(BF16)
    for i, ref in enumerate((q_ref, k_ref, v_ref)):
        out_ref[0, i] = dot(hot, ref[...], ((1,), (0,))).astype(BF16)


def gather_rows(pick, q, k, v):
    block = pl.BlockSpec((TOK, GROUP), lambda s: (0, s))
    return pl.pallas_call(
        gather_kernel,
        grid=(NS,),
        in_specs=[pl.BlockSpec((CAP, 1), lambda s: (0, 0)), block, block, block],
        out_specs=pl.BlockSpec((1, 3, CAP, GROUP), lambda s: (s, 0, 0, 0)),
        out_shape=jax.ShapeDtypeStruct((NS, 3, CAP, GROUP), BF16),
        compiler_params=params("arbitrary"),
        cost_estimate=BRIEF,
    )(pick, q, k, v)


def scatter_kernel(pick_ref, first_ref, rest_ref, q_ref, k_ref, v_ref):
    token = lax.broadcasted_iota(jnp.int32, (TOK, CAP), 0)
    hot = (token == pick_ref[...]).astype(F32).astype(BF16)
    for i, ref in enumerate((q_ref, k_ref, v_ref)):
        rows = jnp.concatenate([first_ref[0, i], rest_ref[0, i]], axis=1)
        ref[...] = dot(hot, rows, ((1,), (0,))).astype(BF16)


def scatter_rows(pick, first, rest):
    block = pl.BlockSpec((TOK, GROUP), lambda s: (0, s))
    return pl.pallas_call(
        scatter_kernel,
        grid=(NS,),
        in_specs=[
            pl.BlockSpec((1, CAP), lambda s: (0, 0)),
            pl.BlockSpec((1, 3, CAP, GROUP - HEAD_DIM), lambda s: (s, 0, 0, 0)),
            pl.BlockSpec((1, 3, CAP, HEAD_DIM), lambda s: (s, 0, 0, 0)),
        ],
        out_specs=[block] * 3,
        out_shape=[jax.ShapeDtypeStruct((TOK, NS * GROUP), BF16)] * 3,
        compiler_params=params("arbitrary"),
        cost_estimate=BRIEF,
    )(pick, first, rest)


QB = 4
NQ = NS // QB
COLUMN = pl.BlockSpec((QB, CAP, 1), lambda h, r: (r, 0, 0))
HEAD_COLUMN = pl.BlockSpec((1, QB, CAP, 1), lambda h, r: (h, r, 0, 0))
HEAD_ROWS = pl.BlockSpec((QB, CAP, HEAD_DIM), lambda h, r: (r, 0, h))
HEAD_SQUARE = pl.BlockSpec((1, QB * CAP, ROWS), lambda h, r: (h, r, 0))


def some_rows(i):
    return pl.BlockSpec((QB, 1, CAP, HEAD_DIM), lambda h, r: (r, i, 0, h))


def all_rows(i):
    return pl.BlockSpec((NS, 1, CAP, HEAD_DIM), lambda h, r: (0, i, 0, h))


def forward_kernel(bias_ref, live_ref, q_ref, k_ref, v_ref, attn_ref, expo_ref, inv_ref):
    scale = math.log2(math.e) / math.sqrt(HEAD_DIM)
    keys = k_ref[...].reshape(ROWS, HEAD_DIM)
    values = v_ref[...].reshape(ROWS, HEAD_DIM)
    bias = bias_ref[...]
    for j in range(QB):
        scores = dot(q_ref[j, 0], keys, ((1,), (1,))) + bias
        top = jnp.max(scores, axis=1, keepdims=True)
        expo = jnp.exp2((scores - top) * scale)
        inv = 1.0 / jnp.sum(expo, axis=1, keepdims=True)
        expo = expo.astype(BF16)
        expo_ref[0, j * CAP : (j + 1) * CAP, :] = expo
        inv_ref[0, j] = inv
        attn_ref[j] = (dot(expo, values, ((1,), (0,))) * (inv * live_ref[j])).astype(BF16)


def forward(bias, live, qkv):
    return pl.pallas_call(
        forward_kernel,
        grid=(HEADS, NQ),
        in_specs=[pl.BlockSpec((1, ROWS), lambda h, r: (0, 0)), COLUMN, some_rows(0), all_rows(1), all_rows(2)],
        out_specs=[HEAD_ROWS, HEAD_SQUARE, HEAD_COLUMN],
        out_shape=[
            jax.ShapeDtypeStruct((NS, CAP, GROUP), BF16),
            jax.ShapeDtypeStruct((HEADS, ROWS, ROWS), BF16),
            jax.ShapeDtypeStruct((HEADS, NS, CAP, 1), F32),
        ],
        compiler_params=params("arbitrary", "arbitrary"),
        cost_estimate=LONG,
    )(bias, live, qkv, qkv, qkv)


def backward_kernel(live_ref, q_ref, k_ref, v_ref, grad_ref, expo_ref, inv_ref, out_ref, gk_ref, gv_ref):
    r = pl.program_id(1)
    scale = 1.0 / math.sqrt(HEAD_DIM)
    keys = k_ref[...].reshape(ROWS, HEAD_DIM)
    values = v_ref[...].reshape(ROWS, HEAD_DIM)

    @pl.when(r == 0)
    def _():
        gk_ref[...] = jnp.zeros_like(gk_ref)
        gv_ref[...] = jnp.zeros_like(gv_ref)

    for j in range(QB):
        inv = inv_ref[0, j]
        grad = (grad_ref[j].astype(F32) * live_ref[j]).astype(BF16)
        expo_b = expo_ref[0, j * CAP : (j + 1) * CAP, :]
        expo = expo_b.astype(F32)
        dsoft = dot(grad, values, ((1,), (1,)))
        delta = jnp.sum(expo * dsoft, axis=1, keepdims=True) * inv
        dscore = (expo * ((dsoft - delta) * (inv * scale))).astype(BF16)
        out_ref[r * QB + j, 0] = dot(dscore, keys, ((1,), (0,))).astype(BF16)
        gv_ref[...] += dot((grad.astype(F32) * inv).astype(BF16), expo_b, ((0,), (0,)))
        gk_ref[...] += dot(q_ref[j, 0], dscore, ((0,), (0,)))

    @pl.when(r == NQ - 1)
    def _():
        out_ref[:, 1] = gk_ref[...].T.astype(BF16).reshape(NS, CAP, HEAD_DIM)
        out_ref[:, 2] = gv_ref[...].T.astype(BF16).reshape(NS, CAP, HEAD_DIM)


def backward(live, qkv, grad, expo, inv, first, count):
    def at(spec, axis):
        def index(h, r):
            place = list(spec.index_map(h, r))
            place[axis] = place[axis] + first
            return tuple(place)

        return pl.BlockSpec(spec.block_shape, index)

    rows = at(HEAD_ROWS, 2)
    return pl.pallas_call(
        backward_kernel,
        grid=(count, NQ),
        in_specs=[
            COLUMN,
            at(some_rows(0), 3),
            at(all_rows(1), 3),
            at(all_rows(2), 3),
            rows,
            at(HEAD_SQUARE, 0),
            at(HEAD_COLUMN, 0),
        ],
        out_specs=pl.BlockSpec((NS, 3, CAP, HEAD_DIM), lambda h, r: (0, 0, 0, h)),
        out_shape=jax.ShapeDtypeStruct((NS, 3, CAP, count * HEAD_DIM), BF16),
        scratch_shapes=[pltpu.VMEM((HEAD_DIM, ROWS), F32), pltpu.VMEM((HEAD_DIM, ROWS), F32)],
        compiler_params=params("arbitrary", "arbitrary"),
        cost_estimate=LONG,
    )(live, qkv, qkv, qkv, grad, expo, inv)


def column(place_ref, x, h):
    block = (h ^ place_ref[1]) * NX + x
    return pl.ds(pl.multiple_of(block * HALF, HALF), HALF)


def split_kernel(place_ref, in_ref, out_ref):
    for x in range(NX):
        for h in range(2):
            out_ref[x, h] = in_ref[:, column(place_ref, x, h)]


SMEM = pl.BlockSpec(memory_space=pltpu.SMEM)


def split_columns(place, rows):
    return pl.pallas_call(
        split_kernel,
        in_specs=[SMEM, pl.BlockSpec(memory_space=pltpu.VMEM)],
        out_specs=pl.BlockSpec(memory_space=pltpu.VMEM),
        out_shape=jax.ShapeDtypeStruct((NX, 2, CAP, HALF), BF16),
        compiler_params=params(),
        cost_estimate=BRIEF,
    )(place, rows)


def join_kernel(place_ref, in_ref, out_ref):
    for x in range(NX):
        for h in range(2):
            out_ref[:, column(place_ref, x, h)] = in_ref[x, h]


def join_columns(place, blocks):
    return pl.pallas_call(
        join_kernel,
        in_specs=[SMEM, pl.BlockSpec(memory_space=pltpu.VMEM)],
        out_specs=pl.BlockSpec(memory_space=pltpu.VMEM),
        out_shape=jax.ShapeDtypeStruct((CAP, D), BF16),
        compiler_params=params(),
        cost_estimate=BRIEF,
    )(place, blocks)


def x_exchange(blocks):
    return lax.all_to_all(blocks, "x", split_axis=0, concat_axis=0, tiled=True)


def whole_block(shape):
    return pl.BlockSpec(shape, lambda s, place: (0,) * len(shape))


LOW = GROUP // 2
UPPER = pl.BlockSpec((1, LOW, HALF), lambda s, place: (s, 0, 0))
LOWER = pl.BlockSpec((2, 1, LOW, HALF), lambda s, place: (0, s, 0, 0))
PAIR = pl.BlockSpec((NX, 2, 1, CAP, GROUP), lambda s, place: (0, 0, s, 0, 0))


def weight_rows(up, far, low):
    return jnp.concatenate([up[0], low[0, 0], far[0], low[1, 0]], axis=0)


def grad_attn_kernel(place_ref, in_ref, u0, f0, l0, u1, f1, l1, out_ref, cot_ref):
    @pl.when(pl.program_id(0) == 0)
    def _():
        for j in range(NX):
            for h in range(2):
                cot_ref[h, j * CAP : (j + 1) * CAP] = in_ref[j, h]

    total = dot(cot_ref[0], weight_rows(u0, f0, l0), ((1,), (1,)))
    total = (total + dot(cot_ref[1], weight_rows(u1, f1, l1), ((1,), (1,)))).astype(BF16)
    for j in range(NX):
        for i in range(2):
            part = total[j * CAP : (j + 1) * CAP, i * GROUP : (i + 1) * GROUP]
            out_ref[j, place_ref[2] ^ i, 0] = part


def grad_attn_part(place, cot, pieces):
    return pl.pallas_call(
        grad_attn_kernel,
        grid_spec=pltpu.PrefetchScalarGridSpec(
            num_scalar_prefetch=1,
            grid=(NS // 2,),
            in_specs=[whole_block((NX, 2, CAP, HALF))] + [UPPER, UPPER, LOWER] * 2,
            out_specs=PAIR,
            scratch_shapes=[pltpu.VMEM((2, XROWS, HALF), BF16)],
        ),
        out_shape=jax.ShapeDtypeStruct((NX, 2, NS // 2, CAP, GROUP), BF16),
        compiler_params=params("arbitrary"),
        cost_estimate=LONG,
    )(place, cot, *pieces).reshape(NX, NS, CAP, GROUP)


def ring_rows(ref, i):
    return ref[:, i, 0].reshape(XROWS, GROUP)


PIECE = HALF // 4


def weight_kernel(place_ref, attn_ref, cot_ref, keep_ref, send_ref, turn_ref):
    core = place_ref[1]

    @pl.when(pl.program_id(0) == 0)
    def _():
        for h in range(2):
            for j in range(NX):
                turned = cot_ref[j, h].T
                for c in range(2):
                    part = turned[2 * c * PIECE : 2 * (c + 1) * PIECE]
                    turn_ref[c ^ core, h ^ core, :, j * CAP : (j + 1) * CAP] = part

    rows = jnp.concatenate([ring_rows(attn_ref, i) for i in range(2)], axis=1)
    for other, ref in enumerate((keep_ref, send_ref)):
        for zl in range(2):
            total = dot(turn_ref[other, zl], rows, ((1,), (0,))).astype(BF16)
            for i in range(2):
                for p in range(2):
                    ref[p, zl, i, 0] = total[p * PIECE : (p + 1) * PIECE, i * GROUP : (i + 1) * GROUP]


def weight_part(place, attn, cot):
    grad = pl.BlockSpec((2, 2, 2, 1, PIECE, GROUP), lambda s, place: (0, 0, 0, s, 0, 0))
    return pl.pallas_call(
        weight_kernel,
        grid_spec=pltpu.PrefetchScalarGridSpec(
            num_scalar_prefetch=1,
            grid=(NS // 2,),
            in_specs=[PAIR, whole_block((NX, 2, CAP, HALF))],
            out_specs=[grad, grad],
            scratch_shapes=[pltpu.VMEM((2, 2, 2 * PIECE, XROWS), BF16)],
        ),
        out_shape=[jax.ShapeDtypeStruct((2, 2, 2, NS // 2, PIECE, GROUP), BF16)] * 2,
        compiler_params=params("arbitrary"),
        cost_estimate=BRIEF,
    )(place, attn, cot)


def out_kernel(place_ref, attn_ref, u0, f0, l0, u1, f1, l1, out_ref, acc_ref):
    s = pl.program_id(0)

    @pl.when(s == 0)
    def _():
        acc_ref[...] = jnp.zeros_like(acc_ref)

    rows = jnp.concatenate([ring_rows(attn_ref, place_ref[2] ^ i) for i in range(2)], axis=1)
    acc_ref[0] += dot(rows, weight_rows(u0, f0, l0), ((1,), (0,)))
    acc_ref[1] += dot(rows, weight_rows(u1, f1, l1), ((1,), (0,)))

    @pl.when(s == NS // 2 - 1)
    def _():
        for j in range(NX):
            for h in range(2):
                out_ref[j, h] = acc_ref[h, j * CAP : (j + 1) * CAP].astype(BF16)


def out_part(place, attn, pieces):
    return pl.pallas_call(
        out_kernel,
        grid_spec=pltpu.PrefetchScalarGridSpec(
            num_scalar_prefetch=1,
            grid=(NS // 2,),
            in_specs=[PAIR] + [UPPER, UPPER, LOWER] * 2,
            out_specs=whole_block((NX, 2, CAP, HALF)),
            scratch_shapes=[pltpu.VMEM((2, XROWS, HALF), F32)],
        ),
        out_shape=jax.ShapeDtypeStruct((NX, 2, CAP, HALF), BF16),
        compiler_params=params("arbitrary"),
        cost_estimate=LONG,
    )(place, attn, *pieces)


def other_core(value):
    return lax.ppermute(value, "c", [(0, 1), (1, 0)])


def swap(value):
    return lax.all_to_all(value, SEQ, split_axis=0, concat_axis=0, tiled=True)


def after(value, *others):
    return lax.optimization_barrier((value,) + others)[0]


def along_y(value, k):
    return lax.ppermute(value, "y", [(p, (p + k) % 4) for p in range(4)])


def along_z(value, k):
    index = [0, 2, 1, 3]
    return lax.ppermute(value, ("zl", "zh"), [(index[z], index[(z + k) % 4]) for z in range(4)])


def next_half(value):
    return lax.ppermute(value, ("zl", "zh"), [(0, 3), (3, 0), (2, 1), (1, 2)])


def add(values):
    return functools.reduce(jnp.add, [v.astype(F32) for v in values])


def projection(out_weight, x, core, y, rows):
    mine = lax.dynamic_slice(out_weight, (0, core * (NX * HALF) + x * HALF), (GROUP, HALF))

    def gather(value):
        parts = [value] + [along_y(value, k) for k in (1, 3, 2)]
        zero = jnp.zeros((4,) + value.shape, BF16)
        for k, part in zip((0, -1, 1, 2), parts):
            zero = lax.dynamic_update_slice_in_dim(zero, part[None], (y + k) % 4, 0)
        return zero

    up = gather(mine[:LOW])
    low = jnp.stack([mine[LOW:], next_half(mine[LOW:])])
    up, low, rows = lax.optimization_barrier((up, low, rows))
    far = next_half(up)
    low = jnp.moveaxis(gather(low), 0, 1)
    return [up, far, low], rows


def cut_kernel(place_ref, keep_ref, got_ref, z0, z1, z2, z3, y0, y1, y2, y3):
    for k, (z_ref, y_ref) in enumerate(zip((z0, z1, z2, z3), (y0, y1, y2, y3))):
        z = lax.rem(2 * place_ref[2] + place_ref[4] + k, 4)
        zl, zh, y = lax.rem(z, 2), z // 2, lax.rem(place_ref[3] + k, 4)
        z_ref[...] = (keep_ref[0, zl, zh].astype(F32) + got_ref[0, zl, zh].astype(F32)).astype(BF16)
        for i in range(2):
            for j in range(2):
                y_ref[i, j] = (keep_ref[1, i, j, y].astype(F32) + got_ref[1, i, j, y].astype(F32)).astype(BF16)


def cut_pieces(place, keep, got):
    vmem = pl.BlockSpec(memory_space=pltpu.VMEM)
    out = pl.pallas_call(
        cut_kernel,
        in_specs=[SMEM, vmem, vmem],
        out_specs=[vmem] * 8,
        out_shape=[jax.ShapeDtypeStruct((4, PIECE, GROUP), BF16)] * 4
        + [jax.ShapeDtypeStruct((2, 2, PIECE, GROUP), BF16)] * 4,
        compiler_params=params(),
        cost_estimate=BRIEF,
    )(place, keep, got)
    return out[:4], out[4:]


def ring(along, parts):
    return add([parts[0]] + [along(parts[k], k) for k in (1, 3, 2)])


def second_phase(first, second, place):
    zh, y, zl = place[2], place[3], place[4]
    first = [lax.dynamic_index_in_dim(first, (y + k) % 4, 0, keepdims=False) for k in range(4)]
    z = [(2 * zh + zl + k) % 4 for k in range(4)]
    second = [lax.dynamic_slice(second, (k % 2, k // 2, 0, 0), (1, 1, PIECE, GROUP))[0, 0] for k in z]
    return jnp.concatenate([ring(along_y, first), ring(along_z, second)])


def on_device(query_all, key_all, value_all, out_weight, cotangent, visible, counts):
    x, core, zh, y, zl = [lax.axis_index(a).astype(jnp.int32) for a in ("x", "c", "zh", "y", "zl")]
    place = jnp.stack([x, core, zh, y, zl])
    shard = 4 * zh + y

    slots = jnp.arange(CAP, dtype=jnp.int32)
    alive_all = slots[None, :] < counts[0][:, None]
    own_count = jnp.sum(jnp.where(jnp.arange(NS, dtype=jnp.int32) == shard, counts[0], 0))
    pick = jnp.where(slots < own_count, visible[0], -1)
    bias = jnp.where(alive_all, 0.0, -1e30).astype(F32).reshape(1, ROWS)
    live = alive_all.astype(F32)[:, :, None]

    rows = gather_rows(pick[:, None], query_all[0], key_all[0], value_all[0])
    own, rows = projection(out_weight, x, core, y, rows)
    cot = x_exchange(split_columns(place, after(cotangent[0], rows)))
    own = [after(v, cot) for v in own]
    qkv = swap(after(rows, cot, *own))
    pieces = own + [other_core(v) for v in own]
    grad_part = grad_attn_part(place, cot, pieces)
    grad_attn = swap(lax.psum_scatter(grad_part, "x", scatter_dimension=0, tiled=False))

    attn, expo, inv = forward(bias, live, after(qkv, grad_part))
    attn = lax.all_gather(swap(attn), "x", axis=0, tiled=False).reshape(NX, 2, NS // 2, CAP, GROUP)

    head_grads = backward(live, qkv, grad_attn, expo, inv, 0, HEADS - 1)
    grads = backward(after(live, head_grads), qkv, grad_attn, expo, inv, HEADS - 1, 1)
    keep, send = weight_part(place, after(attn, grads), cot)
    head_grads = swap(head_grads)
    grads = swap(grads)
    first, second = cut_pieces(place, keep, other_core(after(send, head_grads)))
    token_grads = scatter_rows(pick[None, :], head_grads, grads)
    out = out_part(place, after(attn, *first, *second, *token_grads), pieces)
    first, second = ring(along_z, first).astype(BF16), ring(along_y, second).astype(BF16)
    first, second, out = lax.optimization_barrier((first, second, out))
    output = join_columns(place, x_exchange(out))
    grad_weight = second_phase(first, second, place).T
    grad_query, grad_key, grad_value = token_grads
    return (output[None], grad_query[None], grad_key[None], grad_value[None], grad_weight)


def solution(mesh):
    fine = Mesh(np.asarray(mesh.devices).reshape(2, NX, 2, 2, 4), AXES)
    dp = ("zl", "x", "c")
    return jax.shard_map(
        on_device,
        mesh=fine,
        in_specs=(
            P(dp, SEQ, None),
            P(dp, SEQ, None),
            P(dp, SEQ, None),
            P(SEQ, None),
            P(dp, SEQ, None),
            P(dp, SEQ),
            P(dp, None),
        ),
        out_specs=(
            P(dp, SEQ, None),
            P(dp, SEQ, None),
            P(dp, SEQ, None),
            P(dp, SEQ, None),
            P(SEQ, dp),
        ),
        check_vma=False,
    )
```

time: 359 us -> 313 us (0.87)
  blocking collectives: 106 us -> 28.1 us
  starting transfers between devices: 15.5 us -> 56.4 us
  waiting for transfers between devices: 96.2 us -> 88.6 us
  local copies, waits for them, and re-layouts: 9.58 us -> 13.5 us
  other arithmetic: 12 us -> 8.29 us
    all_to_all x3 -> x1, blocking collectives: 106 us -> 28.1 us  [swap(): return lax.all_to_all(value, SEQ, split_axis=0, concat_axis=0, tiled=True)]
    ppermute x2 -> x24, starting transfers between devices: 0.09 us -> 29.3 us  [the longest x12 16.8 us: along_y(): return lax.ppermute(value, 'y', [(p, (p + k) % 4) for p in range(4)])]
    all_to_all x3 -> x6, waiting for transfers between devices: 77.9 us -> 52.8 us  [the longest x4 49 us: swap(): return lax.all_to_all(value, SEQ, split_axis=0, concat_axis=0, tiled=True)]
    ppermute x2 -> x24, waiting for transfers between devices: 6.99 us -> 30.3 us  [the longest x12 16.3 us: along_y(): return lax.ppermute(value, 'y', [(p, (p + k) % 4) for p in range(4)])]
    all_to_all x3 -> x6, starting transfers between devices: 15.2 us -> 26.9 us  [the longest x4 19 us: swap(): return lax.all_to_all(value, SEQ, split_axis=0, concat_axis=0, tiled=True)]
    reduce_scatter x1, waiting for transfers between devices: 9.76 us -> 0.01 us  [on_device(): lax.psum_scatter(grad_part, 'x', scatter_dimension=0, tiled=False)]
    dynamic_update_slice x0 -> x8, local copies, waits for them, and re-layouts: none -> 5.48 us  [gather(): zero = lax.dynamic_update_slice_in_dim(zero, part[None], (y + k) % 4, 0)]
    pallas_call x5 -> x8, Pallas kernels: 66.6 us -> 71.6 us  [the longest x2 25.7 us: backward(): pl.pallas_call(backward_kernel, grid=(count, NQ), in_specs=[COLUMN, at(so...]
  transfers between devices with their start and end apart: 9 -> 32, of which waited for: 5 -> 14; matrix products, arithmetic and copies ran while one was open for 3% -> 5% of each run, Pallas kernels for 28% -> 32%
where the time goes in v2:
time: 313 us; the launch traced here: 311 us
  Pallas kernels  102 us (33%)
  waiting for transfers between devices  88.6 us (28%)
  starting transfers between devices  56.4 us (18%)
  blocking collectives  28.1 us (9%)
  between operations  14.5 us (5%)
  local copies, waits for them, and re-layouts  13.5 us (4%)
  other arithmetic  8.29 us (3%)
    all_to_all x4, waiting for transfers between devices, swap(): return lax.all_to_all(value, SEQ, split_axis=0, concat_axis=0, tiled=True)  49 us
    all_to_all x1, blocking collectives, swap(): return lax.all_to_all(value, SEQ, split_axis=0, concat_axis=0, tiled=True)  28.1 us
    pallas_call x2, Pallas kernels, backward(): pl.pallas_call(backward_kernel, grid=(count, NQ), in_specs=[COLUMN, at(so...  25.7 us
    all_to_all x4, starting transfers between devices, swap(): return lax.all_to_all(value, SEQ, split_axis=0, concat_axis=0, tiled=True)  19 us
    ppermute x12, starting transfers between devices, along_y(): return lax.ppermute(value, 'y', [(p, (p + k) % 4) for p in range(4)])  16.8 us
    ppermute x12, waiting for transfers between devices, along_y(): return lax.ppermute(value, 'y', [(p, (p + k) % 4) for p in range(4)])  16.3 us
    pallas_call x1, Pallas kernels, forward(): pl.pallas_call(forward_kernel, grid=(HEADS, NQ), in_specs=[pl.BlockSpec((...  14.9 us
    pallas_call x1, Pallas kernels, weight_part(): pl.pallas_call(weight_kernel, grid_spec=pltpu.PrefetchScalarGridSpec(num_...  12.1 us
  transfers between devices with their start and end apart: 32, of which 14 were waited for; matrix products, arithmetic and copies ran while one was open for 5% of the time, Pallas kernels for 32%

profile of v2, /device:TPU:0, one launch (start us, length us, event | category | flops | bytes accessed | tf_op | source)
XLA Modules:
  0.0 311.1 jit_solution(6088721900105945495)
XLA Ops:
  14.6 4.1 %collective-permute-start.3 = (bf16[192,640]{1,0:T(8,128)(2,1)S(1)}, bf16[192,640]{1,0:T(8,128)(2,1)S(1)}, u32[]{:S(2)}, u32[]{:S(2)}) collective-permute-start(bf16[192,640]{1,0:T(8,128)(2,1)S(1)} %dynamic-slice.1), channel_id=1, source_target_pairs={{0,68},{68,0},{64,4},{4,64},{1,69},{69,1},{65,5},{5,65},{2,70},{70... | collective-permute-start | bytes 737288 | tf_op jit(solution)/shard_map/ppermute | solution.py:384
  21.8 7.9 %shard_map.110 = bf16[8,3,160,384]{3,2,1,0:T(8,128)(2,1)} custom-call(s32[160,1]{1,0:T(8,128)} %fusion.5.pick_ref, bf16[256,3072]{1,0:T(8,128)(2,1)} %bitcast.70, bf16[256,3072]{1,0:T(8,128)(2,1)} %bitcast.71, bf16[256,3072]{1,0:T(8,128)(2,1)} %bitcast.72), custom_call_target="tpu_custom_call" | custom-call | flops 1 | bytes 1 | tf_op jit(solution)/shard_map/pallas_call | solution.py:49
  31.2 2.7 shard_map.111
  34.0 4.3 %all-to-all-start = ((bf16[4,2,160,640]{3,2,1,0:T(8,128)(2,1)}), bf16[4,2,160,640]{3,2,1,0:T(8,128)(2,1)S(1)}, u32[]{:S(2)}, u32[]{:S(2)}) async-start(bf16[4,2,160,640]{3,2,1,0:T(8,128)(2,1)} %shard_map.111), calls=%async_computation | async-start | bytes 3276800 | tf_op jit(solution)/shard_map/all_to_all | solution.py:235
  38.2 2.6 collective-permute-start.6
  43.4 10.2 %collective-permute-done.5 = bf16[2,192,640]{2,1,0:T(8,128)(2,1)} collective-permute-done((bf16[2,192,640]{2,1,0:T(8,128)(2,1)S(1)}, bf16[2,192,640]{2,1,0:T(8,128)(2,1)}, u32[]{:S(2)}, u32[]{:S(2)}) %collective-permute-start.5) | collective-permute-done | bytes 491552 | tf_op jit(solution)/shard_map/ppermute | solution.py:375
  55.5 4.7 %collective-permute-done.6 = bf16[2,192,640]{2,1,0:T(8,128)(2,1)S(1)} collective-permute-done((bf16[2,192,640]{2,1,0:T(8,128)(2,1)S(1)}, bf16[2,192,640]{2,1,0:T(8,128)(2,1)S(1)}, u32[]{:S(2)}, u32[]{:S(2)}) %collective-permute-start.6) | collective-permute-done | bytes 491552 | tf_op jit(solution)/shard_map/ppermute | solution.py:375
  66.1 4.5 %all-to-all-start.1 = ((bf16[8,3,160,384]{3,2,1,0:T(8,128)(2,1)}), bf16[8,3,160,384]{3,2,1,0:T(8,128)(2,1)}, u32[]{:S(2)}, u32[]{:S(2)}) async-start(bf16[8,3,160,384]{3,2,1,0:T(8,128)(2,1)} %shard_map.110), calls=%async_computation.1 | async-start | bytes 5898240 | tf_op jit(solution)/shard_map/all_to_all | solution.py:367
  70.6 11.2 %shard_map.112 = bf16[4,2,4,160,384]{4,3,2,1,0:T(8,128)(2,1)} custom-call(s32[5]{0:T(128)} %stack.32.place_ref, bf16[4,2,160,640]{3,2,1,0:T(8,128)(2,1)} %copy-done.1, bf16[4,192,640]{2,1,0:T(8,128)(2,1)} %copy-done.3, bf16[4,192,640]{2,1,0:T(8,128)(2,1)} %collective-permute-done.4.f0, bf16[2,4,192,640]{3,2,1,0:T(8,128)(2,1)} %bitcast.24.l0, ...), custom_call_target="tpu_custom_call" | custom-call | flops 199999995904 | bytes 1 | tf_op jit(solution)/shard_map/pallas_call | solution.py:268
  81.9 26.7 %all-to-all-done.1.q_ref.k_ref.v_ref = bf16[8,3,160,384]{3,2,1,0:T(8,128)(2,1)} async-done(((bf16[8,3,160,384]{3,2,1,0:T(8,128)(2,1)}), bf16[8,3,160,384]{3,2,1,0:T(8,128)(2,1)}, u32[]{:S(2)}, u32[]{:S(2)}) %all-to-all-start.1) | async-done | bytes 2949152 | tf_op jit(solution)/shard_map/all_to_all | solution.py:367
  108.6 14.9 %shard_map.113 = (bf16[8,160,384]{2,1,0:T(8,128)(2,1)}, bf16[3,1280,1280]{2,1,0:T(8,128)(2,1)}, f32[3,8,160,1]{3,2,1,0:T(8,128)}) custom-call(f32[1,1280]{1,0:T(1,128)} %select_n.165.bias_ref, f32[8,160,1]{2,1,0:T(8,128)} %fusion.live_ref, bf16[8,3,160,384]{3,2,1,0:T(8,128)(2,1)} %all-to-all-done.1.q_ref.k_ref.v_ref, ...), custom_call_target="tpu_custom_call" | custom-call | flops 199999995904 | bytes 1 | tf_op jit(solution)/shard_map/pallas_call | solution.py:118
  123.5 28.1 %all_to_all.35 = bf16[8,160,384]{2,1,0:T(8,128)(2,1)} all-to-all(bf16[8,160,384]{2,1,0:T(8,128)(2,1)} %get-tuple-element.46), channel_id=1, replica_groups=mesh['zl'=2,'x'=4,'c'=2,'zh'=2,'y'=4] {'zh','y'}, dimensions={0} | all-to-all | bytes 1966080 | tf_op jit(solution)/shard_map/all_to_all | solution.py:367
  151.6 3.6 %all-to-all-start.3 = ((bf16[8,160,384]{2,1,0:T(8,128)(2,1)}), bf16[8,160,384]{2,1,0:T(8,128)(2,1)S(1)}, u32[]{:S(2)}, u32[]{:S(2)}) async-start(bf16[8,160,384]{2,1,0:T(8,128)(2,1)} %bitcast.73), calls=%async_computation.4 | async-start | bytes 1966080 | tf_op jit(solution)/shard_map/all_to_all | solution.py:367
  156.0 13.7 %all-to-all-done.3.grad_ref = bf16[8,160,384]{2,1,0:T(8,128)(2,1)S(1)} async-done(((bf16[8,160,384]{2,1,0:T(8,128)(2,1)}), bf16[8,160,384]{2,1,0:T(8,128)(2,1)S(1)}, u32[]{:S(2)}, u32[]{:S(2)}) %all-to-all-start.3) | async-done | bytes 983072 | tf_op jit(solution)/shard_map/all_to_all | solution.py:367
  170.6 16.3 %shard_map.114 = bf16[8,3,160,256]{3,2,1,0:T(8,128)(2,1)} custom-call(f32[8,160,1]{2,1,0:T(8,128)} %fusion.live_ref, bf16[8,3,160,384]{3,2,1,0:T(8,128)(2,1)} %all-to-all-done.1.q_ref.k_ref.v_ref, bf16[8,3,160,384]{3,2,1,0:T(8,128)(2,1)} %all-to-all-done.1.q_ref.k_ref.v_ref, bf16[8,3,160,384]{3,2,1,0:T(8,128)(2,1)} %all-to-all-done.1.q_ref.k_ref.v_ref, ...), custom_call_target="tpu_custom_call" | custom-call | flops 199999995904 | bytes 1 | tf_op jit(solution)/shard_map/pallas_call | solution.py:172
  186.9 4.3 %all-to-all-start.4 = ((bf16[8,3,160,256]{3,2,1,0:T(8,128)(2,1)}), bf16[8,3,160,256]{3,2,1,0:T(8,128)(2,1)}, u32[]{:S(2)}, u32[]{:S(2)}) async-start(bf16[8,3,160,256]{3,2,1,0:T(8,128)(2,1)} %shard_map.114), calls=%async_computation.5 | async-start | bytes 3932160 | tf_op jit(solution)/shard_map/all_to_all | solution.py:367
  191.2 9.4 %shard_map.115 = bf16[8,3,160,128]{3,2,1,0:T(8,128)(2,1)} custom-call(f32[8,160,1]{2,1,0:T(8,128)} %fusion.live_ref, bf16[8,3,160,384]{3,2,1,0:T(8,128)(2,1)} %all-to-all-done.1.q_ref.k_ref.v_ref, bf16[8,3,160,384]{3,2,1,0:T(8,128)(2,1)} %all-to-all-done.1.q_ref.k_ref.v_ref, bf16[8,3,160,384]{3,2,1,0:T(8,128)(2,1)} %all-to-all-done.1.q_ref.k_ref.v_ref, ...), custom_call_target="tpu_custom_call" | custom-call | flops 199999995904 | bytes 1 | tf_op jit(solution)/shard_map/pallas_call | solution.py:172
  200.6 5.0 %all-gather.3.cloned.1.call-done = bf16[32,160,384]{2,1,0:T(8,128)(2,1)} async-done(((bf16[8,160,384]{2,1,0:T(8,128)(2,1)}), bf16[32,160,384]{2,1,0:T(8,128)(2,1)}) %all-gather.3.cloned.1.call-update) | async-done | bytes 3932176 | tf_op jit(solution)/shard_map/all_gather | solution.py:467
  205.6 12.1 %shard_map.116 = (bf16[2,2,2,4,160,384]{5,4,3,2,1,0:T(8,128)(2,1)}, bf16[2,2,2,4,160,384]{5,4,3,2,1,0:T(8,128)(2,1)}) custom-call(s32[5]{0:T(128)} %stack.32.place_ref, bf16[4,2,4,160,384]{4,3,2,1,0:T(8,128)(2,1)} %bitcast.65, bf16[4,2,160,640]{3,2,1,0:T(8,128)(2,1)} %copy-done.1), custom_call_target="tpu_custom_call" | custom-call | flops 1 | bytes 1 | tf_op jit(solution)/shard_map/pallas_call | solution.py:313
  218.0 6.7 %all-to-all-start.5 = ((bf16[8,3,160,128]{3,2,1,0:T(8,128)(2,1)}), bf16[8,3,160,128]{3,2,1,0:T(8,128)(2,1)S(1)}, u32[]{:S(2)}, u32[]{:S(2)}) async-start(bf16[8,3,160,128]{3,2,1,0:T(8,128)(2,1)} %shard_map.115), calls=%async_computation.6 | async-start | bytes 1966080 | tf_op jit(solution)/shard_map/all_to_all | solution.py:367
  225.1 6.0 %shard_map.117 = (bf16[4,160,384]{2,1,0:T(8,128)(2,1)}, bf16[4,160,384]{2,1,0:T(8,128)(2,1)}, bf16[4,160,384]{2,1,0:T(8,128)(2,1)}, bf16[4,160,384]{2,1,0:T(8,12...) custom-call(s32[5]{0:T(128)} %stack.32.place_ref, ...), custom_call_target="tpu_custom_call" | custom-call | flops 1 | bytes 1 | tf_op jit(solution)/shard_map/pallas_call | solution.py:421
  233.8 8.4 %all-to-all-done.5.rest_ref = bf16[8,3,160,128]{3,2,1,0:T(8,128)(2,1)S(1)} async-done(((bf16[8,3,160,128]{3,2,1,0:T(8,128)(2,1)}), bf16[8,3,160,128]{3,2,1,0:T(8,128)(2,1)S(1)}, u32[]{:S(2)}, u32[]{:S(2)}) %all-to-all-start.5) | async-done | bytes 983072 | tf_op jit(solution)/shard_map/all_to_all | solution.py:367
  243.1 7.1 %shard_map.118 = (bf16[256,3072]{1,0:T(8,128)(2,1)}, bf16[256,3072]{1,0:T(8,128)(2,1)}, bf16[256,3072]{1,0:T(8,128)(2,1)}) custom-call(s32[1,160]{1,0:T(1,128)} %compare_select_fusion.pick_ref, bf16[8,3,160,256]{3,2,1,0:T(8,128)(2,1)} %all-to-all-done.4.first_ref, bf16[8,3,160,128]{3,2,1,0:T(8,128)(2,1)} %copy-done.2), custom_call_target="tpu_custom_call" | custom-call | flops 1 | bytes 1 | tf_op jit(solution)/shard_map/pallas_call | solution.py:70
  253.5 2.6 collective-permute-start.13
  256.1 11.2 %shard_map.119 = bf16[4,2,160,640]{3,2,1,0:T(8,128)(2,1)} custom-call(s32[5]{0:T(128)} %stack.32.place_ref, bf16[4,2,4,160,384]{4,3,2,1,0:T(8,128)(2,1)} %bitcast.66, bf16[4,192,640]{2,1,0:T(8,128)(2,1)} %copy-done.3, bf16[4,192,640]{2,1,0:T(8,128)(2,1)} %collective-permute-done.4.f0, bf16[2,4,192,640]{3,2,1,0:T(8,128)(2,1)} %bitcast.24.l0, ...), custom_call_target="tpu_custom_call" | custom-call | flops 199999995904 | bytes 1 | tf_op jit(solution)/shard_map/pallas_call | solution.py:347
  268.9 7.9 %collective-permute-done.12 = bf16[4,160,384]{2,1,0:T(8,128)(2,1)} collective-permute-done((bf16[4,160,384]{2,1,0:T(8,128)(2,1)}, bf16[4,160,384]{2,1,0:T(8,128)(2,1)}, u32[]{:S(2)}, u32[]{:S(2)}) %collective-permute-start.12) | collective-permute-done | bytes 491552 | tf_op jit(solution)/shard_map/ppermute | solution.py:380
  278.4 3.6 %all-to-all-start.6 = ((bf16[4,2,160,640]{3,2,1,0:T(8,128)(2,1)}), bf16[4,2,160,640]{3,2,1,0:T(8,128)(2,1)S(1)}, u32[]{:S(2)}, u32[]{:S(2)}) async-start(bf16[4,2,160,640]{3,2,1,0:T(8,128)(2,1)} %shard_map.119), calls=%async_computation.7 | async-start | bytes 3276800 | tf_op jit(solution)/shard_map/all_to_all | solution.py:235
  282.3 3.2 %collective-permute-start.19 = (bf16[160,384]{1,0:T(8,128)(2,1)S(1)}, bf16[160,384]{1,0:T(8,128)(2,1)S(1)}, u32[]{:S(2)}, u32[]{:S(2)}) collective-permute-start(bf16[160,384]{1,0:T(8,128)(2,1)S(1)} %get-tuple-element.73), channel_id=1, source_target_pairs={{0,3},{1,0},{2,1},{3,2},{4,7},{5,4},{6,5},{7,6},{8,11},{9,8},{10,9... | collective-permute-start | bytes 368648 | tf_op jit(solution)/shard_map/ppermute | solution.py:375
  286.9 2.4 collective-permute-start.22
  292.3 3.4 %collective-permute-done.23 = bf16[160,384]{1,0:T(8,128)(2,1)S(1)} collective-permute-done((bf16[160,384]{1,0:T(8,128)(2,1)S(1)}, bf16[160,384]{1,0:T(8,128)(2,1)S(1)}, u32[]{:S(2)}, u32[]{:S(2)}) %collective-permute-start.23) | collective-permute-done | bytes 122912 | tf_op jit(solution)/shard_map/ppermute | solution.py:380
  296.5 3.8 %all-to-all-done.6.in_ref = bf16[4,2,160,640]{3,2,1,0:T(8,128)(2,1)S(1)} async-done(((bf16[4,2,160,640]{3,2,1,0:T(8,128)(2,1)}), bf16[4,2,160,640]{3,2,1,0:T(8,128)(2,1)S(1)}, u32[]{:S(2)}, u32[]{:S(2)}) %all-to-all-start.6) | async-done | bytes 1638432 | tf_op jit(solution)/shard_map/all_to_all | solution.py:235
  301.5 2.7 shard_map.120
  (96 shorter events, 41.5 us)
Async XLA Ops:
  8.3 21.3 %collective-permute-start = (bf16[192,640]{1,0:T(8,128)(2,1)S(1)}, bf16[192,640]{1,0:T(8,128)(2,1)S(1)}, u32[]{:S(2)}, u32[]{:S(2)}) collective-permute-start(bf16[192,640]{1,0:T(8,128)(2,1)S(1)} %get-tuple-element.70), channel_id=1, source_target_pairs={{0,1},{1,2},{2,3},{3,0},{4,5},{5,6},{6,7},{7,4},{8,9},{9,10},{10,1... | collective-permute-start | bytes 737288 | tf_op jit(solution)/shard_map/ppermute | solution.py:375
  10.0 19.7 %collective-permute-start.1 = (bf16[192,640]{1,0:T(8,128)(2,1)S(1)}, bf16[192,640]{1,0:T(8,128)(2,1)S(1)}, u32[]{:S(2)}, u32[]{:S(2)}) collective-permute-start(bf16[192,640]{1,0:T(8,128)(2,1)S(1)} %get-tuple-element.70), channel_id=1, source_target_pairs={{0,3},{1,0},{2,1},{3,2},{4,7},{5,4},{6,5},{7,6},{8,11},{9,8},{10,9... | collective-permute-start | bytes 737288 | tf_op jit(solution)/shard_map/ppermute | solution.py:375
  11.6 18.2 %collective-permute-start.2 = (bf16[192,640]{1,0:T(8,128)(2,1)S(1)}, bf16[192,640]{1,0:T(8,128)(2,1)S(1)}, u32[]{:S(2)}, u32[]{:S(2)}) collective-permute-start(bf16[192,640]{1,0:T(8,128)(2,1)S(1)} %get-tuple-element.70), channel_id=1, source_target_pairs={{0,2},{1,3},{2,0},{3,1},{4,6},{5,7},{6,4},{7,5},{8,10},{9,11},{10,... | collective-permute-start | bytes 737288 | tf_op jit(solution)/shard_map/ppermute | solution.py:375
  14.6 15.0 %collective-permute-start.3 = (bf16[192,640]{1,0:T(8,128)(2,1)S(1)}, bf16[192,640]{1,0:T(8,128)(2,1)S(1)}, u32[]{:S(2)}, u32[]{:S(2)}) collective-permute-start(bf16[192,640]{1,0:T(8,128)(2,1)S(1)} %dynamic-slice.1), channel_id=1, source_target_pairs={{0,68},{68,0},{64,4},{4,64},{1,69},{69,1},{65,5},{5,65},{2,70},{70... | collective-permute-start | bytes 737288 | tf_op jit(solution)/shard_map/ppermute | solution.py:384
  29.9 23.8 %collective-permute-start.5 = (bf16[2,192,640]{2,1,0:T(8,128)(2,1)S(1)}, bf16[2,192,640]{2,1,0:T(8,128)(2,1)}, u32[]{:S(2)}, u32[]{:S(2)}) collective-permute-start(bf16[2,192,640]{2,1,0:T(8,128)(2,1)S(1)} %pad_maximum_fusion), channel_id=1, source_target_pairs={{0,1},{1,2},{2,3},{3,0},{4,5},{5,6},{6,7},{7,4},{8,9},{9,10},{10,1... | collective-permute-start | bytes 1474568 | tf_op jit(solution)/shard_map/ppermute | solution.py:375
  34.0 27.9 %all-to-all-start = ((bf16[4,2,160,640]{3,2,1,0:T(8,128)(2,1)}), bf16[4,2,160,640]{3,2,1,0:T(8,128)(2,1)S(1)}, u32[]{:S(2)}, u32[]{:S(2)}) async-start(bf16[4,2,160,640]{3,2,1,0:T(8,128)(2,1)} %shard_map.111), calls=%async_computation | async-start | bytes 3276800 | tf_op jit(solution)/shard_map/all_to_all | solution.py:235
  38.2 21.9 %collective-permute-start.6 = (bf16[2,192,640]{2,1,0:T(8,128)(2,1)S(1)}, bf16[2,192,640]{2,1,0:T(8,128)(2,1)S(1)}, u32[]{:S(2)}, u32[]{:S(2)}) collective-permute-start(bf16[2,192,640]{2,1,0:T(8,128)(2,1)S(1)} %pad_maximum_fusion), channel_id=1, source_target_pairs={{0,3},{1,0},{2,1},{3,2},{4,7},{5,4},{6,5},{7,6},{8,11},{9,8},{10,9... | collective-permute-start | bytes 1474568 | tf_op jit(solution)/shard_map/ppermute | solution.py:375
  40.8 20.2 %collective-permute-start.7 = (bf16[2,192,640]{2,1,0:T(8,128)(2,1)S(1)}, bf16[2,192,640]{2,1,0:T(8,128)(2,1)S(1)}, u32[]{:S(2)}, u32[]{:S(2)}) collective-permute-start(bf16[2,192,640]{2,1,0:T(8,128)(2,1)S(1)} %pad_maximum_fusion), channel_id=1, source_target_pairs={{0,2},{1,3},{2,0},{3,1},{4,6},{5,7},{6,4},{7,5},{8,10},{9,11},{10,... | collective-permute-start | bytes 1474568 | tf_op jit(solution)/shard_map/ppermute | solution.py:375
  41.1 22.7 %collective-permute-start.4 = (bf16[4,192,640]{2,1,0:T(8,128)(2,1)S(1)}, bf16[4,192,640]{2,1,0:T(8,128)(2,1)}, u32[]{:S(2)}, u32[]{:S(2)}) collective-permute-start(bf16[4,192,640]{2,1,0:T(8,128)(2,1)S(1)} %bitcast_dynamic-update-slice_fusion.4.u0), channel_id=1, source_target_pairs={{0,68},{68,0},{64,4},{4,64},{1,69},{69,1},{65,5},{5,65},{2,70},{70... | collective-permute-start | bytes 2949128 | tf_op jit(solution)/shard_map/ppermute | solution.py:384
  61.9 8.7 %collective-permute-start.10 = (bf16[2,4,192,640]{3,2,1,0:T(8,128)(2,1)}, bf16[2,4,192,640]{3,2,1,0:T(8,128)(2,1)}, u32[]{:S(2)}, u32[]{:S(2)}) collective-permute-start(bf16[2,4,192,640]{3,2,1,0:T(8,128)(2,1)} %bitcast.24.l0), channel_id=1, source_target_pairs={{0,8},{8,0},{1,9},{9,1},{2,10},{10,2},{3,11},{11,3},{4,12},{12,4},... | collective-permute-start | bytes 5898248 | tf_op jit(solution)/shard_map/ppermute | solution.py:363
  63.9 6.7 %collective-permute-start.9 = (bf16[4,192,640]{2,1,0:T(8,128)(2,1)}, bf16[4,192,640]{2,1,0:T(8,128)(2,1)}, u32[]{:S(2)}, u32[]{:S(2)}) collective-permute-start(bf16[4,192,640]{2,1,0:T(8,128)(2,1)} %collective-permute-done.4.f0), channel_id=1, source_target_pairs={{0,8},{8,0},{1,9},{9,1},{2,10},{10,2},{3,11},{11,3},{4,12},{12,4},... | collective-permute-start | bytes 2949128 | tf_op jit(solution)/shard_map/ppermute | solution.py:363
  63.9 6.7 %collective-permute-start.8 = (bf16[4,192,640]{2,1,0:T(8,128)(2,1)S(1)}, bf16[4,192,640]{2,1,0:T(8,128)(2,1)}, u32[]{:S(2)}, u32[]{:S(2)}) collective-permute-start(bf16[4,192,640]{2,1,0:T(8,128)(2,1)S(1)} %bitcast_dynamic-update-slice_fusion.4.u0), channel_id=1, source_target_pairs={{0,8},{8,0},{1,9},{9,1},{2,10},{10,2},{3,11},{11,3},{4,12},{12,4},... | collective-permute-start | bytes 2949128 | tf_op jit(solution)/shard_map/ppermute | solution.py:363
  66.1 42.5 %all-to-all-start.1 = ((bf16[8,3,160,384]{3,2,1,0:T(8,128)(2,1)}), bf16[8,3,160,384]{3,2,1,0:T(8,128)(2,1)}, u32[]{:S(2)}, u32[]{:S(2)}) async-start(bf16[8,3,160,384]{3,2,1,0:T(8,128)(2,1)} %shard_map.110), calls=%async_computation.1 | async-start | bytes 5898240 | tf_op jit(solution)/shard_map/all_to_all | solution.py:367
  70.5 81.1 %reduce-scatter.2.cloned.1.call-start = ((), (), s32[]{:S(2)}) async-start(), calls=%async_computation.8 | async-start | bytes 4915200 | tf_op jit(solution)/shard_map/reduce_scatter | solution.py:464
  151.6 18.0 %all-to-all-start.3 = ((bf16[8,160,384]{2,1,0:T(8,128)(2,1)}), bf16[8,160,384]{2,1,0:T(8,128)(2,1)S(1)}, u32[]{:S(2)}, u32[]{:S(2)}) async-start(bf16[8,160,384]{2,1,0:T(8,128)(2,1)} %bitcast.73), calls=%async_computation.4 | async-start | bytes 1966080 | tf_op jit(solution)/shard_map/all_to_all | solution.py:367
  155.2 50.4 %all-gather.3.cloned.1.call-start = ((), (), s32[]{:S(2)}) async-start(), calls=%async_computation.9 | async-start | bytes 4915200 | tf_op jit(solution)/shard_map/all_gather | solution.py:467
  186.9 31.1 %all-to-all-start.4 = ((bf16[8,3,160,256]{3,2,1,0:T(8,128)(2,1)}), bf16[8,3,160,256]{3,2,1,0:T(8,128)(2,1)}, u32[]{:S(2)}, u32[]{:S(2)}) async-start(bf16[8,3,160,256]{3,2,1,0:T(8,128)(2,1)} %shard_map.114), calls=%async_computation.5 | async-start | bytes 3932160 | tf_op jit(solution)/shard_map/all_to_all | solution.py:367
  218.0 7.1 %collective-permute-start.11 = (bf16[2,2,2,4,160,384]{5,4,3,2,1,0:T(8,128)(2,1)}, bf16[2,2,2,4,160,384]{5,4,3,2,1,0:T(8,128)(2,1)}, u32[]{:S(2)}, u32[]{:S(2)}) collective-permute-start(bf16[2,2,2,4,160,384]{5,4,3,2,1,0:T(8,128)(2,1)} %get-tuple-element.53), channel_id=1, source_target_pairs={{0,8},{8,0},{1,9},{9,1},{2,10},{10,2},{3,11},{11,3},{4,12},{12,4},... | collective-permute-start | bytes 11796488 | tf_op jit(solution)/shard_map/ppermute | solution.py:363
  218.0 24.2 %all-to-all-start.5 = ((bf16[8,3,160,128]{3,2,1,0:T(8,128)(2,1)}), bf16[8,3,160,128]{3,2,1,0:T(8,128)(2,1)S(1)}, u32[]{:S(2)}, u32[]{:S(2)}) async-start(bf16[8,3,160,128]{3,2,1,0:T(8,128)(2,1)} %shard_map.115), calls=%async_computation.6 | async-start | bytes 1966080 | tf_op jit(solution)/shard_map/all_to_all | solution.py:367
  231.1 25.0 %collective-permute-start.15 = (bf16[2,2,160,384]{3,2,1,0:T(8,128)(2,1)}, bf16[2,2,160,384]{3,2,1,0:T(8,128)(2,1)S(1)}, u32[]{:S(2)}, u32[]{:S(2)}) collective-permute-start(bf16[2,2,160,384]{3,2,1,0:T(8,128)(2,1)} %get-tuple-element.59), channel_id=1, source_target_pairs={{0,1},{1,2},{2,3},{3,0},{4,5},{5,6},{6,7},{7,4},{8,9},{9,10},{10,1... | collective-permute-start | bytes 1474568 | tf_op jit(solution)/shard_map/ppermute | solution.py:375
  250.2 17.0 %collective-permute-start.16 = (bf16[2,2,160,384]{3,2,1,0:T(8,128)(2,1)}, bf16[2,2,160,384]{3,2,1,0:T(8,128)(2,1)}, u32[]{:S(2)}, u32[]{:S(2)}) collective-permute-start(bf16[2,2,160,384]{3,2,1,0:T(8,128)(2,1)} %get-tuple-element.60), channel_id=1, source_target_pairs={{0,3},{1,0},{2,1},{3,2},{4,7},{5,4},{6,5},{7,6},{8,11},{9,8},{10,9... | collective-permute-start | bytes 1474568 | tf_op jit(solution)/shard_map/ppermute | solution.py:375
  250.4 16.8 %collective-permute-start.17 = (bf16[2,2,160,384]{3,2,1,0:T(8,128)(2,1)}, bf16[2,2,160,384]{3,2,1,0:T(8,128)(2,1)}, u32[]{:S(2)}, u32[]{:S(2)}) collective-permute-start(bf16[2,2,160,384]{3,2,1,0:T(8,128)(2,1)} %get-tuple-element.61), channel_id=1, source_target_pairs={{0,2},{1,3},{2,0},{3,1},{4,6},{5,7},{6,4},{7,5},{8,10},{9,11},{10,... | collective-permute-start | bytes 1474568 | tf_op jit(solution)/shard_map/ppermute | solution.py:375
  252.8 24.0 %collective-permute-start.12 = (bf16[4,160,384]{2,1,0:T(8,128)(2,1)}, bf16[4,160,384]{2,1,0:T(8,128)(2,1)}, u32[]{:S(2)}, u32[]{:S(2)}) collective-permute-start(bf16[4,160,384]{2,1,0:T(8,128)(2,1)} %get-tuple-element.55), channel_id=1, source_target_pairs={{0,64},{64,4},{4,68},{68,0},{1,65},{65,5},{5,69},{69,1},{2,66},{66... | collective-permute-start | bytes 1474568 | tf_op jit(solution)/shard_map/ppermute | solution.py:380
  253.5 23.4 %collective-permute-start.13 = (bf16[4,160,384]{2,1,0:T(8,128)(2,1)}, bf16[4,160,384]{2,1,0:T(8,128)(2,1)}, u32[]{:S(2)}, u32[]{:S(2)}) collective-permute-start(bf16[4,160,384]{2,1,0:T(8,128)(2,1)} %get-tuple-element.56), channel_id=1, source_target_pairs={{0,68},{64,0},{4,64},{68,4},{1,69},{65,1},{5,65},{69,5},{2,70},{66... | collective-permute-start | bytes 1474568 | tf_op jit(solution)/shard_map/ppermute | solution.py:380
  256.0 20.8 %collective-permute-start.14 = (bf16[4,160,384]{2,1,0:T(8,128)(2,1)}, bf16[4,160,384]{2,1,0:T(8,128)(2,1)}, u32[]{:S(2)}, u32[]{:S(2)}) collective-permute-start(bf16[4,160,384]{2,1,0:T(8,128)(2,1)} %get-tuple-element.57), channel_id=1, source_target_pairs={{0,4},{64,68},{4,0},{68,64},{1,5},{65,69},{5,1},{69,65},{2,6},{66,... | collective-permute-start | bytes 1474568 | tf_op jit(solution)/shard_map/ppermute | solution.py:380
  278.4 21.9 %all-to-all-start.6 = ((bf16[4,2,160,640]{3,2,1,0:T(8,128)(2,1)}), bf16[4,2,160,640]{3,2,1,0:T(8,128)(2,1)S(1)}, u32[]{:S(2)}, u32[]{:S(2)}) async-start(bf16[4,2,160,640]{3,2,1,0:T(8,128)(2,1)} %shard_map.119), calls=%async_computation.7 | async-start | bytes 3276800 | tf_op jit(solution)/shard_map/all_to_all | solution.py:235
  282.2 7.0 %collective-permute-start.18 = (bf16[160,384]{1,0:T(8,128)(2,1)S(1)}, bf16[160,384]{1,0:T(8,128)(2,1)S(1)}, u32[]{:S(2)}, u32[]{:S(2)}) collective-permute-start(bf16[160,384]{1,0:T(8,128)(2,1)S(1)} %get-tuple-element.71), channel_id=1, source_target_pairs={{0,1},{1,2},{2,3},{3,0},{4,5},{5,6},{6,7},{7,4},{8,9},{9,10},{10,1... | collective-permute-start | bytes 368648 | tf_op jit(solution)/shard_map/ppermute | solution.py:375
  282.3 8.2 %collective-permute-start.19 = (bf16[160,384]{1,0:T(8,128)(2,1)S(1)}, bf16[160,384]{1,0:T(8,128)(2,1)S(1)}, u32[]{:S(2)}, u32[]{:S(2)}) collective-permute-start(bf16[160,384]{1,0:T(8,128)(2,1)S(1)} %get-tuple-element.73), channel_id=1, source_target_pairs={{0,3},{1,0},{2,1},{3,2},{4,7},{5,4},{6,5},{7,6},{8,11},{9,8},{10,9... | collective-permute-start | bytes 368648 | tf_op jit(solution)/shard_map/ppermute | solution.py:375
  285.5 6.4 %collective-permute-start.20 = (bf16[160,384]{1,0:T(8,128)(2,1)S(1)}, bf16[160,384]{1,0:T(8,128)(2,1)S(1)}, u32[]{:S(2)}, u32[]{:S(2)}) collective-permute-start(bf16[160,384]{1,0:T(8,128)(2,1)S(1)} %get-tuple-element.72), channel_id=1, source_target_pairs={{0,2},{1,3},{2,0},{3,1},{4,6},{5,7},{6,4},{7,5},{8,10},{9,11},{10,... | collective-permute-start | bytes 368648 | tf_op jit(solution)/shard_map/ppermute | solution.py:375
  286.0 6.3 %collective-permute-start.21 = (bf16[160,384]{1,0:T(8,128)(2,1)S(1)}, bf16[160,384]{1,0:T(8,128)(2,1)S(1)}, u32[]{:S(2)}, u32[]{:S(2)}) collective-permute-start(bf16[160,384]{1,0:T(8,128)(2,1)S(1)} %get-tuple-element.74), channel_id=1, source_target_pairs={{0,64},{64,4},{4,68},{68,0},{1,65},{65,5},{5,69},{69,1},{2,66},{66... | collective-permute-start | bytes 368648 | tf_op jit(solution)/shard_map/ppermute | solution.py:380
  286.9 5.4 %collective-permute-start.22 = (bf16[160,384]{1,0:T(8,128)(2,1)S(1)}, bf16[160,384]{1,0:T(8,128)(2,1)S(1)}, u32[]{:S(2)}, u32[]{:S(2)}) collective-permute-start(bf16[160,384]{1,0:T(8,128)(2,1)S(1)} %get-tuple-element.76), channel_id=1, source_target_pairs={{0,68},{64,0},{4,64},{68,4},{1,69},{65,1},{5,65},{69,5},{2,70},{66... | collective-permute-start | bytes 368648 | tf_op jit(solution)/shard_map/ppermute | solution.py:380
  289.3 6.4 %collective-permute-start.23 = (bf16[160,384]{1,0:T(8,128)(2,1)S(1)}, bf16[160,384]{1,0:T(8,128)(2,1)S(1)}, u32[]{:S(2)}, u32[]{:S(2)}) collective-permute-start(bf16[160,384]{1,0:T(8,128)(2,1)S(1)} %get-tuple-element.75), channel_id=1, source_target_pairs={{0,4},{64,68},{4,0},{68,64},{1,5},{65,69},{5,1},{69,65},{2,6},{66,... | collective-permute-start | bytes 368648 | tf_op jit(solution)/shard_map/ppermute | solution.py:380
  (11 other events, 104.2 us)
Sparse Core Ops, SparseCore 0:
  82.0 46.3 reduce-scatter.1
  157.7 47.8 all-gather.2

commit v3 on v2

--- a/solution.py
+++ b/solution.py
@@ -41,16 +41,18 @@
     token = lax.broadcasted_iota(jnp.int32, (CAP, TOK), 1)
     hot = (token == pick_ref[...]).astype(F32).astype(BF16)
     for i, ref in enumerate((q_ref, k_ref, v_ref)):
-        out_ref[0, i] = dot(hot, ref[...], ((1,), (0,))).astype(BF16)
+        rows = dot(hot, ref[...], ((1,), (0,))).astype(BF16)
+        for s in range(2):
+            out_ref[s, i] = rows[:, s * GROUP : (s + 1) * GROUP]
 
 
 def gather_rows(pick, q, k, v):
-    block = pl.BlockSpec((TOK, GROUP), lambda s: (0, s))
+    block = pl.BlockSpec((TOK, 2 * GROUP), lambda s: (0, s))
     return pl.pallas_call(
         gather_kernel,
-        grid=(NS,),
+        grid=(NS // 2,),
         in_specs=[pl.BlockSpec((CAP, 1), lambda s: (0, 0)), block, block, block],
-        out_specs=pl.BlockSpec((1, 3, CAP, GROUP), lambda s: (s, 0, 0, 0)),
+        out_specs=pl.BlockSpec((2, 3, CAP, GROUP), lambda s: (s, 0, 0, 0)),
         out_shape=jax.ShapeDtypeStruct((NS, 3, CAP, GROUP), BF16),
         compiler_params=params("arbitrary"),
         cost_estimate=BRIEF,
@@ -61,19 +63,19 @@
     token = lax.broadcasted_iota(jnp.int32, (TOK, CAP), 0)
     hot = (token == pick_ref[...]).astype(F32).astype(BF16)
     for i, ref in enumerate((q_ref, k_ref, v_ref)):
-        rows = jnp.concatenate([first_ref[0, i], rest_ref[0, i]], axis=1)
-        ref[...] = dot(hot, rows, ((1,), (0,))).astype(BF16)
+        rows = [part[s, i] for s in range(2) for part in (first_ref, rest_ref)]
+        ref[...] = dot(hot, jnp.concatenate(rows, axis=1), ((1,), (0,))).astype(BF16)
 
 
 def scatter_rows(pick, first, rest):
-    block = pl.BlockSpec((TOK, GROUP), lambda s: (0, s))
+    block = pl.BlockSpec((TOK, 2 * GROUP), lambda s: (0, s))
     return pl.pallas_call(
         scatter_kernel,
-        grid=(NS,),
+        grid=(NS // 2,),
         in_specs=[
             pl.BlockSpec((1, CAP), lambda s: (0, 0)),
-            pl.BlockSpec((1, 3, CAP, GROUP - HEAD_DIM), lambda s: (s, 0, 0, 0)),
-            pl.BlockSpec((1, 3, CAP, HEAD_DIM), lambda s: (s, 0, 0, 0)),
+            pl.BlockSpec((2, 3, CAP, GROUP - HEAD_DIM), lambda s: (s, 0, 0, 0)),
+            pl.BlockSpec((2, 3, CAP, HEAD_DIM), lambda s: (s, 0, 0, 0)),
         ],
         out_specs=[block] * 3,
         out_shape=[jax.ShapeDtypeStruct((TOK, NS * GROUP), BF16)] * 3,
@@ -355,7 +357,7 @@
         ),
         out_shape=jax.ShapeDtypeStruct((NX, 2, CAP, HALF), BF16),
         compiler_params=params("arbitrary"),
-        cost_estimate=LONG,
+        cost_estimate=BRIEF,
     )(place, attn, *pieces)
 
 
@@ -473,9 +475,10 @@
     grads = swap(grads)
     first, second = cut_pieces(place, keep, other_core(after(send, head_grads)))
     token_grads = scatter_rows(pick[None, :], head_grads, grads)
-    out = out_part(place, after(attn, *first, *second, *token_grads), pieces)
+    out = out_part(place, after(attn, *first, *second), pieces)
+    first = [*first[:2], after(first[2], out), first[3]]
     first, second = ring(along_z, first).astype(BF16), ring(along_y, second).astype(BF16)
-    first, second, out = lax.optimization_barrier((first, second, out))
+    out = after(out, second, *token_grads)
     output = join_columns(place, x_exchange(out))
     grad_weight = second_phase(first, second, place).T
     grad_query, grad_key, grad_value = token_grads

time: 313 us -> 297 us (0.949)
  waiting for transfers between devices: 88.6 us -> 76.9 us
  Pallas kernels: 102 us -> 96.9 us
  starting transfers between devices: 56.4 us -> 61.3 us
  local copies, waits for them, and re-layouts: 13.5 us -> 9.97 us
    ppermute x6, waiting for transfers between devices: 11.6 us -> 3.37 us  [along_z(): lax.ppermute(value, ('zl', 'zh'), [(index[z], index[(z + k) % 4]) for z i...]
    all_to_all x4, waiting for transfers between devices: 49 us -> 40.9 us  [swap(): return lax.all_to_all(value, SEQ, split_axis=0, concat_axis=0, tiled=True)]
    pallas_call x2, Pallas kernels: 15 us -> 10.3 us  [the longest x1 5.29 us: gather_rows(): pl.pallas_call(gather_kernel, grid=(NS // 2,), in_specs=[pl.BlockSpec((CA...]
    ppermute x6, starting transfers between devices: 7.83 us -> 11.6 us  [along_z(): lax.ppermute(value, ('zl', 'zh'), [(index[z], index[(z + k) % 4]) for z i...]
  transfers between devices with their start and end apart: 32 -> 32, of which waited for: 14 -> 14; matrix products, arithmetic and copies ran while one was open for 5% -> 4% of each run, Pallas kernels for 32% -> 32%
where the time goes in v3:
time: 297 us; the launch traced here: 296 us
  Pallas kernels  96.9 us (33%)
  waiting for transfers between devices  76.9 us (26%)
  starting transfers between devices  61.3 us (21%)
  blocking collectives  28.1 us (9%)
  between operations  14.6 us (5%)
  local copies, waits for them, and re-layouts  9.97 us (3%)
  other arithmetic  7.93 us (3%)
    all_to_all x4, waiting for transfers between devices, swap(): return lax.all_to_all(value, SEQ, split_axis=0, concat_axis=0, tiled=True)  40.9 us
    all_to_all x1, blocking collectives, swap(): return lax.all_to_all(value, SEQ, split_axis=0, concat_axis=0, tiled=True)  28.1 us
    pallas_call x2, Pallas kernels, backward(): pl.pallas_call(backward_kernel, grid=(count, NQ), in_specs=[COLUMN, at(so...  25.7 us
    all_to_all x4, starting transfers between devices, swap(): return lax.all_to_all(value, SEQ, split_axis=0, concat_axis=0, tiled=True)  18.8 us
    ppermute x12, waiting for transfers between devices, along_y(): return lax.ppermute(value, 'y', [(p, (p + k) % 4) for p in range(4)])  18.6 us
    ppermute x12, starting transfers between devices, along_y(): return lax.ppermute(value, 'y', [(p, (p + k) % 4) for p in range(4)])  17.3 us
    pallas_call x1, Pallas kernels, forward(): pl.pallas_call(forward_kernel, grid=(HEADS, NQ), in_specs=[pl.BlockSpec((...  14.9 us
    pallas_call x1, Pallas kernels, weight_part(): pl.pallas_call(weight_kernel, grid_spec=pltpu.PrefetchScalarGridSpec(num_...  12.1 us
  transfers between devices with their start and end apart: 32, of which 14 were waited for; matrix products, arithmetic and copies ran while one was open for 4% of the time, Pallas kernels for 32%

profile of v3, /device:TPU:0, one launch (start us, length us, event | category | flops | bytes accessed | tf_op | source)
XLA Modules:
  0.0 295.7 jit_solution(329889773826490440)
XLA Ops:
  11.6 2.1 collective-permute-start.2
  14.6 4.1 %collective-permute-start.3 = (bf16[192,640]{1,0:T(8,128)(2,1)S(1)}, bf16[192,640]{1,0:T(8,128)(2,1)S(1)}, u32[]{:S(2)}, u32[]{:S(2)}) collective-permute-start(bf16[192,640]{1,0:T(8,128)(2,1)S(1)} %dynamic-slice.1), channel_id=1, source_target_pairs={{0,68},{68,0},{64,4},{4,64},{1,69},{69,1},{65,5},{5,65},{2,70},{70... | collective-permute-start | bytes 737288 | tf_op jit(solution)/shard_map/ppermute | solution.py:386
  21.8 5.3 %shard_map.110 = bf16[8,3,160,384]{3,2,1,0:T(8,128)(2,1)} custom-call(s32[160,1]{1,0:T(8,128)} %fusion.5.pick_ref, bf16[256,3072]{1,0:T(8,128)(2,1)} %bitcast.73, bf16[256,3072]{1,0:T(8,128)(2,1)} %bitcast.74, bf16[256,3072]{1,0:T(8,128)(2,1)} %bitcast.75), custom_call_target="tpu_custom_call" | custom-call | flops 1 | bytes 1 | tf_op jit(solution)/shard_map/pallas_call | solution.py:51
  28.6 2.7 shard_map.111
  31.4 4.3 %all-to-all-start = ((bf16[4,2,160,640]{3,2,1,0:T(8,128)(2,1)}), bf16[4,2,160,640]{3,2,1,0:T(8,128)(2,1)}, u32[]{:S(2)}, u32[]{:S(2)}) async-start(bf16[4,2,160,640]{3,2,1,0:T(8,128)(2,1)} %shard_map.111), calls=%async_computation | async-start | bytes 3276800 | tf_op jit(solution)/shard_map/all_to_all | solution.py:237
  35.7 2.6 collective-permute-start.6
  41.6 16.4 %collective-permute-done.6 = bf16[2,192,640]{2,1,0:T(8,128)(2,1)S(1)} collective-permute-done((bf16[2,192,640]{2,1,0:T(8,128)(2,1)S(1)}, bf16[2,192,640]{2,1,0:T(8,128)(2,1)S(1)}, u32[]{:S(2)}, u32[]{:S(2)}) %collective-permute-start.6) | collective-permute-done | bytes 491552 | tf_op jit(solution)/shard_map/ppermute | solution.py:377
  58.3 3.4 %collective-permute-done.4.f0 = bf16[4,192,640]{2,1,0:T(8,128)(2,1)} collective-permute-done((bf16[4,192,640]{2,1,0:T(8,128)(2,1)S(1)}, bf16[4,192,640]{2,1,0:T(8,128)(2,1)}, u32[]{:S(2)}, u32[]{:S(2)}) %collective-permute-start.4) | collective-permute-done | bytes 983072 | tf_op jit(solution)/shard_map/ppermute | solution.py:386
  63.9 4.5 %all-to-all-start.1 = ((bf16[8,3,160,384]{3,2,1,0:T(8,128)(2,1)}), bf16[8,3,160,384]{3,2,1,0:T(8,128)(2,1)}, u32[]{:S(2)}, u32[]{:S(2)}) async-start(bf16[8,3,160,384]{3,2,1,0:T(8,128)(2,1)} %shard_map.110), calls=%async_computation.1 | async-start | bytes 5898240 | tf_op jit(solution)/shard_map/all_to_all | solution.py:369
  68.4 11.2 %shard_map.112 = bf16[4,2,4,160,384]{4,3,2,1,0:T(8,128)(2,1)} custom-call(s32[5]{0:T(128)} %stack.32.place_ref, bf16[4,2,160,640]{3,2,1,0:T(8,128)(2,1)} %all-to-all-done.in_ref.cot_ref, bf16[4,192,640]{2,1,0:T(8,128)(2,1)} %copy-done.3, bf16[4,192,640]{2,1,0:T(8,128)(2,1)} %collective-permute-done.4.f0, bf16[2,4,192,640]{3,2,1,0:T(8,128)(2,1)} %bitcast.68, ...), custom_call_target="tpu_custom_call" | custom-call | flops 199999995904 | bytes 1 | tf_op jit(solution)/shard_map/pallas_call | solution.py:270
  79.7 26.7 %all-to-all-done.1.q_ref.k_ref.v_ref = bf16[8,3,160,384]{3,2,1,0:T(8,128)(2,1)} async-done(((bf16[8,3,160,384]{3,2,1,0:T(8,128)(2,1)}), bf16[8,3,160,384]{3,2,1,0:T(8,128)(2,1)}, u32[]{:S(2)}, u32[]{:S(2)}) %all-to-all-start.1) | async-done | bytes 2949152 | tf_op jit(solution)/shard_map/all_to_all | solution.py:369
  106.4 14.9 %shard_map.113 = (bf16[8,160,384]{2,1,0:T(8,128)(2,1)}, bf16[3,1280,1280]{2,1,0:T(8,128)(2,1)}, f32[3,8,160,1]{3,2,1,0:T(8,128)}) custom-call(f32[1,1280]{1,0:T(1,128)} %select_n.165.bias_ref, f32[8,160,1]{2,1,0:T(8,128)} %fusion.live_ref, bf16[8,3,160,384]{3,2,1,0:T(8,128)(2,1)} %all-to-all-done.1.q_ref.k_ref.v_ref, ...), custom_call_target="tpu_custom_call" | custom-call | flops 199999995904 | bytes 1 | tf_op jit(solution)/shard_map/pallas_call | solution.py:120
  121.3 28.1 %all_to_all.35 = bf16[8,160,384]{2,1,0:T(8,128)(2,1)} all-to-all(bf16[8,160,384]{2,1,0:T(8,128)(2,1)} %get-tuple-element.45), channel_id=1, replica_groups=mesh['zl'=2,'x'=4,'c'=2,'zh'=2,'y'=4] {'zh','y'}, dimensions={0} | all-to-all | bytes 1966080 | tf_op jit(solution)/shard_map/all_to_all | solution.py:369
  149.5 3.6 %all-to-all-start.3 = ((bf16[8,160,384]{2,1,0:T(8,128)(2,1)}), bf16[8,160,384]{2,1,0:T(8,128)(2,1)S(1)}, u32[]{:S(2)}, u32[]{:S(2)}) async-start(bf16[8,160,384]{2,1,0:T(8,128)(2,1)} %bitcast.76), calls=%async_computation.4 | async-start | bytes 1966080 | tf_op jit(solution)/shard_map/all_to_all | solution.py:369
  153.8 13.7 %all-to-all-done.3.grad_ref = bf16[8,160,384]{2,1,0:T(8,128)(2,1)S(1)} async-done(((bf16[8,160,384]{2,1,0:T(8,128)(2,1)}), bf16[8,160,384]{2,1,0:T(8,128)(2,1)S(1)}, u32[]{:S(2)}, u32[]{:S(2)}) %all-to-all-start.3) | async-done | bytes 983072 | tf_op jit(solution)/shard_map/all_to_all | solution.py:369
  168.4 16.3 %shard_map.114 = bf16[8,3,160,256]{3,2,1,0:T(8,128)(2,1)} custom-call(f32[8,160,1]{2,1,0:T(8,128)} %fusion.live_ref, bf16[8,3,160,384]{3,2,1,0:T(8,128)(2,1)} %all-to-all-done.1.q_ref.k_ref.v_ref, bf16[8,3,160,384]{3,2,1,0:T(8,128)(2,1)} %all-to-all-done.1.q_ref.k_ref.v_ref, bf16[8,3,160,384]{3,2,1,0:T(8,128)(2,1)} %all-to-all-done.1.q_ref.k_ref.v_ref, ...), custom_call_target="tpu_custom_call" | custom-call | flops 199999995904 | bytes 1 | tf_op jit(solution)/shard_map/pallas_call | solution.py:174
  184.8 4.3 %all-to-all-start.4 = ((bf16[8,3,160,256]{3,2,1,0:T(8,128)(2,1)}), bf16[8,3,160,256]{3,2,1,0:T(8,128)(2,1)}, u32[]{:S(2)}, u32[]{:S(2)}) async-start(bf16[8,3,160,256]{3,2,1,0:T(8,128)(2,1)} %shard_map.114), calls=%async_computation.5 | async-start | bytes 3932160 | tf_op jit(solution)/shard_map/all_to_all | solution.py:369
  189.1 9.4 %shard_map.115 = bf16[8,3,160,128]{3,2,1,0:T(8,128)(2,1)} custom-call(f32[8,160,1]{2,1,0:T(8,128)} %fusion.live_ref, bf16[8,3,160,384]{3,2,1,0:T(8,128)(2,1)} %all-to-all-done.1.q_ref.k_ref.v_ref, bf16[8,3,160,384]{3,2,1,0:T(8,128)(2,1)} %all-to-all-done.1.q_ref.k_ref.v_ref, bf16[8,3,160,384]{3,2,1,0:T(8,128)(2,1)} %all-to-all-done.1.q_ref.k_ref.v_ref, ...), custom_call_target="tpu_custom_call" | custom-call | flops 199999995904 | bytes 1 | tf_op jit(solution)/shard_map/pallas_call | solution.py:174
  198.5 4.8 %all-gather.3.cloned.1.call-done = bf16[32,160,384]{2,1,0:T(8,128)(2,1)} async-done(((bf16[8,160,384]{2,1,0:T(8,128)(2,1)}), bf16[32,160,384]{2,1,0:T(8,128)(2,1)}) %all-gather.3.cloned.1.call-update) | async-done | bytes 3932176 | tf_op jit(solution)/shard_map/all_gather | solution.py:469
  203.4 12.1 %shard_map.116 = (bf16[2,2,2,4,160,384]{5,4,3,2,1,0:T(8,128)(2,1)}, bf16[2,2,2,4,160,384]{5,4,3,2,1,0:T(8,128)(2,1)}) custom-call(s32[5]{0:T(128)} %stack.32.place_ref, bf16[4,2,4,160,384]{4,3,2,1,0:T(8,128)(2,1)} %bitcast.65, bf16[4,2,160,640]{3,2,1,0:T(8,128)(2,1)} %all-to-all-done.in_ref.cot_ref), custom_call_target="tpu_custom_call" | custom-call | flops 1 | bytes 1 | tf_op jit(solution)/shard_map/pallas_call | solution.py:315
  215.9 6.4 %all-to-all-start.5 = ((bf16[8,3,160,128]{3,2,1,0:T(8,128)(2,1)}), bf16[8,3,160,128]{3,2,1,0:T(8,128)(2,1)S(1)}, u32[]{:S(2)}, u32[]{:S(2)}) async-start(bf16[8,3,160,128]{3,2,1,0:T(8,128)(2,1)} %shard_map.115), calls=%async_computation.6 | async-start | bytes 1966080 | tf_op jit(solution)/shard_map/all_to_all | solution.py:369
  223.0 5.9 %shard_map.117 = (bf16[4,160,384]{2,1,0:T(8,128)(2,1)}, bf16[4,160,384]{2,1,0:T(8,128)(2,1)}, bf16[4,160,384]{2,1,0:T(8,128)(2,1)}, bf16[4,160,384]{2,1,0:T(8,12...) custom-call(s32[5]{0:T(128)} %stack.32.place_ref, ...), custom_call_target="tpu_custom_call" | custom-call | flops 1 | bytes 1 | tf_op jit(solution)/shard_map/pallas_call | solution.py:423
  237.1 11.2 %shard_map.118 = bf16[4,2,160,640]{3,2,1,0:T(8,128)(2,1)} custom-call(s32[5]{0:T(128)} %stack.32.place_ref, bf16[4,2,4,160,384]{4,3,2,1,0:T(8,128)(2,1)} %bitcast.66, bf16[4,192,640]{2,1,0:T(8,128)(2,1)} %copy-done.3, bf16[4,192,640]{2,1,0:T(8,128)(2,1)} %collective-permute-done.4.f0, bf16[2,4,192,640]{3,2,1,0:T(8,128)(2,1)} %bitcast.69, ...), custom_call_target="tpu_custom_call" | custom-call | flops 1 | bytes 1 | tf_op jit(solution)/shard_map/pallas_call | solution.py:349
  248.3 2.5 collective-permute-start.17
  252.9 5.1 %shard_map.119 = (bf16[256,3072]{1,0:T(8,128)(2,1)}, bf16[256,3072]{1,0:T(8,128)(2,1)}, bf16[256,3072]{1,0:T(8,128)(2,1)}) custom-call(s32[1,160]{1,0:T(1,128)} %compare_select_fusion.pick_ref, bf16[8,3,160,256]{3,2,1,0:T(8,128)(2,1)} %all-to-all-done.4.first_ref, bf16[8,3,160,128]{3,2,1,0:T(8,128)(2,1)} %copy-done.2), custom_call_target="tpu_custom_call" | custom-call | flops 1 | bytes 1 | tf_op jit(solution)/shard_map/pallas_call | solution.py:72
  260.0 3.7 %all-to-all-start.6 = ((bf16[4,2,160,640]{3,2,1,0:T(8,128)(2,1)}), bf16[4,2,160,640]{3,2,1,0:T(8,128)(2,1)S(1)}, u32[]{:S(2)}, u32[]{:S(2)}) async-start(bf16[4,2,160,640]{3,2,1,0:T(8,128)(2,1)} %shard_map.118), calls=%async_computation.7 | async-start | bytes 3276800 | tf_op jit(solution)/shard_map/all_to_all | solution.py:237
  266.9 2.7 collective-permute-start.19
  270.5 2.6 collective-permute-start.22
  273.1 2.5 collective-permute-start.23
  276.8 2.6 collective-permute-done.23
  280.3 4.6 %all-to-all-done.6.in_ref = bf16[4,2,160,640]{3,2,1,0:T(8,128)(2,1)S(1)} async-done(((bf16[4,2,160,640]{3,2,1,0:T(8,128)(2,1)}), bf16[4,2,160,640]{3,2,1,0:T(8,128)(2,1)S(1)}, u32[]{:S(2)}, u32[]{:S(2)}) %all-to-all-start.6) | async-done | bytes 1638432 | tf_op jit(solution)/shard_map/all_to_all | solution.py:237
  286.1 2.7 shard_map.120
  (96 shorter events, 37.8 us)
Async XLA Ops:
  8.3 18.8 %collective-permute-start = (bf16[192,640]{1,0:T(8,128)(2,1)S(1)}, bf16[192,640]{1,0:T(8,128)(2,1)S(1)}, u32[]{:S(2)}, u32[]{:S(2)}) collective-permute-start(bf16[192,640]{1,0:T(8,128)(2,1)S(1)} %get-tuple-element.68), channel_id=1, source_target_pairs={{0,1},{1,2},{2,3},{3,0},{4,5},{5,6},{6,7},{7,4},{8,9},{9,10},{10,1... | collective-permute-start | bytes 737288 | tf_op jit(solution)/shard_map/ppermute | solution.py:377
  10.0 17.1 %collective-permute-start.1 = (bf16[192,640]{1,0:T(8,128)(2,1)S(1)}, bf16[192,640]{1,0:T(8,128)(2,1)S(1)}, u32[]{:S(2)}, u32[]{:S(2)}) collective-permute-start(bf16[192,640]{1,0:T(8,128)(2,1)S(1)} %get-tuple-element.68), channel_id=1, source_target_pairs={{0,3},{1,0},{2,1},{3,2},{4,7},{5,4},{6,5},{7,6},{8,11},{9,8},{10,9... | collective-permute-start | bytes 737288 | tf_op jit(solution)/shard_map/ppermute | solution.py:377
  11.6 15.6 %collective-permute-start.2 = (bf16[192,640]{1,0:T(8,128)(2,1)S(1)}, bf16[192,640]{1,0:T(8,128)(2,1)S(1)}, u32[]{:S(2)}, u32[]{:S(2)}) collective-permute-start(bf16[192,640]{1,0:T(8,128)(2,1)S(1)} %get-tuple-element.68), channel_id=1, source_target_pairs={{0,2},{1,3},{2,0},{3,1},{4,6},{5,7},{6,4},{7,5},{8,10},{9,11},{10,... | collective-permute-start | bytes 737288 | tf_op jit(solution)/shard_map/ppermute | solution.py:377
  14.6 12.5 %collective-permute-start.3 = (bf16[192,640]{1,0:T(8,128)(2,1)S(1)}, bf16[192,640]{1,0:T(8,128)(2,1)S(1)}, u32[]{:S(2)}, u32[]{:S(2)}) collective-permute-start(bf16[192,640]{1,0:T(8,128)(2,1)S(1)} %dynamic-slice.1), channel_id=1, source_target_pairs={{0,68},{68,0},{64,4},{4,64},{1,69},{69,1},{65,5},{5,65},{2,70},{70... | collective-permute-start | bytes 737288 | tf_op jit(solution)/shard_map/ppermute | solution.py:386
  27.3 13.2 %collective-permute-start.5 = (bf16[2,192,640]{2,1,0:T(8,128)(2,1)S(1)}, bf16[2,192,640]{2,1,0:T(8,128)(2,1)}, u32[]{:S(2)}, u32[]{:S(2)}) collective-permute-start(bf16[2,192,640]{2,1,0:T(8,128)(2,1)S(1)} %pad_maximum_fusion), channel_id=1, source_target_pairs={{0,1},{1,2},{2,3},{3,0},{4,5},{5,6},{6,7},{7,4},{8,9},{9,10},{10,1... | collective-permute-start | bytes 1474568 | tf_op jit(solution)/shard_map/ppermute | solution.py:377
  31.4 26.8 %all-to-all-start = ((bf16[4,2,160,640]{3,2,1,0:T(8,128)(2,1)}), bf16[4,2,160,640]{3,2,1,0:T(8,128)(2,1)}, u32[]{:S(2)}, u32[]{:S(2)}) async-start(bf16[4,2,160,640]{3,2,1,0:T(8,128)(2,1)} %shard_map.111), calls=%async_computation | async-start | bytes 3276800 | tf_op jit(solution)/shard_map/all_to_all | solution.py:237
  35.7 22.3 %collective-permute-start.6 = (bf16[2,192,640]{2,1,0:T(8,128)(2,1)S(1)}, bf16[2,192,640]{2,1,0:T(8,128)(2,1)S(1)}, u32[]{:S(2)}, u32[]{:S(2)}) collective-permute-start(bf16[2,192,640]{2,1,0:T(8,128)(2,1)S(1)} %pad_maximum_fusion), channel_id=1, source_target_pairs={{0,3},{1,0},{2,1},{3,2},{4,7},{5,4},{6,5},{7,6},{8,11},{9,8},{10,9... | collective-permute-start | bytes 1474568 | tf_op jit(solution)/shard_map/ppermute | solution.py:377
  38.4 19.7 %collective-permute-start.7 = (bf16[2,192,640]{2,1,0:T(8,128)(2,1)S(1)}, bf16[2,192,640]{2,1,0:T(8,128)(2,1)S(1)}, u32[]{:S(2)}, u32[]{:S(2)}) collective-permute-start(bf16[2,192,640]{2,1,0:T(8,128)(2,1)S(1)} %pad_maximum_fusion), channel_id=1, source_target_pairs={{0,2},{1,3},{2,0},{3,1},{4,6},{5,7},{6,4},{7,5},{8,10},{9,11},{10,... | collective-permute-start | bytes 1474568 | tf_op jit(solution)/shard_map/ppermute | solution.py:377
  38.7 23.0 %collective-permute-start.4 = (bf16[4,192,640]{2,1,0:T(8,128)(2,1)S(1)}, bf16[4,192,640]{2,1,0:T(8,128)(2,1)}, u32[]{:S(2)}, u32[]{:S(2)}) collective-permute-start(bf16[4,192,640]{2,1,0:T(8,128)(2,1)S(1)} %bitcast_dynamic-update-slice_fusion.4.u0), channel_id=1, source_target_pairs={{0,68},{68,0},{64,4},{4,64},{1,69},{69,1},{65,5},{5,65},{2,70},{70... | collective-permute-start | bytes 2949128 | tf_op jit(solution)/shard_map/ppermute | solution.py:386
  58.2 10.3 %collective-permute-start.10 = (bf16[2,4,192,640]{3,2,1,0:T(8,128)(2,1)S(1)}, bf16[2,4,192,640]{3,2,1,0:T(8,128)(2,1)}, u32[]{:S(2)}, u32[]{:S(2)}) collective-permute-start(bf16[2,4,192,640]{3,2,1,0:T(8,128)(2,1)S(1)} %bitcast.67), channel_id=1, source_target_pairs={{0,8},{8,0},{1,9},{9,1},{2,10},{10,2},{3,11},{11,3},{4,12},{12,4},... | collective-permute-start | bytes 5898248 | tf_op jit(solution)/shard_map/ppermute | solution.py:365
  61.7 6.7 %collective-permute-start.9 = (bf16[4,192,640]{2,1,0:T(8,128)(2,1)}, bf16[4,192,640]{2,1,0:T(8,128)(2,1)}, u32[]{:S(2)}, u32[]{:S(2)}) collective-permute-start(bf16[4,192,640]{2,1,0:T(8,128)(2,1)} %collective-permute-done.4.f0), channel_id=1, source_target_pairs={{0,8},{8,0},{1,9},{9,1},{2,10},{10,2},{3,11},{11,3},{4,12},{12,4},... | collective-permute-start | bytes 2949128 | tf_op jit(solution)/shard_map/ppermute | solution.py:365
  61.7 6.7 %collective-permute-start.8 = (bf16[4,192,640]{2,1,0:T(8,128)(2,1)S(1)}, bf16[4,192,640]{2,1,0:T(8,128)(2,1)}, u32[]{:S(2)}, u32[]{:S(2)}) collective-permute-start(bf16[4,192,640]{2,1,0:T(8,128)(2,1)S(1)} %bitcast_dynamic-update-slice_fusion.4.u0), channel_id=1, source_target_pairs={{0,8},{8,0},{1,9},{9,1},{2,10},{10,2},{3,11},{11,3},{4,12},{12,4},... | collective-permute-start | bytes 2949128 | tf_op jit(solution)/shard_map/ppermute | solution.py:365
  63.9 42.5 %all-to-all-start.1 = ((bf16[8,3,160,384]{3,2,1,0:T(8,128)(2,1)}), bf16[8,3,160,384]{3,2,1,0:T(8,128)(2,1)}, u32[]{:S(2)}, u32[]{:S(2)}) async-start(bf16[8,3,160,384]{3,2,1,0:T(8,128)(2,1)} %shard_map.110), calls=%async_computation.1 | async-start | bytes 5898240 | tf_op jit(solution)/shard_map/all_to_all | solution.py:369
  68.4 81.1 %reduce-scatter.2.cloned.1.call-start = ((), (), s32[]{:S(2)}) async-start(), calls=%async_computation.8 | async-start | bytes 4915200 | tf_op jit(solution)/shard_map/reduce_scatter | solution.py:466
  149.5 18.0 %all-to-all-start.3 = ((bf16[8,160,384]{2,1,0:T(8,128)(2,1)}), bf16[8,160,384]{2,1,0:T(8,128)(2,1)S(1)}, u32[]{:S(2)}, u32[]{:S(2)}) async-start(bf16[8,160,384]{2,1,0:T(8,128)(2,1)} %bitcast.76), calls=%async_computation.4 | async-start | bytes 1966080 | tf_op jit(solution)/shard_map/all_to_all | solution.py:369
  153.0 50.3 %all-gather.3.cloned.1.call-start = ((), (), s32[]{:S(2)}) async-start(), calls=%async_computation.9 | async-start | bytes 4915200 | tf_op jit(solution)/shard_map/all_gather | solution.py:469
  184.8 31.1 %all-to-all-start.4 = ((bf16[8,3,160,256]{3,2,1,0:T(8,128)(2,1)}), bf16[8,3,160,256]{3,2,1,0:T(8,128)(2,1)}, u32[]{:S(2)}, u32[]{:S(2)}) async-start(bf16[8,3,160,256]{3,2,1,0:T(8,128)(2,1)} %shard_map.114), calls=%async_computation.5 | async-start | bytes 3932160 | tf_op jit(solution)/shard_map/all_to_all | solution.py:369
  215.9 7.1 %collective-permute-start.11 = (bf16[2,2,2,4,160,384]{5,4,3,2,1,0:T(8,128)(2,1)}, bf16[2,2,2,4,160,384]{5,4,3,2,1,0:T(8,128)(2,1)}, u32[]{:S(2)}, u32[]{:S(2)}) collective-permute-start(bf16[2,2,2,4,160,384]{5,4,3,2,1,0:T(8,128)(2,1)} %get-tuple-element.52), channel_id=1, source_target_pairs={{0,8},{8,0},{1,9},{9,1},{2,10},{10,2},{3,11},{11,3},{4,12},{12,4},... | collective-permute-start | bytes 11796488 | tf_op jit(solution)/shard_map/ppermute | solution.py:365
  215.9 36.1 %all-to-all-start.5 = ((bf16[8,3,160,128]{3,2,1,0:T(8,128)(2,1)}), bf16[8,3,160,128]{3,2,1,0:T(8,128)(2,1)S(1)}, u32[]{:S(2)}, u32[]{:S(2)}) async-start(bf16[8,3,160,128]{3,2,1,0:T(8,128)(2,1)} %shard_map.115), calls=%async_computation.6 | async-start | bytes 1966080 | tf_op jit(solution)/shard_map/all_to_all | solution.py:369
  229.0 19.3 %collective-permute-start.12 = (bf16[2,2,160,384]{3,2,1,0:T(8,128)(2,1)}, bf16[2,2,160,384]{3,2,1,0:T(8,128)(2,1)S(1)}, u32[]{:S(2)}, u32[]{:S(2)}) collective-permute-start(bf16[2,2,160,384]{3,2,1,0:T(8,128)(2,1)} %get-tuple-element.58), channel_id=1, source_target_pairs={{0,1},{1,2},{2,3},{3,0},{4,5},{5,6},{6,7},{7,4},{8,9},{9,10},{10,1... | collective-permute-start | bytes 1474568 | tf_op jit(solution)/shard_map/ppermute | solution.py:377
  230.3 27.7 %collective-permute-start.13 = (bf16[2,2,160,384]{3,2,1,0:T(8,128)(2,1)}, bf16[2,2,160,384]{3,2,1,0:T(8,128)(2,1)S(1)}, u32[]{:S(2)}, u32[]{:S(2)}) collective-permute-start(bf16[2,2,160,384]{3,2,1,0:T(8,128)(2,1)} %get-tuple-element.60), channel_id=1, source_target_pairs={{0,3},{1,0},{2,1},{3,2},{4,7},{5,4},{6,5},{7,6},{8,11},{9,8},{10,9... | collective-permute-start | bytes 1474568 | tf_op jit(solution)/shard_map/ppermute | solution.py:377
  232.2 26.5 %collective-permute-start.14 = (bf16[2,2,160,384]{3,2,1,0:T(8,128)(2,1)}, bf16[2,2,160,384]{3,2,1,0:T(8,128)(2,1)}, u32[]{:S(2)}, u32[]{:S(2)}) collective-permute-start(bf16[2,2,160,384]{3,2,1,0:T(8,128)(2,1)} %get-tuple-element.59), channel_id=1, source_target_pairs={{0,2},{1,3},{2,0},{3,1},{4,6},{5,7},{6,4},{7,5},{8,10},{9,11},{10,... | collective-permute-start | bytes 1474568 | tf_op jit(solution)/shard_map/ppermute | solution.py:377
  233.8 30.0 %collective-permute-start.15 = (bf16[4,160,384]{2,1,0:T(8,128)(2,1)}, bf16[4,160,384]{2,1,0:T(8,128)(2,1)}, u32[]{:S(2)}, u32[]{:S(2)}) collective-permute-start(bf16[4,160,384]{2,1,0:T(8,128)(2,1)} %get-tuple-element.54), channel_id=1, source_target_pairs={{0,64},{64,4},{4,68},{68,0},{1,65},{65,5},{5,69},{69,1},{2,66},{66... | collective-permute-start | bytes 1474568 | tf_op jit(solution)/shard_map/ppermute | solution.py:382
  235.1 29.6 %collective-permute-start.16 = (bf16[4,160,384]{2,1,0:T(8,128)(2,1)}, bf16[4,160,384]{2,1,0:T(8,128)(2,1)}, u32[]{:S(2)}, u32[]{:S(2)}) collective-permute-start(bf16[4,160,384]{2,1,0:T(8,128)(2,1)} %get-tuple-element.56), channel_id=1, source_target_pairs={{0,68},{64,0},{4,64},{68,4},{1,69},{65,1},{5,65},{69,5},{2,70},{66... | collective-permute-start | bytes 1474568 | tf_op jit(solution)/shard_map/ppermute | solution.py:382
  248.3 15.6 %collective-permute-start.17 = (bf16[4,160,384]{2,1,0:T(8,128)(2,1)}, bf16[4,160,384]{2,1,0:T(8,128)(2,1)S(1)}, u32[]{:S(2)}, u32[]{:S(2)}) collective-permute-start(bf16[4,160,384]{2,1,0:T(8,128)(2,1)} %get-tuple-element.66), channel_id=1, source_target_pairs={{0,4},{64,68},{4,0},{68,64},{1,5},{65,69},{5,1},{69,65},{2,6},{66,... | collective-permute-start | bytes 1474568 | tf_op jit(solution)/shard_map/ppermute | solution.py:382
  260.0 24.9 %all-to-all-start.6 = ((bf16[4,2,160,640]{3,2,1,0:T(8,128)(2,1)}), bf16[4,2,160,640]{3,2,1,0:T(8,128)(2,1)S(1)}, u32[]{:S(2)}, u32[]{:S(2)}) async-start(bf16[4,2,160,640]{3,2,1,0:T(8,128)(2,1)} %shard_map.118), calls=%async_computation.7 | async-start | bytes 3276800 | tf_op jit(solution)/shard_map/all_to_all | solution.py:237
  266.3 6.7 %collective-permute-start.18 = (bf16[160,384]{1,0:T(8,128)(2,1)S(1)}, bf16[160,384]{1,0:T(8,128)(2,1)S(1)}, u32[]{:S(2)}, u32[]{:S(2)}) collective-permute-start(bf16[160,384]{1,0:T(8,128)(2,1)S(1)} %get-tuple-element.69), channel_id=1, source_target_pairs={{0,1},{1,2},{2,3},{3,0},{4,5},{5,6},{6,7},{7,4},{8,9},{9,10},{10,1... | collective-permute-start | bytes 368648 | tf_op jit(solution)/shard_map/ppermute | solution.py:377
  266.9 8.7 %collective-permute-start.19 = (bf16[160,384]{1,0:T(8,128)(2,1)S(1)}, bf16[160,384]{1,0:T(8,128)(2,1)S(1)}, u32[]{:S(2)}, u32[]{:S(2)}) collective-permute-start(bf16[160,384]{1,0:T(8,128)(2,1)S(1)} %get-tuple-element.71), channel_id=1, source_target_pairs={{0,3},{1,0},{2,1},{3,2},{4,7},{5,4},{6,5},{7,6},{8,11},{9,8},{10,9... | collective-permute-start | bytes 368648 | tf_op jit(solution)/shard_map/ppermute | solution.py:377
  269.6 6.4 %collective-permute-start.20 = (bf16[160,384]{1,0:T(8,128)(2,1)S(1)}, bf16[160,384]{1,0:T(8,128)(2,1)S(1)}, u32[]{:S(2)}, u32[]{:S(2)}) collective-permute-start(bf16[160,384]{1,0:T(8,128)(2,1)S(1)} %get-tuple-element.70), channel_id=1, source_target_pairs={{0,2},{1,3},{2,0},{3,1},{4,6},{5,7},{6,4},{7,5},{8,10},{9,11},{10,... | collective-permute-start | bytes 368648 | tf_op jit(solution)/shard_map/ppermute | solution.py:377
  269.8 6.7 %collective-permute-start.21 = (bf16[160,384]{1,0:T(8,128)(2,1)S(1)}, bf16[160,384]{1,0:T(8,128)(2,1)S(1)}, u32[]{:S(2)}, u32[]{:S(2)}) collective-permute-start(bf16[160,384]{1,0:T(8,128)(2,1)S(1)} %get-tuple-element.72), channel_id=1, source_target_pairs={{0,64},{64,4},{4,68},{68,0},{1,65},{65,5},{5,69},{69,1},{2,66},{66... | collective-permute-start | bytes 368648 | tf_op jit(solution)/shard_map/ppermute | solution.py:382
  270.5 6.3 %collective-permute-start.22 = (bf16[160,384]{1,0:T(8,128)(2,1)S(1)}, bf16[160,384]{1,0:T(8,128)(2,1)S(1)}, u32[]{:S(2)}, u32[]{:S(2)}) collective-permute-start(bf16[160,384]{1,0:T(8,128)(2,1)S(1)} %get-tuple-element.74), channel_id=1, source_target_pairs={{0,68},{64,0},{4,64},{68,4},{1,69},{65,1},{5,65},{69,5},{2,70},{66... | collective-permute-start | bytes 368648 | tf_op jit(solution)/shard_map/ppermute | solution.py:382
  273.1 6.4 %collective-permute-start.23 = (bf16[160,384]{1,0:T(8,128)(2,1)S(1)}, bf16[160,384]{1,0:T(8,128)(2,1)S(1)}, u32[]{:S(2)}, u32[]{:S(2)}) collective-permute-start(bf16[160,384]{1,0:T(8,128)(2,1)S(1)} %get-tuple-element.73), channel_id=1, source_target_pairs={{0,4},{64,68},{4,0},{68,64},{1,5},{65,69},{5,1},{69,65},{2,6},{66,... | collective-permute-start | bytes 368648 | tf_op jit(solution)/shard_map/ppermute | solution.py:382
  (11 other events, 96.2 us)
Sparse Core Ops, SparseCore 0:
  79.8 46.5 reduce-scatter.1
  155.6 47.7 all-gather.2

commit v4 on v3

--- a/solution.py
+++ b/solution.py
@@ -251,12 +251,22 @@
     return jnp.concatenate([up[0], low[0, 0], far[0], low[1, 0]], axis=0)
 
 
-def grad_attn_kernel(place_ref, in_ref, u0, f0, l0, u1, f1, l1, out_ref, cot_ref):
+PIECE = HALF // 4
+TURNED = (2, 2, 2 * PIECE, XROWS)
+
+
+def grad_attn_kernel(place_ref, in_ref, u0, f0, l0, u1, f1, l1, out_ref, turn_ref, cot_ref):
+    core = place_ref[1]
+
     @pl.when(pl.program_id(0) == 0)
     def _():
         for j in range(NX):
             for h in range(2):
                 cot_ref[h, j * CAP : (j + 1) * CAP] = in_ref[j, h]
+                turned = in_ref[j, h].T
+                for c in range(2):
+                    part = turned[2 * c * PIECE : 2 * (c + 1) * PIECE]
+                    turn_ref[c ^ core, h ^ core, :, j * CAP : (j + 1) * CAP] = part
 
     total = dot(cot_ref[0], weight_rows(u0, f0, l0), ((1,), (1,)))
     total = (total + dot(cot_ref[1], weight_rows(u1, f1, l1), ((1,), (1,)))).astype(BF16)
@@ -267,40 +277,30 @@
 
 
 def grad_attn_part(place, cot, pieces):
-    return pl.pallas_call(
+    part, turned = pl.pallas_call(
         grad_attn_kernel,
         grid_spec=pltpu.PrefetchScalarGridSpec(
             num_scalar_prefetch=1,
             grid=(NS // 2,),
             in_specs=[whole_block((NX, 2, CAP, HALF))] + [UPPER, UPPER, LOWER] * 2,
-            out_specs=PAIR,
+            out_specs=[PAIR, whole_block(TURNED)],
             scratch_shapes=[pltpu.VMEM((2, XROWS, HALF), BF16)],
         ),
-        out_shape=jax.ShapeDtypeStruct((NX, 2, NS // 2, CAP, GROUP), BF16),
+        out_shape=[
+            jax.ShapeDtypeStruct((NX, 2, NS // 2, CAP, GROUP), BF16),
+            jax.ShapeDtypeStruct(TURNED, BF16),
+        ],
         compiler_params=params("arbitrary"),
         cost_estimate=LONG,
-    )(place, cot, *pieces).reshape(NX, NS, CAP, GROUP)
+    )(place, cot, *pieces)
+    return part.reshape(NX, NS, CAP, GROUP), turned
 
 
 def ring_rows(ref, i):
     return ref[:, i, 0].reshape(XROWS, GROUP)
 
 
-PIECE = HALF // 4
-
-
-def weight_kernel(place_ref, attn_ref, cot_ref, keep_ref, send_ref, turn_ref):
-    core = place_ref[1]
-
-    @pl.when(pl.program_id(0) == 0)
-    def _():
-        for h in range(2):
-            for j in range(NX):
-                turned = cot_ref[j, h].T
-                for c in range(2):
-                    part = turned[2 * c * PIECE : 2 * (c + 1) * PIECE]
-                    turn_ref[c ^ core, h ^ core, :, j * CAP : (j + 1) * CAP] = part
-
+def weight_kernel(attn_ref, turn_ref, keep_ref, send_ref):
     rows = jnp.concatenate([ring_rows(attn_ref, i) for i in range(2)], axis=1)
     for other, ref in enumerate((keep_ref, send_ref)):
         for zl in range(2):
@@ -310,21 +310,20 @@
                     ref[p, zl, i, 0] = total[p * PIECE : (p + 1) * PIECE, i * GROUP : (i + 1) * GROUP]
 
 
-def weight_part(place, attn, cot):
-    grad = pl.BlockSpec((2, 2, 2, 1, PIECE, GROUP), lambda s, place: (0, 0, 0, s, 0, 0))
+def weight_part(attn, turned):
+    grad = pl.BlockSpec((2, 2, 2, 1, PIECE, GROUP), lambda s: (0, 0, 0, s, 0, 0))
     return pl.pallas_call(
         weight_kernel,
-        grid_spec=pltpu.PrefetchScalarGridSpec(
-            num_scalar_prefetch=1,
-            grid=(NS // 2,),
-            in_specs=[PAIR, whole_block((NX, 2, CAP, HALF))],
-            out_specs=[grad, grad],
-            scratch_shapes=[pltpu.VMEM((2, 2, 2 * PIECE, XROWS), BF16)],
-        ),
+        grid=(NS // 2,),
+        in_specs=[
+            pl.BlockSpec((NX, 2, 1, CAP, GROUP), lambda s: (0, 0, s, 0, 0)),
+            pl.BlockSpec(TURNED, lambda s: (0, 0, 0, 0)),
+        ],
+        out_specs=[grad, grad],
         out_shape=[jax.ShapeDtypeStruct((2, 2, 2, NS // 2, PIECE, GROUP), BF16)] * 2,
         compiler_params=params("arbitrary"),
         cost_estimate=BRIEF,
-    )(place, attn, cot)
+    )(attn, turned)
 
 
 def out_kernel(place_ref, attn_ref, u0, f0, l0, u1, f1, l1, out_ref, acc_ref):
@@ -409,24 +408,31 @@
 
 
 def cut_kernel(place_ref, keep_ref, got_ref, z0, z1, z2, z3, y0, y1, y2, y3):
+    z = 2 * pl.program_id(1) + pl.program_id(0)
+    step = lax.rem(z + 4 - (2 * place_ref[2] + place_ref[4]), 4)
     for k, (z_ref, y_ref) in enumerate(zip((z0, z1, z2, z3), (y0, y1, y2, y3))):
-        z = lax.rem(2 * place_ref[2] + place_ref[4] + k, 4)
-        zl, zh, y = lax.rem(z, 2), z // 2, lax.rem(place_ref[3] + k, 4)
-        z_ref[...] = (keep_ref[0, zl, zh].astype(F32) + got_ref[0, zl, zh].astype(F32)).astype(BF16)
-        for i in range(2):
-            for j in range(2):
-                y_ref[i, j] = (keep_ref[1, i, j, y].astype(F32) + got_ref[1, i, j, y].astype(F32)).astype(BF16)
+        y = lax.rem(place_ref[3] + k, 4)
+        y_ref[0, 0] = (keep_ref[1, 0, 0, y].astype(F32) + got_ref[1, 0, 0, y].astype(F32)).astype(BF16)
+
+        @pl.when(step == k)
+        def _():
+            z_ref[...] = (keep_ref[0, 0, 0].astype(F32) + got_ref[0, 0, 0].astype(F32)).astype(BF16)
 
 
 def cut_pieces(place, keep, got):
-    vmem = pl.BlockSpec(memory_space=pltpu.VMEM)
+    piece = pl.BlockSpec((2, 1, 1, 4, PIECE, GROUP), lambda zl, zh, place: (0, zl, zh, 0, 0, 0))
     out = pl.pallas_call(
         cut_kernel,
-        in_specs=[SMEM, vmem, vmem],
-        out_specs=[vmem] * 8,
+        grid_spec=pltpu.PrefetchScalarGridSpec(
+            num_scalar_prefetch=1,
+            grid=(2, 2),
+            in_specs=[piece, piece],
+            out_specs=[pl.BlockSpec((4, PIECE, GROUP), lambda zl, zh, place: (0, 0, 0))] * 4
+            + [pl.BlockSpec((1, 1, PIECE, GROUP), lambda zl, zh, place: (zl, zh, 0, 0))] * 4,
+        ),
         out_shape=[jax.ShapeDtypeStruct((4, PIECE, GROUP), BF16)] * 4
         + [jax.ShapeDtypeStruct((2, 2, PIECE, GROUP), BF16)] * 4,
-        compiler_params=params(),
+        compiler_params=params("arbitrary", "arbitrary"),
         cost_estimate=BRIEF,
     )(place, keep, got)
     return out[:4], out[4:]
@@ -462,7 +468,7 @@
     own = [after(v, cot) for v in own]
     qkv = swap(after(rows, cot, *own))
     pieces = own + [other_core(v) for v in own]
-    grad_part = grad_attn_part(place, cot, pieces)
+    grad_part, turned = grad_attn_part(place, cot, pieces)
     grad_attn = swap(lax.psum_scatter(grad_part, "x", scatter_dimension=0, tiled=False))
 
     attn, expo, inv = forward(bias, live, after(qkv, grad_part))
@@ -470,7 +476,7 @@
 
     head_grads = backward(live, qkv, grad_attn, expo, inv, 0, HEADS - 1)
     grads = backward(after(live, head_grads), qkv, grad_attn, expo, inv, HEADS - 1, 1)
-    keep, send = weight_part(place, after(attn, grads), cot)
+    keep, send = weight_part(after(attn, grads), turned)
     head_grads = swap(head_grads)
     grads = swap(grads)
     first, second = cut_pieces(place, keep, other_core(after(send, head_grads)))

time: 297 us -> 295 us (level)
  starting transfers between devices: 61.3 us -> 57.6 us
  transfers between devices with their start and end apart: 32 -> 32, of which waited for: 14 -> 13; matrix products, arithmetic and copies ran while one was open for 4% -> 4% of each run, Pallas kernels for 32% -> 32%
where the time goes in v4:
time: 295 us; the launch traced here: 294 us
  Pallas kernels  97.4 us (33%)
  waiting for transfers between devices  78.3 us (27%)
  starting transfers between devices  57.6 us (20%)
  blocking collectives  28.1 us (10%)
  between operations  14.4 us (5%)
  local copies, waits for them, and re-layouts  10 us (3%)
  other arithmetic  8 us (3%)
    all_to_all x4, waiting for transfers between devices, swap(): return lax.all_to_all(value, SEQ, split_axis=0, concat_axis=0, tiled=True)  41.1 us
    all_to_all x1, blocking collectives, swap(): return lax.all_to_all(value, SEQ, split_axis=0, concat_axis=0, tiled=True)  28.1 us
    pallas_call x2, Pallas kernels, backward(): pl.pallas_call(backward_kernel, grid=(count, NQ), in_specs=[COLUMN, at(so...  25.7 us
    ppermute x12, waiting for transfers between devices, along_y(): return lax.ppermute(value, 'y', [(p, (p + k) % 4) for p in range(4)])  18 us
    ppermute x12, starting transfers between devices, along_y(): return lax.ppermute(value, 'y', [(p, (p + k) % 4) for p in range(4)])  17.2 us
    all_to_all x4, starting transfers between devices, swap(): return lax.all_to_all(value, SEQ, split_axis=0, concat_axis=0, tiled=True)  16.8 us
    pallas_call x1, Pallas kernels, forward(): pl.pallas_call(forward_kernel, grid=(HEADS, NQ), in_specs=[pl.BlockSpec((...  15 us
    pallas_call x1, Pallas kernels, grad_attn_part(): pl.pallas_call(grad_attn_kernel, grid_spec=pltpu.PrefetchScalarGridSpec(n...  13 us
  transfers between devices with their start and end apart: 32, of which 13 were waited for; matrix products, arithmetic and copies ran while one was open for 4% of the time, Pallas kernels for 32%

profile of v4, /device:TPU:0, one launch (start us, length us, event | category | flops | bytes accessed | tf_op | source)
XLA Modules:
  0.0 293.8 jit_solution(14506593344767619936)
XLA Ops:
  14.6 4.1 %collective-permute-start.3 = (bf16[192,640]{1,0:T(8,128)(2,1)S(1)}, bf16[192,640]{1,0:T(8,128)(2,1)S(1)}, u32[]{:S(2)}, u32[]{:S(2)}) collective-permute-start(bf16[192,640]{1,0:T(8,128)(2,1)S(1)} %dynamic-slice.1), channel_id=1, source_target_pairs={{0,68},{68,0},{64,4},{4,64},{1,69},{69,1},{65,5},{5,65},{2,70},{70... | collective-permute-start | bytes 737288 | tf_op jit(solution)/shard_map/ppermute | solution.py:385
  21.8 5.3 %shard_map.110 = bf16[8,3,160,384]{3,2,1,0:T(8,128)(2,1)} custom-call(s32[160,1]{1,0:T(8,128)} %fusion.5.pick_ref, bf16[256,3072]{1,0:T(8,128)(2,1)} %bitcast.73, bf16[256,3072]{1,0:T(8,128)(2,1)} %bitcast.74, bf16[256,3072]{1,0:T(8,128)(2,1)} %bitcast.75), custom_call_target="tpu_custom_call" | custom-call | flops 1 | bytes 1 | tf_op jit(solution)/shard_map/pallas_call | solution.py:51
  28.7 2.7 shard_map.111
  31.5 4.4 %all-to-all-start = ((bf16[4,2,160,640]{3,2,1,0:T(8,128)(2,1)}), bf16[4,2,160,640]{3,2,1,0:T(8,128)(2,1)}, u32[]{:S(2)}, u32[]{:S(2)}) async-start(bf16[4,2,160,640]{3,2,1,0:T(8,128)(2,1)} %shard_map.111), calls=%async_computation | async-start | bytes 3276800 | tf_op jit(solution)/shard_map/all_to_all | solution.py:237
  35.8 2.6 collective-permute-start.6
  41.6 16.5 %collective-permute-done.6 = bf16[2,192,640]{2,1,0:T(8,128)(2,1)S(1)} collective-permute-done((bf16[2,192,640]{2,1,0:T(8,128)(2,1)S(1)}, bf16[2,192,640]{2,1,0:T(8,128)(2,1)S(1)}, u32[]{:S(2)}, u32[]{:S(2)}) %collective-permute-start.6) | collective-permute-done | bytes 491552 | tf_op jit(solution)/shard_map/ppermute | solution.py:376
  58.4 3.4 %collective-permute-done.4.f0 = bf16[4,192,640]{2,1,0:T(8,128)(2,1)} collective-permute-done((bf16[4,192,640]{2,1,0:T(8,128)(2,1)S(1)}, bf16[4,192,640]{2,1,0:T(8,128)(2,1)}, u32[]{:S(2)}, u32[]{:S(2)}) %collective-permute-start.4) | collective-permute-done | bytes 983072 | tf_op jit(solution)/shard_map/ppermute | solution.py:385
  64.0 4.4 %all-to-all-start.1 = ((bf16[8,3,160,384]{3,2,1,0:T(8,128)(2,1)}), bf16[8,3,160,384]{3,2,1,0:T(8,128)(2,1)}, u32[]{:S(2)}, u32[]{:S(2)}) async-start(bf16[8,3,160,384]{3,2,1,0:T(8,128)(2,1)} %shard_map.110), calls=%async_computation.1 | async-start | bytes 5898240 | tf_op jit(solution)/shard_map/all_to_all | solution.py:368
  68.5 13.0 %shard_map.112 = (bf16[4,2,4,160,384]{4,3,2,1,0:T(8,128)(2,1)}, bf16[2,2,320,640]{3,2,1,0:T(8,128)(2,1)}) custom-call(s32[5]{0:T(128)} %stack.32.place_ref, bf16[4,2,160,640]{3,2,1,0:T(8,128)(2,1)} %all-to-all-done.in_ref, bf16[4,192,640]{2,1,0:T(8,128)(2,1)} %copy-done.3, bf16[4,192,640]{2,1,0:T(8,128)(2,1)} %collective-permute-done.4.f0, ...), custom_call_target="tpu_custom_call" | custom-call | flops 199999995904 | bytes 1 | tf_op jit(solution)/shard_map/pallas_call | solution.py:280
  81.5 25.0 %all-to-all-done.1.q_ref.k_ref.v_ref = bf16[8,3,160,384]{3,2,1,0:T(8,128)(2,1)} async-done(((bf16[8,3,160,384]{3,2,1,0:T(8,128)(2,1)}), bf16[8,3,160,384]{3,2,1,0:T(8,128)(2,1)}, u32[]{:S(2)}, u32[]{:S(2)}) %all-to-all-start.1) | async-done | bytes 2949152 | tf_op jit(solution)/shard_map/all_to_all | solution.py:368
  106.5 15.0 %shard_map.113 = (bf16[8,160,384]{2,1,0:T(8,128)(2,1)}, bf16[3,1280,1280]{2,1,0:T(8,128)(2,1)}, f32[3,8,160,1]{3,2,1,0:T(8,128)}) custom-call(f32[1,1280]{1,0:T(1,128)} %select_n.165.bias_ref, f32[8,160,1]{2,1,0:T(8,128)} %fusion.live_ref, bf16[8,3,160,384]{3,2,1,0:T(8,128)(2,1)} %all-to-all-done.1.q_ref.k_ref.v_ref, ...), custom_call_target="tpu_custom_call" | custom-call | flops 199999995904 | bytes 1 | tf_op jit(solution)/shard_map/pallas_call | solution.py:120
  121.5 28.1 %all_to_all.35 = bf16[8,160,384]{2,1,0:T(8,128)(2,1)} all-to-all(bf16[8,160,384]{2,1,0:T(8,128)(2,1)} %get-tuple-element.48), channel_id=1, replica_groups=mesh['zl'=2,'x'=4,'c'=2,'zh'=2,'y'=4] {'zh','y'}, dimensions={0} | all-to-all | bytes 1966080 | tf_op jit(solution)/shard_map/all_to_all | solution.py:368
  149.6 3.6 %all-to-all-start.3 = ((bf16[8,160,384]{2,1,0:T(8,128)(2,1)}), bf16[8,160,384]{2,1,0:T(8,128)(2,1)S(1)}, u32[]{:S(2)}, u32[]{:S(2)}) async-start(bf16[8,160,384]{2,1,0:T(8,128)(2,1)} %bitcast.76), calls=%async_computation.4 | async-start | bytes 1966080 | tf_op jit(solution)/shard_map/all_to_all | solution.py:368
  153.9 13.7 %all-to-all-done.3.grad_ref = bf16[8,160,384]{2,1,0:T(8,128)(2,1)S(1)} async-done(((bf16[8,160,384]{2,1,0:T(8,128)(2,1)}), bf16[8,160,384]{2,1,0:T(8,128)(2,1)S(1)}, u32[]{:S(2)}, u32[]{:S(2)}) %all-to-all-start.3) | async-done | bytes 983072 | tf_op jit(solution)/shard_map/all_to_all | solution.py:368
  168.6 16.3 %shard_map.114 = bf16[8,3,160,256]{3,2,1,0:T(8,128)(2,1)} custom-call(f32[8,160,1]{2,1,0:T(8,128)} %fusion.live_ref, bf16[8,3,160,384]{3,2,1,0:T(8,128)(2,1)} %all-to-all-done.1.q_ref.k_ref.v_ref, bf16[8,3,160,384]{3,2,1,0:T(8,128)(2,1)} %all-to-all-done.1.q_ref.k_ref.v_ref, bf16[8,3,160,384]{3,2,1,0:T(8,128)(2,1)} %all-to-all-done.1.q_ref.k_ref.v_ref, ...), custom_call_target="tpu_custom_call" | custom-call | flops 199999995904 | bytes 1 | tf_op jit(solution)/shard_map/pallas_call | solution.py:174
  184.9 4.3 %all-to-all-start.4 = ((bf16[8,3,160,256]{3,2,1,0:T(8,128)(2,1)}), bf16[8,3,160,256]{3,2,1,0:T(8,128)(2,1)}, u32[]{:S(2)}, u32[]{:S(2)}) async-start(bf16[8,3,160,256]{3,2,1,0:T(8,128)(2,1)} %shard_map.114), calls=%async_computation.5 | async-start | bytes 3932160 | tf_op jit(solution)/shard_map/all_to_all | solution.py:368
  189.2 9.4 %shard_map.115 = bf16[8,3,160,128]{3,2,1,0:T(8,128)(2,1)} custom-call(f32[8,160,1]{2,1,0:T(8,128)} %fusion.live_ref, bf16[8,3,160,384]{3,2,1,0:T(8,128)(2,1)} %all-to-all-done.1.q_ref.k_ref.v_ref, bf16[8,3,160,384]{3,2,1,0:T(8,128)(2,1)} %all-to-all-done.1.q_ref.k_ref.v_ref, bf16[8,3,160,384]{3,2,1,0:T(8,128)(2,1)} %all-to-all-done.1.q_ref.k_ref.v_ref, ...), custom_call_target="tpu_custom_call" | custom-call | flops 199999995904 | bytes 1 | tf_op jit(solution)/shard_map/pallas_call | solution.py:174
  198.6 4.8 %all-gather.3.cloned.1.call-done = bf16[32,160,384]{2,1,0:T(8,128)(2,1)} async-done(((bf16[8,160,384]{2,1,0:T(8,128)(2,1)}), bf16[32,160,384]{2,1,0:T(8,128)(2,1)}) %all-gather.3.cloned.1.call-update) | async-done | bytes 3932176 | tf_op jit(solution)/shard_map/all_gather | solution.py:475
  203.4 10.1 %shard_map.116 = (bf16[2,2,2,4,160,384]{5,4,3,2,1,0:T(8,128)(2,1)}, bf16[2,2,2,4,160,384]{5,4,3,2,1,0:T(8,128)(2,1)}) custom-call(bf16[4,2,4,160,384]{4,3,2,1,0:T(8,128)(2,1)} %bitcast.65, bf16[2,2,320,640]{3,2,1,0:T(8,128)(2,1)} %get-tuple-element.53.turn_ref), custom_call_target="tpu_custom_call" | custom-call | flops 1 | bytes 1 | tf_op jit(solution)/shard_map/pallas_call | solution.py:315
  213.6 2.5 all-to-all-done.4.first_ref
  216.0 4.4 %all-to-all-start.5 = ((bf16[8,3,160,128]{3,2,1,0:T(8,128)(2,1)}), bf16[8,3,160,128]{3,2,1,0:T(8,128)(2,1)S(1)}, u32[]{:S(2)}, u32[]{:S(2)}) async-start(bf16[8,3,160,128]{3,2,1,0:T(8,128)(2,1)} %shard_map.115), calls=%async_computation.6 | async-start | bytes 1966080 | tf_op jit(solution)/shard_map/all_to_all | solution.py:368
  220.5 2.7 collective-permute-done.11.got_ref
  223.2 6.7 %shard_map.117 = (bf16[4,160,384]{2,1,0:T(8,128)(2,1)}, bf16[4,160,384]{2,1,0:T(8,128)(2,1)}, bf16[4,160,384]{2,1,0:T(8,128)(2,1)}, bf16[4,160,384]{2,1,0:T(8,12...) custom-call(s32[5]{0:T(128)} %stack.32.place_ref, ...), custom_call_target="tpu_custom_call" | custom-call | flops 1 | bytes 1 | tf_op jit(solution)/shard_map/pallas_call | solution.py:424
  230.7 2.4 collective-permute-start.13
  234.0 2.4 collective-permute-start.16
  236.3 11.2 %shard_map.118 = bf16[4,2,160,640]{3,2,1,0:T(8,128)(2,1)} custom-call(s32[5]{0:T(128)} %stack.32.place_ref, bf16[4,2,4,160,384]{4,3,2,1,0:T(8,128)(2,1)} %bitcast.66, bf16[4,192,640]{2,1,0:T(8,128)(2,1)} %copy-done.3, bf16[4,192,640]{2,1,0:T(8,128)(2,1)} %collective-permute-done.4.f0, bf16[2,4,192,640]{3,2,1,0:T(8,128)(2,1)} %bitcast.69, ...), custom_call_target="tpu_custom_call" | custom-call | flops 1 | bytes 1 | tf_op jit(solution)/shard_map/pallas_call | solution.py:348
  251.2 5.1 %shard_map.119 = (bf16[256,3072]{1,0:T(8,128)(2,1)}, bf16[256,3072]{1,0:T(8,128)(2,1)}, bf16[256,3072]{1,0:T(8,128)(2,1)}) custom-call(s32[1,160]{1,0:T(1,128)} %compare_select_fusion.pick_ref, bf16[8,3,160,256]{3,2,1,0:T(8,128)(2,1)} %all-to-all-done.4.first_ref, bf16[8,3,160,128]{3,2,1,0:T(8,128)(2,1)} %copy-done.2), custom_call_target="tpu_custom_call" | custom-call | flops 1 | bytes 1 | tf_op jit(solution)/shard_map/pallas_call | solution.py:72
  258.1 3.9 %all-to-all-start.6 = ((bf16[4,2,160,640]{3,2,1,0:T(8,128)(2,1)}), bf16[4,2,160,640]{3,2,1,0:T(8,128)(2,1)S(1)}, u32[]{:S(2)}, u32[]{:S(2)}) async-start(bf16[4,2,160,640]{3,2,1,0:T(8,128)(2,1)} %shard_map.118), calls=%async_computation.7 | async-start | bytes 3276800 | tf_op jit(solution)/shard_map/all_to_all | solution.py:237
  265.0 2.8 collective-permute-start.19
  269.7 2.9 collective-permute-start.22
  279.9 3.1 %all-to-all-done.6.in_ref = bf16[4,2,160,640]{3,2,1,0:T(8,128)(2,1)S(1)} async-done(((bf16[4,2,160,640]{3,2,1,0:T(8,128)(2,1)}), bf16[4,2,160,640]{3,2,1,0:T(8,128)(2,1)S(1)}, u32[]{:S(2)}, u32[]{:S(2)}) %all-to-all-start.6) | async-done | bytes 1638432 | tf_op jit(solution)/shard_map/all_to_all | solution.py:237
  284.2 2.7 shard_map.120
  (96 shorter events, 40.0 us)
Async XLA Ops:
  8.3 18.8 %collective-permute-start = (bf16[192,640]{1,0:T(8,128)(2,1)S(1)}, bf16[192,640]{1,0:T(8,128)(2,1)S(1)}, u32[]{:S(2)}, u32[]{:S(2)}) collective-permute-start(bf16[192,640]{1,0:T(8,128)(2,1)S(1)} %get-tuple-element.72), channel_id=1, source_target_pairs={{0,1},{1,2},{2,3},{3,0},{4,5},{5,6},{6,7},{7,4},{8,9},{9,10},{10,1... | collective-permute-start | bytes 737288 | tf_op jit(solution)/shard_map/ppermute | solution.py:376
  10.0 17.2 %collective-permute-start.1 = (bf16[192,640]{1,0:T(8,128)(2,1)S(1)}, bf16[192,640]{1,0:T(8,128)(2,1)S(1)}, u32[]{:S(2)}, u32[]{:S(2)}) collective-permute-start(bf16[192,640]{1,0:T(8,128)(2,1)S(1)} %get-tuple-element.72), channel_id=1, source_target_pairs={{0,3},{1,0},{2,1},{3,2},{4,7},{5,4},{6,5},{7,6},{8,11},{9,8},{10,9... | collective-permute-start | bytes 737288 | tf_op jit(solution)/shard_map/ppermute | solution.py:376
  11.6 15.6 %collective-permute-start.2 = (bf16[192,640]{1,0:T(8,128)(2,1)S(1)}, bf16[192,640]{1,0:T(8,128)(2,1)S(1)}, u32[]{:S(2)}, u32[]{:S(2)}) collective-permute-start(bf16[192,640]{1,0:T(8,128)(2,1)S(1)} %get-tuple-element.72), channel_id=1, source_target_pairs={{0,2},{1,3},{2,0},{3,1},{4,6},{5,7},{6,4},{7,5},{8,10},{9,11},{10,... | collective-permute-start | bytes 737288 | tf_op jit(solution)/shard_map/ppermute | solution.py:376
  14.6 12.5 %collective-permute-start.3 = (bf16[192,640]{1,0:T(8,128)(2,1)S(1)}, bf16[192,640]{1,0:T(8,128)(2,1)S(1)}, u32[]{:S(2)}, u32[]{:S(2)}) collective-permute-start(bf16[192,640]{1,0:T(8,128)(2,1)S(1)} %dynamic-slice.1), channel_id=1, source_target_pairs={{0,68},{68,0},{64,4},{4,64},{1,69},{69,1},{65,5},{5,65},{2,70},{70... | collective-permute-start | bytes 737288 | tf_op jit(solution)/shard_map/ppermute | solution.py:385
  27.3 13.2 %collective-permute-start.5 = (bf16[2,192,640]{2,1,0:T(8,128)(2,1)S(1)}, bf16[2,192,640]{2,1,0:T(8,128)(2,1)}, u32[]{:S(2)}, u32[]{:S(2)}) collective-permute-start(bf16[2,192,640]{2,1,0:T(8,128)(2,1)S(1)} %pad_maximum_fusion), channel_id=1, source_target_pairs={{0,1},{1,2},{2,3},{3,0},{4,5},{5,6},{6,7},{7,4},{8,9},{9,10},{10,1... | collective-permute-start | bytes 1474568 | tf_op jit(solution)/shard_map/ppermute | solution.py:376
  31.5 26.8 %all-to-all-start = ((bf16[4,2,160,640]{3,2,1,0:T(8,128)(2,1)}), bf16[4,2,160,640]{3,2,1,0:T(8,128)(2,1)}, u32[]{:S(2)}, u32[]{:S(2)}) async-start(bf16[4,2,160,640]{3,2,1,0:T(8,128)(2,1)} %shard_map.111), calls=%async_computation | async-start | bytes 3276800 | tf_op jit(solution)/shard_map/all_to_all | solution.py:237
  35.8 22.3 %collective-permute-start.6 = (bf16[2,192,640]{2,1,0:T(8,128)(2,1)S(1)}, bf16[2,192,640]{2,1,0:T(8,128)(2,1)S(1)}, u32[]{:S(2)}, u32[]{:S(2)}) collective-permute-start(bf16[2,192,640]{2,1,0:T(8,128)(2,1)S(1)} %pad_maximum_fusion), channel_id=1, source_target_pairs={{0,3},{1,0},{2,1},{3,2},{4,7},{5,4},{6,5},{7,6},{8,11},{9,8},{10,9... | collective-permute-start | bytes 1474568 | tf_op jit(solution)/shard_map/ppermute | solution.py:376
  38.5 19.7 %collective-permute-start.7 = (bf16[2,192,640]{2,1,0:T(8,128)(2,1)S(1)}, bf16[2,192,640]{2,1,0:T(8,128)(2,1)S(1)}, u32[]{:S(2)}, u32[]{:S(2)}) collective-permute-start(bf16[2,192,640]{2,1,0:T(8,128)(2,1)S(1)} %pad_maximum_fusion), channel_id=1, source_target_pairs={{0,2},{1,3},{2,0},{3,1},{4,6},{5,7},{6,4},{7,5},{8,10},{9,11},{10,... | collective-permute-start | bytes 1474568 | tf_op jit(solution)/shard_map/ppermute | solution.py:376
  38.8 23.0 %collective-permute-start.4 = (bf16[4,192,640]{2,1,0:T(8,128)(2,1)S(1)}, bf16[4,192,640]{2,1,0:T(8,128)(2,1)}, u32[]{:S(2)}, u32[]{:S(2)}) collective-permute-start(bf16[4,192,640]{2,1,0:T(8,128)(2,1)S(1)} %bitcast_dynamic-update-slice_fusion.4.u0), channel_id=1, source_target_pairs={{0,68},{68,0},{64,4},{4,64},{1,69},{69,1},{65,5},{5,65},{2,70},{70... | collective-permute-start | bytes 2949128 | tf_op jit(solution)/shard_map/ppermute | solution.py:385
  58.3 10.3 %collective-permute-start.10 = (bf16[2,4,192,640]{3,2,1,0:T(8,128)(2,1)S(1)}, bf16[2,4,192,640]{3,2,1,0:T(8,128)(2,1)}, u32[]{:S(2)}, u32[]{:S(2)}) collective-permute-start(bf16[2,4,192,640]{3,2,1,0:T(8,128)(2,1)S(1)} %bitcast.67), channel_id=1, source_target_pairs={{0,8},{8,0},{1,9},{9,1},{2,10},{10,2},{3,11},{11,3},{4,12},{12,4},... | collective-permute-start | bytes 5898248 | tf_op jit(solution)/shard_map/ppermute | solution.py:364
  61.8 6.7 %collective-permute-start.9 = (bf16[4,192,640]{2,1,0:T(8,128)(2,1)}, bf16[4,192,640]{2,1,0:T(8,128)(2,1)}, u32[]{:S(2)}, u32[]{:S(2)}) collective-permute-start(bf16[4,192,640]{2,1,0:T(8,128)(2,1)} %collective-permute-done.4.f0), channel_id=1, source_target_pairs={{0,8},{8,0},{1,9},{9,1},{2,10},{10,2},{3,11},{11,3},{4,12},{12,4},... | collective-permute-start | bytes 2949128 | tf_op jit(solution)/shard_map/ppermute | solution.py:364
  61.8 6.7 %collective-permute-start.8 = (bf16[4,192,640]{2,1,0:T(8,128)(2,1)S(1)}, bf16[4,192,640]{2,1,0:T(8,128)(2,1)}, u32[]{:S(2)}, u32[]{:S(2)}) collective-permute-start(bf16[4,192,640]{2,1,0:T(8,128)(2,1)S(1)} %bitcast_dynamic-update-slice_fusion.4.u0), channel_id=1, source_target_pairs={{0,8},{8,0},{1,9},{9,1},{2,10},{10,2},{3,11},{11,3},{4,12},{12,4},... | collective-permute-start | bytes 2949128 | tf_op jit(solution)/shard_map/ppermute | solution.py:364
  64.0 42.5 %all-to-all-start.1 = ((bf16[8,3,160,384]{3,2,1,0:T(8,128)(2,1)}), bf16[8,3,160,384]{3,2,1,0:T(8,128)(2,1)}, u32[]{:S(2)}, u32[]{:S(2)}) async-start(bf16[8,3,160,384]{3,2,1,0:T(8,128)(2,1)} %shard_map.110), calls=%async_computation.1 | async-start | bytes 5898240 | tf_op jit(solution)/shard_map/all_to_all | solution.py:368
  68.5 81.1 %reduce-scatter.2.cloned.1.call-start = ((), (), s32[]{:S(2)}) async-start(), calls=%async_computation.8 | async-start | bytes 4915200 | tf_op jit(solution)/shard_map/reduce_scatter | solution.py:472
  149.6 18.0 %all-to-all-start.3 = ((bf16[8,160,384]{2,1,0:T(8,128)(2,1)}), bf16[8,160,384]{2,1,0:T(8,128)(2,1)S(1)}, u32[]{:S(2)}, u32[]{:S(2)}) async-start(bf16[8,160,384]{2,1,0:T(8,128)(2,1)} %bitcast.76), calls=%async_computation.4 | async-start | bytes 1966080 | tf_op jit(solution)/shard_map/all_to_all | solution.py:368
  153.2 50.2 %all-gather.3.cloned.1.call-start = ((), (), s32[]{:S(2)}) async-start(), calls=%async_computation.9 | async-start | bytes 4915200 | tf_op jit(solution)/shard_map/all_gather | solution.py:475
  184.9 31.2 %all-to-all-start.4 = ((bf16[8,3,160,256]{3,2,1,0:T(8,128)(2,1)}), bf16[8,3,160,256]{3,2,1,0:T(8,128)(2,1)}, u32[]{:S(2)}, u32[]{:S(2)}) async-start(bf16[8,3,160,256]{3,2,1,0:T(8,128)(2,1)} %shard_map.114), calls=%async_computation.5 | async-start | bytes 3932160 | tf_op jit(solution)/shard_map/all_to_all | solution.py:368
  216.0 7.1 %collective-permute-start.11 = (bf16[2,2,2,4,160,384]{5,4,3,2,1,0:T(8,128)(2,1)}, bf16[2,2,2,4,160,384]{5,4,3,2,1,0:T(8,128)(2,1)}, u32[]{:S(2)}, u32[]{:S(2)}) collective-permute-start(bf16[2,2,2,4,160,384]{5,4,3,2,1,0:T(8,128)(2,1)} %get-tuple-element.56), channel_id=1, source_target_pairs={{0,8},{8,0},{1,9},{9,1},{2,10},{10,2},{3,11},{11,3},{4,12},{12,4},... | collective-permute-start | bytes 11796488 | tf_op jit(solution)/shard_map/ppermute | solution.py:364
  216.0 34.2 %all-to-all-start.5 = ((bf16[8,3,160,128]{3,2,1,0:T(8,128)(2,1)}), bf16[8,3,160,128]{3,2,1,0:T(8,128)(2,1)S(1)}, u32[]{:S(2)}, u32[]{:S(2)}) async-start(bf16[8,3,160,128]{3,2,1,0:T(8,128)(2,1)} %shard_map.115), calls=%async_computation.6 | async-start | bytes 1966080 | tf_op jit(solution)/shard_map/all_to_all | solution.py:368
  229.8 17.7 %collective-permute-start.12 = (bf16[2,2,160,384]{3,2,1,0:T(8,128)(2,1)}, bf16[2,2,160,384]{3,2,1,0:T(8,128)(2,1)S(1)}, u32[]{:S(2)}, u32[]{:S(2)}) collective-permute-start(bf16[2,2,160,384]{3,2,1,0:T(8,128)(2,1)} %get-tuple-element.62), channel_id=1, source_target_pairs={{0,1},{1,2},{2,3},{3,0},{4,5},{5,6},{6,7},{7,4},{8,9},{9,10},{10,1... | collective-permute-start | bytes 1474568 | tf_op jit(solution)/shard_map/ppermute | solution.py:376
  230.7 25.5 %collective-permute-start.13 = (bf16[2,2,160,384]{3,2,1,0:T(8,128)(2,1)}, bf16[2,2,160,384]{3,2,1,0:T(8,128)(2,1)S(1)}, u32[]{:S(2)}, u32[]{:S(2)}) collective-permute-start(bf16[2,2,160,384]{3,2,1,0:T(8,128)(2,1)} %get-tuple-element.64), channel_id=1, source_target_pairs={{0,3},{1,0},{2,1},{3,2},{4,7},{5,4},{6,5},{7,6},{8,11},{9,8},{10,9... | collective-permute-start | bytes 1474568 | tf_op jit(solution)/shard_map/ppermute | solution.py:376
  233.1 23.7 %collective-permute-start.14 = (bf16[2,2,160,384]{3,2,1,0:T(8,128)(2,1)}, bf16[2,2,160,384]{3,2,1,0:T(8,128)(2,1)}, u32[]{:S(2)}, u32[]{:S(2)}) collective-permute-start(bf16[2,2,160,384]{3,2,1,0:T(8,128)(2,1)} %get-tuple-element.63), channel_id=1, source_target_pairs={{0,2},{1,3},{2,0},{3,1},{4,6},{5,7},{6,4},{7,5},{8,10},{9,11},{10,... | collective-permute-start | bytes 1474568 | tf_op jit(solution)/shard_map/ppermute | solution.py:376
  233.1 28.9 %collective-permute-start.15 = (bf16[4,160,384]{2,1,0:T(8,128)(2,1)}, bf16[4,160,384]{2,1,0:T(8,128)(2,1)}, u32[]{:S(2)}, u32[]{:S(2)}) collective-permute-start(bf16[4,160,384]{2,1,0:T(8,128)(2,1)} %get-tuple-element.58), channel_id=1, source_target_pairs={{0,64},{64,4},{4,68},{68,0},{1,65},{65,5},{5,69},{69,1},{2,66},{66... | collective-permute-start | bytes 1474568 | tf_op jit(solution)/shard_map/ppermute | solution.py:381
  234.0 28.8 %collective-permute-start.16 = (bf16[4,160,384]{2,1,0:T(8,128)(2,1)}, bf16[4,160,384]{2,1,0:T(8,128)(2,1)}, u32[]{:S(2)}, u32[]{:S(2)}) collective-permute-start(bf16[4,160,384]{2,1,0:T(8,128)(2,1)} %get-tuple-element.60), channel_id=1, source_target_pairs={{0,68},{64,0},{4,64},{68,4},{1,69},{65,1},{5,65},{69,5},{2,70},{66... | collective-permute-start | bytes 1474568 | tf_op jit(solution)/shard_map/ppermute | solution.py:381
  247.5 14.4 %collective-permute-start.17 = (bf16[4,160,384]{2,1,0:T(8,128)(2,1)}, bf16[4,160,384]{2,1,0:T(8,128)(2,1)S(1)}, u32[]{:S(2)}, u32[]{:S(2)}) collective-permute-start(bf16[4,160,384]{2,1,0:T(8,128)(2,1)} %get-tuple-element.70), channel_id=1, source_target_pairs={{0,4},{64,68},{4,0},{68,64},{1,5},{65,69},{5,1},{69,65},{2,6},{66,... | collective-permute-start | bytes 1474568 | tf_op jit(solution)/shard_map/ppermute | solution.py:381
  258.1 24.9 %all-to-all-start.6 = ((bf16[4,2,160,640]{3,2,1,0:T(8,128)(2,1)}), bf16[4,2,160,640]{3,2,1,0:T(8,128)(2,1)S(1)}, u32[]{:S(2)}, u32[]{:S(2)}) async-start(bf16[4,2,160,640]{3,2,1,0:T(8,128)(2,1)} %shard_map.118), calls=%async_computation.7 | async-start | bytes 3276800 | tf_op jit(solution)/shard_map/all_to_all | solution.py:237
  264.4 8.2 %collective-permute-start.18 = (bf16[160,384]{1,0:T(8,128)(2,1)S(1)}, bf16[160,384]{1,0:T(8,128)(2,1)S(1)}, u32[]{:S(2)}, u32[]{:S(2)}) collective-permute-start(bf16[160,384]{1,0:T(8,128)(2,1)S(1)} %get-tuple-element.73), channel_id=1, source_target_pairs={{0,1},{1,2},{2,3},{3,0},{4,5},{5,6},{6,7},{7,4},{8,9},{9,10},{10,1... | collective-permute-start | bytes 368648 | tf_op jit(solution)/shard_map/ppermute | solution.py:376
  265.0 9.5 %collective-permute-start.19 = (bf16[160,384]{1,0:T(8,128)(2,1)S(1)}, bf16[160,384]{1,0:T(8,128)(2,1)S(1)}, u32[]{:S(2)}, u32[]{:S(2)}) collective-permute-start(bf16[160,384]{1,0:T(8,128)(2,1)S(1)} %get-tuple-element.75), channel_id=1, source_target_pairs={{0,3},{1,0},{2,1},{3,2},{4,7},{5,4},{6,5},{7,6},{8,11},{9,8},{10,9... | collective-permute-start | bytes 368648 | tf_op jit(solution)/shard_map/ppermute | solution.py:376
  267.7 6.7 %collective-permute-start.20 = (bf16[160,384]{1,0:T(8,128)(2,1)S(1)}, bf16[160,384]{1,0:T(8,128)(2,1)S(1)}, u32[]{:S(2)}, u32[]{:S(2)}) collective-permute-start(bf16[160,384]{1,0:T(8,128)(2,1)S(1)} %get-tuple-element.74), channel_id=1, source_target_pairs={{0,2},{1,3},{2,0},{3,1},{4,6},{5,7},{6,4},{7,5},{8,10},{9,11},{10,... | collective-permute-start | bytes 368648 | tf_op jit(solution)/shard_map/ppermute | solution.py:376
  269.3 7.1 %collective-permute-start.21 = (bf16[160,384]{1,0:T(8,128)(2,1)S(1)}, bf16[160,384]{1,0:T(8,128)(2,1)S(1)}, u32[]{:S(2)}, u32[]{:S(2)}) collective-permute-start(bf16[160,384]{1,0:T(8,128)(2,1)S(1)} %get-tuple-element.76), channel_id=1, source_target_pairs={{0,64},{64,4},{4,68},{68,0},{1,65},{65,5},{5,69},{69,1},{2,66},{66... | collective-permute-start | bytes 368648 | tf_op jit(solution)/shard_map/ppermute | solution.py:381
  269.7 7.1 %collective-permute-start.22 = (bf16[160,384]{1,0:T(8,128)(2,1)S(1)}, bf16[160,384]{1,0:T(8,128)(2,1)S(1)}, u32[]{:S(2)}, u32[]{:S(2)}) collective-permute-start(bf16[160,384]{1,0:T(8,128)(2,1)S(1)} %get-tuple-element.78), channel_id=1, source_target_pairs={{0,68},{64,0},{4,64},{68,4},{1,69},{65,1},{5,65},{69,5},{2,70},{66... | collective-permute-start | bytes 368648 | tf_op jit(solution)/shard_map/ppermute | solution.py:381
  272.6 6.4 %collective-permute-start.23 = (bf16[160,384]{1,0:T(8,128)(2,1)S(1)}, bf16[160,384]{1,0:T(8,128)(2,1)S(1)}, u32[]{:S(2)}, u32[]{:S(2)}) collective-permute-start(bf16[160,384]{1,0:T(8,128)(2,1)S(1)} %get-tuple-element.77), channel_id=1, source_target_pairs={{0,4},{64,68},{4,0},{68,64},{1,5},{65,69},{5,1},{69,65},{2,6},{66,... | collective-permute-start | bytes 368648 | tf_op jit(solution)/shard_map/ppermute | solution.py:381
  (11 other events, 94.1 us)
Sparse Core Ops, SparseCore 0:
  81.6 46.5 reduce-scatter.1
  155.7 47.6 all-gather.2

commit v5 on v4

--- a/solution.py
+++ b/solution.py
@@ -484,7 +484,7 @@
     out = out_part(place, after(attn, *first, *second), pieces)
     first = [*first[:2], after(first[2], out), first[3]]
     first, second = ring(along_z, first).astype(BF16), ring(along_y, second).astype(BF16)
-    out = after(out, second, *token_grads)
+    out = after(out, *token_grads)
     output = join_columns(place, x_exchange(out))
     grad_weight = second_phase(first, second, place).T
     grad_query, grad_key, grad_value = token_grads

time: 295 us -> 301 us (1.020)
  waiting for transfers between devices: 78.3 us -> 85.9 us
    ppermute x6, waiting for transfers between devices: 4.5 us -> 14.5 us  [along_z(): lax.ppermute(value, ('zl', 'zh'), [(index[z], index[(z + k) % 4]) for z i...]
  transfers between devices with their start and end apart: 32 -> 32, of which waited for: 13 -> 12; matrix products, arithmetic and copies ran while one was open for 4% -> 4% of each run, Pallas kernels for 32% -> 32%
where the time goes in v5:
time: 301 us; the launch traced here: 300 us
  Pallas kernels  97.4 us (32%)
  waiting for transfers between devices  85.9 us (29%)
  starting transfers between devices  56.7 us (19%)
  blocking collectives  28.1 us (9%)
  between operations  14.4 us (5%)
  local copies, waits for them, and re-layouts  9.26 us (3%)
  other arithmetic  8.02 us (3%)
    all_to_all x4, waiting for transfers between devices, swap(): return lax.all_to_all(value, SEQ, split_axis=0, concat_axis=0, tiled=True)  41.1 us
    all_to_all x1, blocking collectives, swap(): return lax.all_to_all(value, SEQ, split_axis=0, concat_axis=0, tiled=True)  28.1 us
    pallas_call x2, Pallas kernels, backward(): pl.pallas_call(backward_kernel, grid=(count, NQ), in_specs=[COLUMN, at(so...  25.7 us
    ppermute x12, starting transfers between devices, along_y(): return lax.ppermute(value, 'y', [(p, (p + k) % 4) for p in range(4)])  17.9 us
    ppermute x12, waiting for transfers between devices, along_y(): return lax.ppermute(value, 'y', [(p, (p + k) % 4) for p in range(4)])  17.5 us
    all_to_all x4, starting transfers between devices, swap(): return lax.all_to_all(value, SEQ, split_axis=0, concat_axis=0, tiled=True)  16.8 us
    pallas_call x1, Pallas kernels, forward(): pl.pallas_call(forward_kernel, grid=(HEADS, NQ), in_specs=[pl.BlockSpec((...  15 us
    ppermute x6, waiting for transfers between devices, along_z(): lax.ppermute(value, ('zl', 'zh'), [(index[z], index[(z + k) % 4]) for z i...  14.5 us
  transfers between devices with their start and end apart: 32, of which 12 were waited for; matrix products, arithmetic and copies ran while one was open for 4% of the time, Pallas kernels for 32%

profile of v5, /device:TPU:0, one launch (start us, length us, event | category | flops | bytes accessed | tf_op | source)
XLA Modules:
  0.0 299.9 jit_solution(3026485556675306290)
XLA Ops:
  14.6 4.1 %collective-permute-start.3 = (bf16[192,640]{1,0:T(8,128)(2,1)S(1)}, bf16[192,640]{1,0:T(8,128)(2,1)S(1)}, u32[]{:S(2)}, u32[]{:S(2)}) collective-permute-start(bf16[192,640]{1,0:T(8,128)(2,1)S(1)} %dynamic-slice.1), channel_id=1, source_target_pairs={{0,68},{68,0},{64,4},{4,64},{1,69},{69,1},{65,5},{5,65},{2,70},{70... | collective-permute-start | bytes 737288 | tf_op jit(solution)/shard_map/ppermute | solution.py:385
  21.8 5.3 %shard_map.110 = bf16[8,3,160,384]{3,2,1,0:T(8,128)(2,1)} custom-call(s32[160,1]{1,0:T(8,128)} %fusion.5.pick_ref, bf16[256,3072]{1,0:T(8,128)(2,1)} %bitcast.73, bf16[256,3072]{1,0:T(8,128)(2,1)} %bitcast.74, bf16[256,3072]{1,0:T(8,128)(2,1)} %bitcast.75), custom_call_target="tpu_custom_call" | custom-call | flops 1 | bytes 1 | tf_op jit(solution)/shard_map/pallas_call | solution.py:51
  28.7 2.7 shard_map.111
  31.5 4.4 %all-to-all-start = ((bf16[4,2,160,640]{3,2,1,0:T(8,128)(2,1)}), bf16[4,2,160,640]{3,2,1,0:T(8,128)(2,1)}, u32[]{:S(2)}, u32[]{:S(2)}) async-start(bf16[4,2,160,640]{3,2,1,0:T(8,128)(2,1)} %shard_map.111), calls=%async_computation | async-start | bytes 3276800 | tf_op jit(solution)/shard_map/all_to_all | solution.py:237
  35.8 2.6 collective-permute-start.6
  41.6 16.5 %collective-permute-done.6 = bf16[2,192,640]{2,1,0:T(8,128)(2,1)S(1)} collective-permute-done((bf16[2,192,640]{2,1,0:T(8,128)(2,1)S(1)}, bf16[2,192,640]{2,1,0:T(8,128)(2,1)S(1)}, u32[]{:S(2)}, u32[]{:S(2)}) %collective-permute-start.6) | collective-permute-done | bytes 491552 | tf_op jit(solution)/shard_map/ppermute | solution.py:376
  58.4 3.4 %collective-permute-done.4.f0 = bf16[4,192,640]{2,1,0:T(8,128)(2,1)} collective-permute-done((bf16[4,192,640]{2,1,0:T(8,128)(2,1)S(1)}, bf16[4,192,640]{2,1,0:T(8,128)(2,1)}, u32[]{:S(2)}, u32[]{:S(2)}) %collective-permute-start.4) | collective-permute-done | bytes 983072 | tf_op jit(solution)/shard_map/ppermute | solution.py:385
  64.0 4.4 %all-to-all-start.1 = ((bf16[8,3,160,384]{3,2,1,0:T(8,128)(2,1)}), bf16[8,3,160,384]{3,2,1,0:T(8,128)(2,1)}, u32[]{:S(2)}, u32[]{:S(2)}) async-start(bf16[8,3,160,384]{3,2,1,0:T(8,128)(2,1)} %shard_map.110), calls=%async_computation.1 | async-start | bytes 5898240 | tf_op jit(solution)/shard_map/all_to_all | solution.py:368
  68.5 13.0 %shard_map.112 = (bf16[4,2,4,160,384]{4,3,2,1,0:T(8,128)(2,1)}, bf16[2,2,320,640]{3,2,1,0:T(8,128)(2,1)}) custom-call(s32[5]{0:T(128)} %stack.32.place_ref, bf16[4,2,160,640]{3,2,1,0:T(8,128)(2,1)} %all-to-all-done.in_ref, bf16[4,192,640]{2,1,0:T(8,128)(2,1)} %copy-done.3, bf16[4,192,640]{2,1,0:T(8,128)(2,1)} %collective-permute-done.4.f0, ...), custom_call_target="tpu_custom_call" | custom-call | flops 199999995904 | bytes 1 | tf_op jit(solution)/shard_map/pallas_call | solution.py:280
  81.5 25.0 %all-to-all-done.1.q_ref.k_ref.v_ref = bf16[8,3,160,384]{3,2,1,0:T(8,128)(2,1)} async-done(((bf16[8,3,160,384]{3,2,1,0:T(8,128)(2,1)}), bf16[8,3,160,384]{3,2,1,0:T(8,128)(2,1)}, u32[]{:S(2)}, u32[]{:S(2)}) %all-to-all-start.1) | async-done | bytes 2949152 | tf_op jit(solution)/shard_map/all_to_all | solution.py:368
  106.5 15.0 %shard_map.113 = (bf16[8,160,384]{2,1,0:T(8,128)(2,1)}, bf16[3,1280,1280]{2,1,0:T(8,128)(2,1)}, f32[3,8,160,1]{3,2,1,0:T(8,128)}) custom-call(f32[1,1280]{1,0:T(1,128)} %select_n.165.bias_ref, f32[8,160,1]{2,1,0:T(8,128)} %fusion.live_ref, bf16[8,3,160,384]{3,2,1,0:T(8,128)(2,1)} %all-to-all-done.1.q_ref.k_ref.v_ref, ...), custom_call_target="tpu_custom_call" | custom-call | flops 199999995904 | bytes 1 | tf_op jit(solution)/shard_map/pallas_call | solution.py:120
  121.5 28.1 %all_to_all.35 = bf16[8,160,384]{2,1,0:T(8,128)(2,1)} all-to-all(bf16[8,160,384]{2,1,0:T(8,128)(2,1)} %get-tuple-element.48), channel_id=1, replica_groups=mesh['zl'=2,'x'=4,'c'=2,'zh'=2,'y'=4] {'zh','y'}, dimensions={0} | all-to-all | bytes 1966080 | tf_op jit(solution)/shard_map/all_to_all | solution.py:368
  149.6 3.6 %all-to-all-start.3 = ((bf16[8,160,384]{2,1,0:T(8,128)(2,1)}), bf16[8,160,384]{2,1,0:T(8,128)(2,1)S(1)}, u32[]{:S(2)}, u32[]{:S(2)}) async-start(bf16[8,160,384]{2,1,0:T(8,128)(2,1)} %bitcast.76), calls=%async_computation.4 | async-start | bytes 1966080 | tf_op jit(solution)/shard_map/all_to_all | solution.py:368
  153.9 13.7 %all-to-all-done.3.grad_ref = bf16[8,160,384]{2,1,0:T(8,128)(2,1)S(1)} async-done(((bf16[8,160,384]{2,1,0:T(8,128)(2,1)}), bf16[8,160,384]{2,1,0:T(8,128)(2,1)S(1)}, u32[]{:S(2)}, u32[]{:S(2)}) %all-to-all-start.3) | async-done | bytes 983072 | tf_op jit(solution)/shard_map/all_to_all | solution.py:368
  168.6 16.3 %shard_map.114 = bf16[8,3,160,256]{3,2,1,0:T(8,128)(2,1)} custom-call(f32[8,160,1]{2,1,0:T(8,128)} %fusion.live_ref, bf16[8,3,160,384]{3,2,1,0:T(8,128)(2,1)} %all-to-all-done.1.q_ref.k_ref.v_ref, bf16[8,3,160,384]{3,2,1,0:T(8,128)(2,1)} %all-to-all-done.1.q_ref.k_ref.v_ref, bf16[8,3,160,384]{3,2,1,0:T(8,128)(2,1)} %all-to-all-done.1.q_ref.k_ref.v_ref, ...), custom_call_target="tpu_custom_call" | custom-call | flops 199999995904 | bytes 1 | tf_op jit(solution)/shard_map/pallas_call | solution.py:174
  184.9 4.3 %all-to-all-start.4 = ((bf16[8,3,160,256]{3,2,1,0:T(8,128)(2,1)}), bf16[8,3,160,256]{3,2,1,0:T(8,128)(2,1)}, u32[]{:S(2)}, u32[]{:S(2)}) async-start(bf16[8,3,160,256]{3,2,1,0:T(8,128)(2,1)} %shard_map.114), calls=%async_computation.5 | async-start | bytes 3932160 | tf_op jit(solution)/shard_map/all_to_all | solution.py:368
  189.2 9.4 %shard_map.115 = bf16[8,3,160,128]{3,2,1,0:T(8,128)(2,1)} custom-call(f32[8,160,1]{2,1,0:T(8,128)} %fusion.live_ref, bf16[8,3,160,384]{3,2,1,0:T(8,128)(2,1)} %all-to-all-done.1.q_ref.k_ref.v_ref, bf16[8,3,160,384]{3,2,1,0:T(8,128)(2,1)} %all-to-all-done.1.q_ref.k_ref.v_ref, bf16[8,3,160,384]{3,2,1,0:T(8,128)(2,1)} %all-to-all-done.1.q_ref.k_ref.v_ref, ...), custom_call_target="tpu_custom_call" | custom-call | flops 199999995904 | bytes 1 | tf_op jit(solution)/shard_map/pallas_call | solution.py:174
  198.6 4.8 %all-gather.3.cloned.1.call-done = bf16[32,160,384]{2,1,0:T(8,128)(2,1)} async-done(((bf16[8,160,384]{2,1,0:T(8,128)(2,1)}), bf16[32,160,384]{2,1,0:T(8,128)(2,1)}) %all-gather.3.cloned.1.call-update) | async-done | bytes 3932176 | tf_op jit(solution)/shard_map/all_gather | solution.py:475
  203.4 10.1 %shard_map.116 = (bf16[2,2,2,4,160,384]{5,4,3,2,1,0:T(8,128)(2,1)}, bf16[2,2,2,4,160,384]{5,4,3,2,1,0:T(8,128)(2,1)}) custom-call(bf16[4,2,4,160,384]{4,3,2,1,0:T(8,128)(2,1)} %bitcast.65, bf16[2,2,320,640]{3,2,1,0:T(8,128)(2,1)} %get-tuple-element.53.turn_ref), custom_call_target="tpu_custom_call" | custom-call | flops 1 | bytes 1 | tf_op jit(solution)/shard_map/pallas_call | solution.py:315
  216.0 4.4 %all-to-all-start.5 = ((bf16[8,3,160,128]{3,2,1,0:T(8,128)(2,1)}), bf16[8,3,160,128]{3,2,1,0:T(8,128)(2,1)S(1)}, u32[]{:S(2)}, u32[]{:S(2)}) async-start(bf16[8,3,160,128]{3,2,1,0:T(8,128)(2,1)} %shard_map.115), calls=%async_computation.6 | async-start | bytes 1966080 | tf_op jit(solution)/shard_map/all_to_all | solution.py:368
  220.5 2.7 collective-permute-done.11.got_ref
  223.2 6.7 %shard_map.117 = (bf16[4,160,384]{2,1,0:T(8,128)(2,1)}, bf16[4,160,384]{2,1,0:T(8,128)(2,1)}, bf16[4,160,384]{2,1,0:T(8,128)(2,1)}, bf16[4,160,384]{2,1,0:T(8,12...) custom-call(s32[5]{0:T(128)} %stack.32.place_ref, ...), custom_call_target="tpu_custom_call" | custom-call | flops 1 | bytes 1 | tf_op jit(solution)/shard_map/pallas_call | solution.py:424
  229.9 11.2 %shard_map.118 = bf16[4,2,160,640]{3,2,1,0:T(8,128)(2,1)} custom-call(s32[5]{0:T(128)} %stack.32.place_ref, bf16[4,2,4,160,384]{4,3,2,1,0:T(8,128)(2,1)} %bitcast.66, bf16[4,192,640]{2,1,0:T(8,128)(2,1)} %copy-done.3, bf16[4,192,640]{2,1,0:T(8,128)(2,1)} %collective-permute-done.4.f0, bf16[2,4,192,640]{3,2,1,0:T(8,128)(2,1)} %bitcast.69, ...), custom_call_target="tpu_custom_call" | custom-call | flops 1 | bytes 1 | tf_op jit(solution)/shard_map/pallas_call | solution.py:348
  242.6 2.6 collective-permute-start.13
  248.4 8.4 %collective-permute-done.14 = bf16[4,160,384]{2,1,0:T(8,128)(2,1)} collective-permute-done((bf16[4,160,384]{2,1,0:T(8,128)(2,1)S(1)}, bf16[4,160,384]{2,1,0:T(8,128)(2,1)}, u32[]{:S(2)}, u32[]{:S(2)}) %collective-permute-start.14) | collective-permute-done | bytes 491552 | tf_op jit(solution)/shard_map/ppermute | solution.py:381
  259.7 5.1 %shard_map.119 = (bf16[256,3072]{1,0:T(8,128)(2,1)}, bf16[256,3072]{1,0:T(8,128)(2,1)}, bf16[256,3072]{1,0:T(8,128)(2,1)}) custom-call(s32[1,160]{1,0:T(1,128)} %compare_select_fusion.pick_ref, bf16[8,3,160,256]{3,2,1,0:T(8,128)(2,1)} %all-to-all-done.4.first_ref, bf16[8,3,160,128]{3,2,1,0:T(8,128)(2,1)} %copy-done.2), custom_call_target="tpu_custom_call" | custom-call | flops 1 | bytes 1 | tf_op jit(solution)/shard_map/pallas_call | solution.py:72
  264.8 4.5 %all-to-all-start.6 = ((bf16[4,2,160,640]{3,2,1,0:T(8,128)(2,1)}), bf16[4,2,160,640]{3,2,1,0:T(8,128)(2,1)S(1)}, u32[]{:S(2)}, u32[]{:S(2)}) async-start(bf16[4,2,160,640]{3,2,1,0:T(8,128)(2,1)} %shard_map.118), calls=%async_computation.7 | async-start | bytes 3276800 | tf_op jit(solution)/shard_map/all_to_all | solution.py:237
  271.6 2.7 collective-permute-start.16
  277.2 3.2 %collective-permute-start.22 = (bf16[160,384]{1,0:T(8,128)(2,1)S(1)}, bf16[160,384]{1,0:T(8,128)(2,1)S(1)}, u32[]{:S(2)}, u32[]{:S(2)}) collective-permute-start(bf16[160,384]{1,0:T(8,128)(2,1)S(1)} %get-tuple-element.78), channel_id=1, source_target_pairs={{0,68},{64,0},{4,64},{68,4},{1,69},{65,1},{5,65},{69,5},{2,70},{66... | collective-permute-start | bytes 368648 | tf_op jit(solution)/shard_map/ppermute | solution.py:381
  280.8 3.4 %collective-permute-done.21 = bf16[160,384]{1,0:T(8,128)(2,1)S(1)} collective-permute-done((bf16[160,384]{1,0:T(8,128)(2,1)S(1)}, bf16[160,384]{1,0:T(8,128)(2,1)S(1)}, u32[]{:S(2)}, u32[]{:S(2)}) %collective-permute-start.21) | collective-permute-done | bytes 122912 | tf_op jit(solution)/shard_map/ppermute | solution.py:381
  284.2 2.6 collective-permute-done.23
  290.3 2.7 shard_map.120
  (96 shorter events, 38.5 us)
Async XLA Ops:
  8.3 18.8 %collective-permute-start = (bf16[192,640]{1,0:T(8,128)(2,1)S(1)}, bf16[192,640]{1,0:T(8,128)(2,1)S(1)}, u32[]{:S(2)}, u32[]{:S(2)}) collective-permute-start(bf16[192,640]{1,0:T(8,128)(2,1)S(1)} %get-tuple-element.72), channel_id=1, source_target_pairs={{0,1},{1,2},{2,3},{3,0},{4,5},{5,6},{6,7},{7,4},{8,9},{9,10},{10,1... | collective-permute-start | bytes 737288 | tf_op jit(solution)/shard_map/ppermute | solution.py:376
  10.0 17.2 %collective-permute-start.1 = (bf16[192,640]{1,0:T(8,128)(2,1)S(1)}, bf16[192,640]{1,0:T(8,128)(2,1)S(1)}, u32[]{:S(2)}, u32[]{:S(2)}) collective-permute-start(bf16[192,640]{1,0:T(8,128)(2,1)S(1)} %get-tuple-element.72), channel_id=1, source_target_pairs={{0,3},{1,0},{2,1},{3,2},{4,7},{5,4},{6,5},{7,6},{8,11},{9,8},{10,9... | collective-permute-start | bytes 737288 | tf_op jit(solution)/shard_map/ppermute | solution.py:376
  11.6 15.6 %collective-permute-start.2 = (bf16[192,640]{1,0:T(8,128)(2,1)S(1)}, bf16[192,640]{1,0:T(8,128)(2,1)S(1)}, u32[]{:S(2)}, u32[]{:S(2)}) collective-permute-start(bf16[192,640]{1,0:T(8,128)(2,1)S(1)} %get-tuple-element.72), channel_id=1, source_target_pairs={{0,2},{1,3},{2,0},{3,1},{4,6},{5,7},{6,4},{7,5},{8,10},{9,11},{10,... | collective-permute-start | bytes 737288 | tf_op jit(solution)/shard_map/ppermute | solution.py:376
  14.6 12.5 %collective-permute-start.3 = (bf16[192,640]{1,0:T(8,128)(2,1)S(1)}, bf16[192,640]{1,0:T(8,128)(2,1)S(1)}, u32[]{:S(2)}, u32[]{:S(2)}) collective-permute-start(bf16[192,640]{1,0:T(8,128)(2,1)S(1)} %dynamic-slice.1), channel_id=1, source_target_pairs={{0,68},{68,0},{64,4},{4,64},{1,69},{69,1},{65,5},{5,65},{2,70},{70... | collective-permute-start | bytes 737288 | tf_op jit(solution)/shard_map/ppermute | solution.py:385
  27.3 13.2 %collective-permute-start.5 = (bf16[2,192,640]{2,1,0:T(8,128)(2,1)S(1)}, bf16[2,192,640]{2,1,0:T(8,128)(2,1)}, u32[]{:S(2)}, u32[]{:S(2)}) collective-permute-start(bf16[2,192,640]{2,1,0:T(8,128)(2,1)S(1)} %pad_maximum_fusion), channel_id=1, source_target_pairs={{0,1},{1,2},{2,3},{3,0},{4,5},{5,6},{6,7},{7,4},{8,9},{9,10},{10,1... | collective-permute-start | bytes 1474568 | tf_op jit(solution)/shard_map/ppermute | solution.py:376
  31.5 26.8 %all-to-all-start = ((bf16[4,2,160,640]{3,2,1,0:T(8,128)(2,1)}), bf16[4,2,160,640]{3,2,1,0:T(8,128)(2,1)}, u32[]{:S(2)}, u32[]{:S(2)}) async-start(bf16[4,2,160,640]{3,2,1,0:T(8,128)(2,1)} %shard_map.111), calls=%async_computation | async-start | bytes 3276800 | tf_op jit(solution)/shard_map/all_to_all | solution.py:237
  35.8 22.3 %collective-permute-start.6 = (bf16[2,192,640]{2,1,0:T(8,128)(2,1)S(1)}, bf16[2,192,640]{2,1,0:T(8,128)(2,1)S(1)}, u32[]{:S(2)}, u32[]{:S(2)}) collective-permute-start(bf16[2,192,640]{2,1,0:T(8,128)(2,1)S(1)} %pad_maximum_fusion), channel_id=1, source_target_pairs={{0,3},{1,0},{2,1},{3,2},{4,7},{5,4},{6,5},{7,6},{8,11},{9,8},{10,9... | collective-permute-start | bytes 1474568 | tf_op jit(solution)/shard_map/ppermute | solution.py:376
  38.5 19.7 %collective-permute-start.7 = (bf16[2,192,640]{2,1,0:T(8,128)(2,1)S(1)}, bf16[2,192,640]{2,1,0:T(8,128)(2,1)S(1)}, u32[]{:S(2)}, u32[]{:S(2)}) collective-permute-start(bf16[2,192,640]{2,1,0:T(8,128)(2,1)S(1)} %pad_maximum_fusion), channel_id=1, source_target_pairs={{0,2},{1,3},{2,0},{3,1},{4,6},{5,7},{6,4},{7,5},{8,10},{9,11},{10,... | collective-permute-start | bytes 1474568 | tf_op jit(solution)/shard_map/ppermute | solution.py:376
  38.8 23.0 %collective-permute-start.4 = (bf16[4,192,640]{2,1,0:T(8,128)(2,1)S(1)}, bf16[4,192,640]{2,1,0:T(8,128)(2,1)}, u32[]{:S(2)}, u32[]{:S(2)}) collective-permute-start(bf16[4,192,640]{2,1,0:T(8,128)(2,1)S(1)} %bitcast_dynamic-update-slice_fusion.4.u0), channel_id=1, source_target_pairs={{0,68},{68,0},{64,4},{4,64},{1,69},{69,1},{65,5},{5,65},{2,70},{70... | collective-permute-start | bytes 2949128 | tf_op jit(solution)/shard_map/ppermute | solution.py:385
  58.3 10.3 %collective-permute-start.10 = (bf16[2,4,192,640]{3,2,1,0:T(8,128)(2,1)S(1)}, bf16[2,4,192,640]{3,2,1,0:T(8,128)(2,1)}, u32[]{:S(2)}, u32[]{:S(2)}) collective-permute-start(bf16[2,4,192,640]{3,2,1,0:T(8,128)(2,1)S(1)} %bitcast.67), channel_id=1, source_target_pairs={{0,8},{8,0},{1,9},{9,1},{2,10},{10,2},{3,11},{11,3},{4,12},{12,4},... | collective-permute-start | bytes 5898248 | tf_op jit(solution)/shard_map/ppermute | solution.py:364
  61.8 6.7 %collective-permute-start.9 = (bf16[4,192,640]{2,1,0:T(8,128)(2,1)}, bf16[4,192,640]{2,1,0:T(8,128)(2,1)}, u32[]{:S(2)}, u32[]{:S(2)}) collective-permute-start(bf16[4,192,640]{2,1,0:T(8,128)(2,1)} %collective-permute-done.4.f0), channel_id=1, source_target_pairs={{0,8},{8,0},{1,9},{9,1},{2,10},{10,2},{3,11},{11,3},{4,12},{12,4},... | collective-permute-start | bytes 2949128 | tf_op jit(solution)/shard_map/ppermute | solution.py:364
  61.8 6.7 %collective-permute-start.8 = (bf16[4,192,640]{2,1,0:T(8,128)(2,1)S(1)}, bf16[4,192,640]{2,1,0:T(8,128)(2,1)}, u32[]{:S(2)}, u32[]{:S(2)}) collective-permute-start(bf16[4,192,640]{2,1,0:T(8,128)(2,1)S(1)} %bitcast_dynamic-update-slice_fusion.4.u0), channel_id=1, source_target_pairs={{0,8},{8,0},{1,9},{9,1},{2,10},{10,2},{3,11},{11,3},{4,12},{12,4},... | collective-permute-start | bytes 2949128 | tf_op jit(solution)/shard_map/ppermute | solution.py:364
  64.0 42.5 %all-to-all-start.1 = ((bf16[8,3,160,384]{3,2,1,0:T(8,128)(2,1)}), bf16[8,3,160,384]{3,2,1,0:T(8,128)(2,1)}, u32[]{:S(2)}, u32[]{:S(2)}) async-start(bf16[8,3,160,384]{3,2,1,0:T(8,128)(2,1)} %shard_map.110), calls=%async_computation.1 | async-start | bytes 5898240 | tf_op jit(solution)/shard_map/all_to_all | solution.py:368
  68.5 81.1 %reduce-scatter.2.cloned.1.call-start = ((), (), s32[]{:S(2)}) async-start(), calls=%async_computation.8 | async-start | bytes 4915200 | tf_op jit(solution)/shard_map/reduce_scatter | solution.py:472
  149.6 18.0 %all-to-all-start.3 = ((bf16[8,160,384]{2,1,0:T(8,128)(2,1)}), bf16[8,160,384]{2,1,0:T(8,128)(2,1)S(1)}, u32[]{:S(2)}, u32[]{:S(2)}) async-start(bf16[8,160,384]{2,1,0:T(8,128)(2,1)} %bitcast.76), calls=%async_computation.4 | async-start | bytes 1966080 | tf_op jit(solution)/shard_map/all_to_all | solution.py:368
  153.2 50.2 %all-gather.3.cloned.1.call-start = ((), (), s32[]{:S(2)}) async-start(), calls=%async_computation.9 | async-start | bytes 4915200 | tf_op jit(solution)/shard_map/all_gather | solution.py:475
  184.9 31.2 %all-to-all-start.4 = ((bf16[8,3,160,256]{3,2,1,0:T(8,128)(2,1)}), bf16[8,3,160,256]{3,2,1,0:T(8,128)(2,1)}, u32[]{:S(2)}, u32[]{:S(2)}) async-start(bf16[8,3,160,256]{3,2,1,0:T(8,128)(2,1)} %shard_map.114), calls=%async_computation.5 | async-start | bytes 3932160 | tf_op jit(solution)/shard_map/all_to_all | solution.py:368
  216.0 7.1 %collective-permute-start.11 = (bf16[2,2,2,4,160,384]{5,4,3,2,1,0:T(8,128)(2,1)}, bf16[2,2,2,4,160,384]{5,4,3,2,1,0:T(8,128)(2,1)}, u32[]{:S(2)}, u32[]{:S(2)}) collective-permute-start(bf16[2,2,2,4,160,384]{5,4,3,2,1,0:T(8,128)(2,1)} %get-tuple-element.56), channel_id=1, source_target_pairs={{0,8},{8,0},{1,9},{9,1},{2,10},{10,2},{3,11},{11,3},{4,12},{12,4},... | collective-permute-start | bytes 11796488 | tf_op jit(solution)/shard_map/ppermute | solution.py:364
  216.0 42.7 %all-to-all-start.5 = ((bf16[8,3,160,128]{3,2,1,0:T(8,128)(2,1)}), bf16[8,3,160,128]{3,2,1,0:T(8,128)(2,1)S(1)}, u32[]{:S(2)}, u32[]{:S(2)}) async-start(bf16[8,3,160,128]{3,2,1,0:T(8,128)(2,1)} %shard_map.115), calls=%async_computation.6 | async-start | bytes 1966080 | tf_op jit(solution)/shard_map/all_to_all | solution.py:368
  241.0 15.7 %collective-permute-start.14 = (bf16[4,160,384]{2,1,0:T(8,128)(2,1)S(1)}, bf16[4,160,384]{2,1,0:T(8,128)(2,1)}, u32[]{:S(2)}, u32[]{:S(2)}) collective-permute-start(bf16[4,160,384]{2,1,0:T(8,128)(2,1)S(1)} %copy-done.10), channel_id=1, source_target_pairs={{0,4},{64,68},{4,0},{68,64},{1,5},{65,69},{5,1},{69,65},{2,6},{66,... | collective-permute-start | bytes 1474568 | tf_op jit(solution)/shard_map/ppermute | solution.py:381
  241.9 27.4 %collective-permute-start.12 = (bf16[4,160,384]{2,1,0:T(8,128)(2,1)}, bf16[4,160,384]{2,1,0:T(8,128)(2,1)}, u32[]{:S(2)}, u32[]{:S(2)}) collective-permute-start(bf16[4,160,384]{2,1,0:T(8,128)(2,1)} %get-tuple-element.58), channel_id=1, source_target_pairs={{0,64},{64,4},{4,68},{68,0},{1,65},{65,5},{5,69},{69,1},{2,66},{66... | collective-permute-start | bytes 1474568 | tf_op jit(solution)/shard_map/ppermute | solution.py:381
  242.6 26.8 %collective-permute-start.13 = (bf16[4,160,384]{2,1,0:T(8,128)(2,1)}, bf16[4,160,384]{2,1,0:T(8,128)(2,1)}, u32[]{:S(2)}, u32[]{:S(2)}) collective-permute-start(bf16[4,160,384]{2,1,0:T(8,128)(2,1)} %get-tuple-element.60), channel_id=1, source_target_pairs={{0,68},{64,0},{4,64},{68,4},{1,69},{65,1},{5,65},{69,5},{2,70},{66... | collective-permute-start | bytes 1474568 | tf_op jit(solution)/shard_map/ppermute | solution.py:381
  245.1 29.2 %collective-permute-start.18 = (bf16[2,2,160,384]{3,2,1,0:T(8,128)(2,1)}, bf16[2,2,160,384]{3,2,1,0:T(8,128)(2,1)S(1)}, u32[]{:S(2)}, u32[]{:S(2)}) collective-permute-start(bf16[2,2,160,384]{3,2,1,0:T(8,128)(2,1)} %get-tuple-element.62), channel_id=1, source_target_pairs={{0,1},{1,2},{2,3},{3,0},{4,5},{5,6},{6,7},{7,4},{8,9},{9,10},{10,1... | collective-permute-start | bytes 1474568 | tf_op jit(solution)/shard_map/ppermute | solution.py:376
  246.6 29.2 %collective-permute-start.19 = (bf16[2,2,160,384]{3,2,1,0:T(8,128)(2,1)}, bf16[2,2,160,384]{3,2,1,0:T(8,128)(2,1)S(1)}, u32[]{:S(2)}, u32[]{:S(2)}) collective-permute-start(bf16[2,2,160,384]{3,2,1,0:T(8,128)(2,1)} %get-tuple-element.64), channel_id=1, source_target_pairs={{0,3},{1,0},{2,1},{3,2},{4,7},{5,4},{6,5},{7,6},{8,11},{9,8},{10,9... | collective-permute-start | bytes 1474568 | tf_op jit(solution)/shard_map/ppermute | solution.py:376
  256.8 19.1 %collective-permute-start.20 = (bf16[2,2,160,384]{3,2,1,0:T(8,128)(2,1)}, bf16[2,2,160,384]{3,2,1,0:T(8,128)(2,1)}, u32[]{:S(2)}, u32[]{:S(2)}) collective-permute-start(bf16[2,2,160,384]{3,2,1,0:T(8,128)(2,1)} %get-tuple-element.63), channel_id=1, source_target_pairs={{0,2},{1,3},{2,0},{3,1},{4,6},{5,7},{6,4},{7,5},{8,10},{9,11},{10,... | collective-permute-start | bytes 1474568 | tf_op jit(solution)/shard_map/ppermute | solution.py:376
  264.8 24.3 %all-to-all-start.6 = ((bf16[4,2,160,640]{3,2,1,0:T(8,128)(2,1)}), bf16[4,2,160,640]{3,2,1,0:T(8,128)(2,1)S(1)}, u32[]{:S(2)}, u32[]{:S(2)}) async-start(bf16[4,2,160,640]{3,2,1,0:T(8,128)(2,1)} %shard_map.118), calls=%async_computation.7 | async-start | bytes 3276800 | tf_op jit(solution)/shard_map/all_to_all | solution.py:237
  271.0 9.5 %collective-permute-start.15 = (bf16[160,384]{1,0:T(8,128)(2,1)S(1)}, bf16[160,384]{1,0:T(8,128)(2,1)S(1)}, u32[]{:S(2)}, u32[]{:S(2)}) collective-permute-start(bf16[160,384]{1,0:T(8,128)(2,1)S(1)} %get-tuple-element.73), channel_id=1, source_target_pairs={{0,1},{1,2},{2,3},{3,0},{4,5},{5,6},{6,7},{7,4},{8,9},{9,10},{10,1... | collective-permute-start | bytes 368648 | tf_op jit(solution)/shard_map/ppermute | solution.py:376
  271.6 9.1 %collective-permute-start.16 = (bf16[160,384]{1,0:T(8,128)(2,1)S(1)}, bf16[160,384]{1,0:T(8,128)(2,1)S(1)}, u32[]{:S(2)}, u32[]{:S(2)}) collective-permute-start(bf16[160,384]{1,0:T(8,128)(2,1)S(1)} %get-tuple-element.75), channel_id=1, source_target_pairs={{0,3},{1,0},{2,1},{3,2},{4,7},{5,4},{6,5},{7,6},{8,11},{9,8},{10,9... | collective-permute-start | bytes 368648 | tf_op jit(solution)/shard_map/ppermute | solution.py:376
  274.3 6.4 %collective-permute-start.17 = (bf16[160,384]{1,0:T(8,128)(2,1)S(1)}, bf16[160,384]{1,0:T(8,128)(2,1)S(1)}, u32[]{:S(2)}, u32[]{:S(2)}) collective-permute-start(bf16[160,384]{1,0:T(8,128)(2,1)S(1)} %get-tuple-element.74), channel_id=1, source_target_pairs={{0,2},{1,3},{2,0},{3,1},{4,6},{5,7},{6,4},{7,5},{8,10},{9,11},{10,... | collective-permute-start | bytes 368648 | tf_op jit(solution)/shard_map/ppermute | solution.py:376
  277.2 7.0 %collective-permute-start.21 = (bf16[160,384]{1,0:T(8,128)(2,1)S(1)}, bf16[160,384]{1,0:T(8,128)(2,1)S(1)}, u32[]{:S(2)}, u32[]{:S(2)}) collective-permute-start(bf16[160,384]{1,0:T(8,128)(2,1)S(1)} %get-tuple-element.76), channel_id=1, source_target_pairs={{0,64},{64,4},{4,68},{68,0},{1,65},{65,5},{5,69},{69,1},{2,66},{66... | collective-permute-start | bytes 368648 | tf_op jit(solution)/shard_map/ppermute | solution.py:381
  277.2 7.0 %collective-permute-start.22 = (bf16[160,384]{1,0:T(8,128)(2,1)S(1)}, bf16[160,384]{1,0:T(8,128)(2,1)S(1)}, u32[]{:S(2)}, u32[]{:S(2)}) collective-permute-start(bf16[160,384]{1,0:T(8,128)(2,1)S(1)} %get-tuple-element.78), channel_id=1, source_target_pairs={{0,68},{64,0},{4,64},{68,4},{1,69},{65,1},{5,65},{69,5},{2,70},{66... | collective-permute-start | bytes 368648 | tf_op jit(solution)/shard_map/ppermute | solution.py:381
  280.5 6.4 %collective-permute-start.23 = (bf16[160,384]{1,0:T(8,128)(2,1)S(1)}, bf16[160,384]{1,0:T(8,128)(2,1)S(1)}, u32[]{:S(2)}, u32[]{:S(2)}) collective-permute-start(bf16[160,384]{1,0:T(8,128)(2,1)S(1)} %get-tuple-element.77), channel_id=1, source_target_pairs={{0,4},{64,68},{4,0},{68,64},{1,5},{65,69},{5,1},{69,65},{2,6},{66,... | collective-permute-start | bytes 368648 | tf_op jit(solution)/shard_map/ppermute | solution.py:381
  (11 other events, 116.6 us)
Sparse Core Ops, SparseCore 0:
  81.6 46.5 reduce-scatter.1
  155.7 47.6 all-gather.2
